TPU v7x, 32 devices: a whole 2x2x4 slice. The times are simulated.
32 devices in a mesh: groups: 2 (over y), rep: 4 (over x, core), tp: 4 (over z).
Axes of the slice: x: 2, y: 2, z: 4, core: 2. Of those that a mesh axis runs over, the one named last changes fastest.
Arguments:
- base: bfloat16 [16384, 40960], P('tp', 'rep'), may hold values from -0.046875 to 0.046875
- decoded_row_activations: bfloat16 [512, 16384], P('groups', 'tp'), parts along dimension 0, may hold values from -6 to 6
- input_factor: float32 [32768, 32], P(('groups', 'tp'), 'rep'), parts along dimension 0, may hold values from -0.046875 to 0.046875
- output_factor: float32 [32, 81920], P('rep', ('groups', 'tp')), parts along dimension 1, may hold values from -0.3125 to 0.3125
- input_first_moment: float32 [32768, 32], P(('groups', 'tp'), 'rep'), parts along dimension 0, may hold values from -4 to 4
- input_second_moment: float32 [32768, 32], P(('groups', 'tp'), 'rep'), parts along dimension 0, may hold values from 0.02 to 0.5
- output_first_moment: float32 [32, 81920], P('rep', ('groups', 'tp')), parts along dimension 1, may hold values from -4 to 4
- output_second_moment: float32 [32, 81920], P('rep', ('groups', 'tp')), parts along dimension 1, may hold values from 0.02 to 0.5
- replica_input_gradient: float32 [4, 32768, 32], P('rep', ('groups', 'tp')), parts along dimension 1, may hold values from -4 to 4
- replica_output_gradient: float32 [4, 32, 81920], P('rep', None, ('groups', 'tp')), parts along dimension 2, may hold values from -4 to 4
Outputs:
- decoded: float32 [512, 40960], P(('groups', 'tp'), 'rep'), parts along dimension 0
- lora_in_new: float32 [32768, 32], P(('groups', 'tp'), 'rep'), parts along dimension 0
- lora_out_new: float32 [32, 81920], P('rep', ('groups', 'tp')), parts along dimension 1
- input_first_moment_next: float32 [32768, 32], P(('groups', 'tp'), 'rep'), parts along dimension 0
- input_second_moment_next: float32 [32768, 32], P(('groups', 'tp'), 'rep'), parts along dimension 0
- output_first_moment_next: float32 [32, 81920], P('rep', ('groups', 'tp')), parts along dimension 1
- output_second_moment_next: float32 [32, 81920], P('rep', ('groups', 'tp')), parts along dimension 1
There are 2 independent parts, one for each index of `groups`. A program takes and returns all parts, laid end to end along the dimension named above; an argument that names none is the same for every part. Nothing has to cross between parts.
All inputs are finite; a program needn't handle non-finite values.
Results may differ from a plain program's by a relative error of at most 0.0031.
Values may be sent and summed in bfloat16 or wider, within the bound.
No kernel may reach another device: no remote copies, remote signals or barrier semaphores. Data moves between devices by JAX's collectives and lax.ppermute only.
A program may use at most 256 MiB of HBM per device.

v0:
```python
import jax
import jax.numpy as jnp
from jax import lax
from jax.sharding import PartitionSpec as P

ADAM_STEP = 200


beta_one = 0.9
beta_two = 0.999
learn_rate = 0.003
adam_eps = 1e-08
factor_scale = 2.0


def apply_adam_rule(weights, moment, second, grads):
    moment_new = beta_one * moment + (1.0 - beta_one) * grads
    second_new = beta_two * second + (1.0 - beta_two) * grads * grads
    first_fix = 1.0 - beta_one**ADAM_STEP
    second_fix = 1.0 - beta_two**ADAM_STEP
    step_size = moment_new / first_fix / (jnp.sqrt(second_new / second_fix) + adam_eps)
    return (weights - learn_rate * step_size, moment_new, second_new)


def local(
    base,
    decoded_row_activations,
    input_factor,
    output_factor,
    input_first_moment,
    input_second_moment,
    output_first_moment,
    output_second_moment,
    replica_input_gradient,
    replica_output_gradient,
):
    part_in = replica_input_gradient[0]
    part_out = replica_output_gradient[0]
    rank_portion = input_factor.shape[1]
    whole_in, whole_out = (
        lax.psum(part_in.astype(jnp.bfloat16), "rep").astype(jnp.float32),
        lax.psum(part_out.astype(jnp.bfloat16), "rep").astype(jnp.float32),
    )
    offset = lax.axis_index("rep") * rank_portion
    input_gradient_sum = lax.dynamic_slice_in_dim(whole_in, offset, rank_portion, 1)
    output_gradient_sum = lax.dynamic_slice_in_dim(whole_out, offset, rank_portion, 0)
    refreshed_input_factor, input_first_moment_next, input_second_moment_next = apply_adam_rule(
        input_factor, input_first_moment, input_second_moment, input_gradient_sum
    )
    refreshed_output_factor, output_first_moment_next, output_second_moment_next = apply_adam_rule(
        output_factor, output_first_moment, output_second_moment, output_gradient_sum
    )
    half_in = refreshed_input_factor.astype(jnp.bfloat16)
    half_out = refreshed_output_factor.astype(jnp.bfloat16)
    rank_rows = lax.all_gather(half_in, "rep", axis=1, tiled=True)
    quarter = base.shape[1]
    gathered = lax.all_gather(half_out, ("rep", "tp"), axis=1, tiled=True)
    replicas = lax.axis_size("rep")
    rows_share = half_out.shape[0]
    stacked = gathered.reshape(rows_share, replicas, -1)
    full_out = jnp.transpose(stacked, (1, 0, 2)).reshape(rows_share * replicas, -1)
    rank_cols = lax.dynamic_slice_in_dim(full_out, lax.axis_index("rep") * quarter, quarter, 1)
    weight_change = jnp.dot(rank_rows, rank_cols, preferred_element_type=jnp.float32)
    merged_weight = (base.astype(jnp.float32) + factor_scale * weight_change).astype(jnp.bfloat16)
    col_slab = lax.psum_scatter(
        lax.dot_general(
            merged_weight,
            decoded_row_activations,
            (((0,), (1,)), ((), ())),
            preferred_element_type=jnp.float32,
        ),
        "tp",
        scatter_dimension=0,
        tiled=True,
    )
    regrouped = lax.all_to_all(col_slab, "tp", split_axis=1, concat_axis=0, tiled=True)
    decoded = jnp.transpose(regrouped, (1, 0))
    return (
        decoded,
        refreshed_input_factor,
        refreshed_output_factor,
        input_first_moment_next,
        input_second_moment_next,
        output_first_moment_next,
        output_second_moment_next,
    )


def solution(mesh):
    return jax.shard_map(
        local,
        mesh=mesh,
        in_specs=(
            P("tp", "rep"),
            P("groups", "tp"),
            P(("groups", "tp"), "rep"),
            P("rep", ("groups", "tp")),
            P(("groups", "tp"), "rep"),
            P(("groups", "tp"), "rep"),
            P("rep", ("groups", "tp")),
            P("rep", ("groups", "tp")),
            P("rep", ("groups", "tp"), None),
            P("rep", None, ("groups", "tp")),
        ),
        out_specs=(
            P(("groups", "tp"), "rep"),
            P(("groups", "tp"), "rep"),
            P("rep", ("groups", "tp")),
            P(("groups", "tp"), "rep"),
            P(("groups", "tp"), "rep"),
            P("rep", ("groups", "tp")),
            P("rep", ("groups", "tp")),
        ),
        check_vma=False,
    )
```

profile of v0, /device:TPU:0, one launch (start us, length us, event | category | flops | bytes accessed | tf_op | source)
XLA Modules:
  0.0 433.6 jit_solution(630309491520803534)
XLA Ops:
  7.2 0.0 copy-start
  7.2 0.0 copy-start.2
  7.2 0.0 copy-start.3
  7.2 0.0 copy-start.1
  7.2 0.0 all-reduce.3.cloned.1.call-start
  7.3 1.9 convert_bitcast_fusion.1
  9.2 0.0 copy-start.4
  9.2 0.0 copy-start.5
  9.2 0.0 copy-start.6
  9.2 2.3 convert_bitcast_fusion
  11.5 0.0 all-reduce.3.cloned.1.call-update
  11.5 0.0 all-gather.2.cloned.1.call-start
  11.5 38.1 %all-reduce.3.cloned.1.call-done = (bf16[4096,32]{0,1:T(8,128)(2,1)}, bf16[32,10240]{1,0:T(8,128)(2,1)}) async-done(((bf16[4096,32]{0,1:T(8,128)(2,1)}, bf16[32,10240]{1,0:T(8,128)(2,1)}), (bf16[4096,32]{0,1:T(8,128)(2,1)}, bf16[32,10240]{1,0:T(8,128)(2,1)})) %all-reduce.3.cloned.1.call-update) | async-done | bytes 917520 | tf_op jit(solution)/shard_map/psum | solution.py:41
  49.7 0.0 copy-done.2
  49.7 0.0 copy-done.3
  49.7 0.0 copy-done.1
  49.7 2.0 fusion.10
  51.7 0.0 all-gather.2.cloned.1.call-update
  51.7 0.0 reduce-scatter.2.cloned.1.call-start
  51.8 0.0 copy-done.4
  51.8 0.0 copy-done.5
  51.8 0.0 copy-done.6
  51.8 1.6 fusion.13
  53.5 5.8 %all_gather.6 = bf16[4096,32]{0,1:T(8,128)(2,1)S(1)} all-gather(bf16[4096,8]{0,1:T(8,128)(2,1)S(1)} %get-tuple-element.13), channel_id=1, replica_groups=mesh['groups'=2,'rep'=4,'tp'=4] {'rep'}, dimensions={1}, use_global_device_ids=true | all-gather | bytes 327680 | tf_op jit(solution)/shard_map/all_gather | solution.py:55
  59.2 36.9 %all-gather.2.cloned.1.call-done = bf16[8,163840]{1,0:T(8,128)(2,1)} async-done(((bf16[8,10240]{1,0:T(8,128)(2,1)}), bf16[8,163840]{1,0:T(8,128)(2,1)}) %all-gather.2.cloned.1.call-update) | async-done | bytes 2621456 | tf_op jit(solution)/shard_map/all_gather | solution.py:57
  96.1 0.0 copy-done
  96.1 85.0 %fusion = f32[10240,256]{1,0:T(8,128)} fusion(bf16[256,4096]{1,0:T(8,128)(2,1)S(1)} %copy-done, bf16[4096,10240]{1,0:T(8,128)(2,1)} %param.10, bf16[4096,32]{0,1:T(8,128)(2,1)S(1)} %all_gather.6, bf16[32,40960]{1,0:T(8,128)(2,1)} %bitcast.23, s32[]{:T(128)S(6)} %select_n.8), kind=kOutput, calls=%fused_computation.1 | convolution fusion | flops 24326963200 | bytes 97386496 | tf_op jit(solution)/shard_map/dot_general | solution.py:66
  181.1 0.0 reduce-scatter.2.cloned.1.call-update
  181.1 176.8 %reduce-scatter.2.cloned.1.call-done = f32[2560,256]{1,0:T(8,128)} async-done(((f32[10240,256]{1,0:T(8,128)}), f32[2560,256]{1,0:T(8,128)}) %reduce-scatter.2.cloned.1.call-update) | async-done | bytes 2621456 | tf_op jit(solution)/shard_map/reduce_scatter | solution.py:65
  357.9 3.2 copy.19
  361.1 64.2 %all_to_all.19 = f32[2560,4,64]{0,2,1:T(8,128)S(1)} all-to-all(f32[2560,4,64]{0,2,1:T(8,128)} %bitcast.20), channel_id=1, replica_groups=mesh['groups'=2,'rep'=4,'tp'=4] {'tp'}, dimensions={1} | all-to-all | bytes 5242880 | tf_op jit(solution)/shard_map/all_to_all | solution.py:76
  425.4 1.7 copy.21
Async XLA Ops:
  7.2 88.9 %copy-start = (bf16[256,4096]{1,0:T(8,128)(2,1)S(1)}, bf16[256,4096]{1,0:T(8,128)(2,1)}, u32[]{:S(2)}) copy-start(bf16[256,4096]{1,0:T(8,128)(2,1)} %param.11) | copy-start | bytes 6291460
  7.2 42.5 %copy-start.2 = (f32[8,10240]{1,0:T(8,128)S(1)}, f32[8,10240]{1,0:T(8,128)}, u32[]{:S(2)}) copy-start(f32[8,10240]{1,0:T(8,128)} %param.17) | copy-start | bytes 983044
  7.2 42.5 %copy-start.3 = (f32[8,10240]{1,0:T(8,128)S(1)}, f32[8,10240]{1,0:T(8,128)}, u32[]{:S(2)}) copy-start(f32[8,10240]{1,0:T(8,128)} %param.16) | copy-start | bytes 983044
  7.2 42.5 %copy-start.1 = (f32[8,10240]{1,0:T(8,128)S(1)}, f32[8,10240]{1,0:T(8,128)}, u32[]{:S(2)}) copy-start(f32[8,10240]{1,0:T(8,128)} %param.13) | copy-start | bytes 983044
  7.2 42.4 %all-reduce.3.cloned.1.call-start = ((), (), s32[]{:S(2)}) async-start(), calls=%async_computation.4 | async-start | bytes 1835008 | tf_op jit(solution)/shard_map/psum | solution.py:41
  9.2 42.6 %copy-start.4 = (f32[4096,8]{0,1:T(8,128)S(1)}, f32[4096,8]{0,1:T(8,128)}, u32[]{:S(2)}) copy-start(f32[4096,8]{0,1:T(8,128)} %param.12) | copy-start | bytes 393220
  9.2 42.6 %copy-start.5 = (f32[4096,8]{0,1:T(8,128)S(1)}, f32[4096,8]{0,1:T(8,128)}, u32[]{:S(2)}) copy-start(f32[4096,8]{0,1:T(8,128)} %param.15) | copy-start | bytes 393220
  9.2 42.6 %copy-start.6 = (f32[4096,8]{0,1:T(8,128)S(1)}, f32[4096,8]{0,1:T(8,128)}, u32[]{:S(2)}) copy-start(f32[4096,8]{0,1:T(8,128)} %param.14) | copy-start | bytes 393220
  11.5 84.6 %all-gather.2.cloned.1.call-start = ((), (), s32[]{:S(2)}) async-start(), calls=%async_computation.2 | async-start | bytes 2785280 | tf_op jit(solution)/shard_map/all_gather | solution.py:57
  51.7 306.2 %reduce-scatter.2.cloned.1.call-start = ((), (), s32[]{:S(2)}) async-start(), calls=%async_computation.3 | async-start | bytes 13107200 | tf_op jit(solution)/shard_map/reduce_scatter | solution.py:65
Sparse Core Ops, SparseCore 0:
  11.6 38.0 all-reduce.2
  52.5 43.5 all-gather.1
  181.2 176.6 reduce-scatter.1
where the time goes:
time: 434 us
  waiting for transfers between devices  252 us (58%)
  matrix products  85 us (20%)
  blocking collectives  70 us (16%)
  between operations  13.8 us (3%)
  other arithmetic  7.86 us (2%)
  local copies, waits for them, and re-layouts  4.91 us (1%)
    reduce_scatter x1, waiting for transfers between devices, local(): lax.psum_scatter(lax.dot_general(merged_weight, decoded_row_activations,...  177 us
    dot_general x1, matrix products, local(): lax.dot_general(merged_weight, decoded_row_activations, (((0,), (1,)), ((...  85 us
    all_to_all x1, blocking collectives, local(): lax.all_to_all(col_slab, 'tp', split_axis=1, concat_axis=0, tiled=True)  64.2 us
    psum x1, waiting for transfers between devices, local(): lax.psum(part_in.astype(jnp.bfloat16), 'rep').astype(jnp.float32)  38.1 us
    all_gather x1, waiting for transfers between devices, local(): gathered = lax.all_gather(half_out, ('rep', 'tp'), axis=1, tiled=True)  36.9 us
  transfers between devices with their start and end apart: 3, of which 3 were waited for; matrix products, arithmetic and copies ran while one was open for 0% of the time, Pallas kernels for 0%

commit v1 on v0

v1 whole, which is shorter than its diff:
```python
import jax
import jax.numpy as jnp
from jax import lax
from jax.sharding import PartitionSpec as P

ADAM_STEP = 200


beta_one = 0.9
beta_two = 0.999
learn_rate = 0.003
adam_eps = 1e-08
factor_scale = 2.0

CHUNKS = (1, 3, 4, 4, 4, 3, 1)


def apply_adam_rule(weights, moment, second, grads):
    moment_new = beta_one * moment + (1.0 - beta_one) * grads
    second_new = beta_two * second + (1.0 - beta_two) * grads * grads
    first_fix = 1.0 - beta_one**ADAM_STEP
    second_fix = 1.0 - beta_two**ADAM_STEP
    step_size = moment_new / first_fix / (jnp.sqrt(second_new / second_fix) + adam_eps)
    return (weights - learn_rate * step_size, moment_new, second_new)


def scatter_sum_rep(part):
    reps = lax.axis_size("rep")
    me = lax.axis_index("rep")
    share = part.shape[0] // reps
    blocks = part.reshape(reps, share, part.shape[1])
    bit = 1
    while bit < reps:
        pairs = blocks.reshape(blocks.shape[0] // 2, 2, share, part.shape[1])
        mine_bit = (me // bit) % 2
        keep = lax.dynamic_index_in_dim(pairs, mine_bit, 1, keepdims=False)
        send = lax.dynamic_index_in_dim(pairs, 1 - mine_bit, 1, keepdims=False)
        got = lax.ppermute(send.astype(jnp.bfloat16), "rep", [(i, i ^ bit) for i in range(reps)])
        blocks = keep + got.astype(jnp.float32)
        bit *= 2
    return blocks[0]


def split_high_low(values):
    high = values.astype(jnp.bfloat16)
    low = (values - high.astype(jnp.float32)).astype(jnp.bfloat16)
    return high, low


def after(value, *earlier):
    return lax.optimization_barrier((value,) + earlier)[0]


def line_step(k, partial, arrived, me, size, share):
    rows = (size - k) * share
    rightward = me == k - 1
    outgoing = lax.dynamic_slice_in_dim(partial, jnp.where(rightward, k * share, 0), rows, 0)
    if arrived is not None:
        passed = lax.dynamic_slice_in_dim(arrived, jnp.where(rightward, share, 0), rows, 0)
        outgoing = outgoing + passed.astype(jnp.float32)
    return lax.ppermute(outgoing.astype(jnp.bfloat16), "tp", [(k - 1, k), (size - k, size - k - 1)])


def line_total(partial, arrivals, me, size, share):
    total = lax.dynamic_slice_in_dim(partial, me * share, share, 0)
    for k, arrived in enumerate(arrivals, 1):
        offset = jnp.where(me == k, 0, (size - 1 - k) * share)
        total = total + lax.dynamic_slice_in_dim(arrived, offset, share, 0).astype(jnp.float32)
    return total


def chunk_bounds(width, weights):
    unit = width // sum(weights)
    bounds = [0]
    for weight in weights:
        bounds.append(bounds[-1] + weight * unit)
    bounds[-1] = width
    return bounds


def local(
    base,
    decoded_row_activations,
    input_factor,
    output_factor,
    input_first_moment,
    input_second_moment,
    output_first_moment,
    output_second_moment,
    replica_input_gradient,
    replica_output_gradient,
):
    x = decoded_row_activations
    width = base.shape[1]
    features = base.shape[0]
    reps, tps = lax.axis_size("rep"), lax.axis_size("tp")
    share = x.shape[0] // tps
    me = lax.axis_index("tp")
    in_line = tps in (2, 4)

    bounds = chunk_bounds(width, CHUNKS)
    partials, firsts = [], []
    previous = None
    for start, stop in zip(bounds[:-1], bounds[1:]):
        rows = x if previous is None else after(x, previous)
        partial = jnp.dot(rows, base[:, start:stop], preferred_element_type=jnp.float32)
        partials.append(partial)
        previous = partial
        if in_line:
            firsts.append(line_step(1, partial, None, me, tps, share))

    part = jnp.concatenate([replica_input_gradient[0].T, replica_output_gradient[0]], axis=1)
    part = after(part, partials[0])
    grads = scatter_sum_rep(part)
    grads_in, grads_out = grads[:, :features], grads[:, features:]
    new_in, first_in, second_in = apply_adam_rule(input_factor.T, input_first_moment.T, input_second_moment.T, grads_in)
    new_out, first_out, second_out = apply_adam_rule(output_factor, output_first_moment, output_second_moment, grads_out)
    half_in = new_in.astype(jnp.bfloat16)
    half_out = new_out.astype(jnp.bfloat16)

    inner = lax.dot_general(x, half_in, (((1,), (1,)), ((), ())), preferred_element_type=jnp.float32)
    inner = lax.psum_scatter(inner, "tp", scatter_dimension=0, tiled=True)
    inner = lax.all_gather(inner, "rep", axis=1, tiled=True)
    if reps == tps:
        turned = lax.ppermute(
            half_out, ("rep", "tp"), [(a * tps + b, b * tps + a) for a in range(reps) for b in range(tps)]
        )
        full_out = lax.all_gather(turned, "tp", axis=0, tiled=True)
    else:
        gathered = lax.all_gather(half_out, ("rep", "tp"), axis=1, tiled=True)
        stacked = gathered.reshape(half_out.shape[0], reps, -1)
        full_out = jnp.transpose(stacked, (1, 0, 2)).reshape(half_out.shape[0] * reps, -1)
        full_out = lax.dynamic_slice_in_dim(full_out, lax.axis_index("rep") * width, width, 1)

    high, low = split_high_low(factor_scale * inner)
    spread = jnp.concatenate([high, low], axis=1)
    doubled = jnp.concatenate([full_out, full_out], axis=0)
    decoded = jnp.zeros((share, width), jnp.float32)
    for index, (start, stop) in enumerate(zip(bounds[:-1], bounds[1:])):
        partial = partials[index]
        if in_line:
            arrivals = [firsts[index]]
            for k in range(2, tps):
                arrivals.append(line_step(k, partial, arrivals[-1], me, tps, share))
            total = line_total(partial, arrivals, me, tps, share)
        else:
            total = lax.psum_scatter(partial, "tp", scatter_dimension=0, tiled=True)
        change = jnp.dot(spread, doubled[:, start:stop], preferred_element_type=jnp.float32)
        decoded = lax.dynamic_update_slice(decoded, total + change, (0, start))
    return (decoded, new_in.T, new_out, first_in.T, second_in.T, first_out, second_out)


def solution(mesh):
    return jax.shard_map(
        local,
        mesh=mesh,
        in_specs=(
            P("tp", "rep"),
            P("groups", "tp"),
            P(("groups", "tp"), "rep"),
            P("rep", ("groups", "tp")),
            P(("groups", "tp"), "rep"),
            P(("groups", "tp"), "rep"),
            P("rep", ("groups", "tp")),
            P("rep", ("groups", "tp")),
            P("rep", ("groups", "tp"), None),
            P("rep", None, ("groups", "tp")),
        ),
        out_specs=(
            P(("groups", "tp"), "rep"),
            P(("groups", "tp"), "rep"),
            P("rep", ("groups", "tp")),
            P(("groups", "tp"), "rep"),
            P(("groups", "tp"), "rep"),
            P("rep", ("groups", "tp")),
            P("rep", ("groups", "tp")),
        ),
        check_vma=False,
    )
```

time: 434 us -> 278 us (0.64)
  waiting for transfers between devices: 252 us -> 82 us
  starting transfers between devices: 0.12 us -> 41.3 us
  matrix products: 85 us -> 57.6 us
  blocking collectives: 70 us -> 50.3 us
  other arithmetic: 7.86 us -> 17.2 us
  local copies, waits for them, and re-layouts: 4.91 us -> 13.8 us
    reduce_scatter x1 -> x0, waiting for transfers between devices: 177 us -> none  [local(): lax.psum_scatter(lax.dot_general(merged_weight, decoded_row_activations,...]
    all_to_all x1 -> x0, blocking collectives: 64.2 us -> none  [local(): lax.all_to_all(col_slab, 'tp', split_axis=1, concat_axis=0, tiled=True)]
    ppermute x0 -> x24, waiting for transfers between devices: none -> 64 us  [the longest x21 60.3 us: line_step(): lax.ppermute(outgoing.astype(jnp.bfloat16), 'tp', [(k - 1, k), (size - k,...]
    all_gather x1 -> x2, blocking collectives: 5.77 us -> 50.3 us  [the longest x1 45 us: local(): full_out = lax.all_gather(turned, 'tp', axis=0, tiled=True)]
    ppermute x0 -> x24, starting transfers between devices: none -> 41.3 us  [the longest x21 37.8 us: line_step(): lax.ppermute(outgoing.astype(jnp.bfloat16), 'tp', [(k - 1, k), (size - k,...]
    psum x1 -> x0, waiting for transfers between devices: 38.1 us -> none  [local(): lax.psum(part_in.astype(jnp.bfloat16), 'rep').astype(jnp.float32)]
    all_gather x1 -> x0, waiting for transfers between devices: 36.9 us -> none  [local(): gathered = lax.all_gather(half_out, ('rep', 'tp'), axis=1, tiled=True)]
    dot_general x1 -> x15, matrix products: 85 us -> 57.6 us  [the longest x7 48.7 us: local(): jnp.dot(rows, base[:, start:stop], preferred_element_type=jnp.float32)]
  transfers between devices with their start and end apart: 3 -> 25, of which waited for: 3 -> 7; matrix products, arithmetic and copies ran while one was open for 0% -> 28% of each run, Pallas kernels for 0% -> 0%
where the time goes in v1:
time: 278 us; the launch traced here: 277 us
  waiting for transfers between devices  82 us (29%)
  matrix products  57.6 us (21%)
  blocking collectives  50.3 us (18%)
  starting transfers between devices  41.3 us (15%)
  other arithmetic  17.2 us (6%)
  between operations  14.7 us (5%)
  local copies, waits for them, and re-layouts  13.8 us (5%)
    ppermute x21, waiting for transfers between devices, line_step(): lax.ppermute(outgoing.astype(jnp.bfloat16), 'tp', [(k - 1, k), (size - k,...  60.3 us
    dot_general x7, matrix products, local(): jnp.dot(rows, base[:, start:stop], preferred_element_type=jnp.float32)  48.7 us
    all_gather x1, blocking collectives, local(): full_out = lax.all_gather(turned, 'tp', axis=0, tiled=True)  45 us
    ppermute x21, starting transfers between devices, line_step(): lax.ppermute(outgoing.astype(jnp.bfloat16), 'tp', [(k - 1, k), (size - k,...  37.8 us
    unnamed x2, waiting for transfers between devices  18 us
    convert_element_type x14, other arithmetic, line_step(): outgoing.astype(jnp.bfloat16)  11.3 us
    dot_general x7, matrix products, local(): jnp.dot(spread, doubled[:, start:stop], preferred_element_type=jnp.float32)  8.24 us
    convert_element_type x7, local copies, waits for them, and re-layouts, line_step(): outgoing.astype(jnp.bfloat16)  6.35 us
  transfers between devices with their start and end apart: 25, of which 7 were waited for; matrix products, arithmetic and copies ran while one was open for 28% of the time, Pallas kernels for 0%

profile of v1, /device:TPU:0, one launch (start us, length us, event | category | flops | bytes accessed | tf_op | source)
XLA Modules:
  0.0 276.9 jit_solution(17564211378081667530)
XLA Ops:
  7.2 1.5 copy-done
  8.8 3.6 %fusion.12 = f32[256,512]{1,0:T(8,128)S(1)} fusion(bf16[256,4096]{1,0:T(8,128)(2,1)S(1)} %copy-done, bf16[4096,10240]{1,0:T(8,128)(2,1)} %param.10), kind=kOutput, calls=%fused_computation.12 | convolution fusion | flops 1073741824 | bytes 6815744 | tf_op jit(solution)/shard_map/dot_general | solution.py:106
  12.4 1.4 pad_maximum_fusion
  13.8 2.0 fusion.14
  16.2 5.2 %collective-permute-start = (bf16[192,512]{1,0:T(8,128)(2,1)S(1)}, bf16[192,512]{1,0:T(8,128)(2,1)}, u32[]{:S(2)}, u32[]{:S(2)}) collective-permute-start(bf16[192,512]{1,0:T(8,128)(2,1)S(1)} %dynamic-slice_convert_fusion.8), channel_id=1, source_target_pairs={{0,1},{3,2},{4,5},{7,6},{8,9},{11,10},{12,13},{15,14},{16,17},{19,... | collective-permute-start | bytes 589832 | tf_op jit(solution)/shard_map/ppermute | solution.py:61
  21.4 6.4 %fusion.8 = f32[256,1536]{1,0:T(8,128)S(1)} fusion(bf16[256,4096]{1,0:T(8,128)(2,1)S(1)} %copy-done, bf16[4096,10240]{1,0:T(8,128)(2,1)} %param.10), kind=kOutput, calls=%fused_computation.8 | convolution fusion | flops 3221225472 | bytes 16252928 | tf_op jit(solution)/shard_map/dot_general | solution.py:106
  29.2 2.1 collective-permute-start.6
  31.3 8.2 %fusion.4 = f32[256,2048]{1,0:T(8,128)S(1)} fusion(bf16[256,4096]{1,0:T(8,128)(2,1)S(1)} %copy-done, bf16[4096,10240]{1,0:T(8,128)(2,1)} %param.10), kind=kOutput, calls=%fused_computation.4 | convolution fusion | flops 4294967296 | bytes 20971520 | tf_op jit(solution)/shard_map/dot_general | solution.py:106
  40.7 2.2 collective-permute-start.9
  42.9 8.2 %fusion.2 = f32[256,2048]{1,0:T(8,128)S(1)} fusion(bf16[256,4096]{1,0:T(8,128)(2,1)S(1)} %copy-done, bf16[4096,10240]{1,0:T(8,128)(2,1)} %param.10), kind=kOutput, calls=%fused_computation.2 | convolution fusion | flops 4294967296 | bytes 20971520 | tf_op jit(solution)/shard_map/dot_general | solution.py:106
  51.1 8.9 %fusion = f32[256,2048]{1,0:T(8,128)S(1)} fusion(bf16[256,4096]{1,0:T(8,128)(2,1)S(1)} %copy-done, bf16[4096,10240]{1,0:T(8,128)(2,1)} %param.10), kind=kOutput, calls=%fused_computation | convolution fusion | flops 4294967296 | bytes 20971520 | tf_op jit(solution)/shard_map/dot_general | solution.py:106
  60.0 10.0 %fusion.6 = f32[256,1536]{1,0:T(8,128)} fusion(bf16[256,4096]{1,0:T(8,128)(2,1)S(1)} %copy-done, bf16[4096,10240]{1,0:T(8,128)(2,1)} %param.10), kind=kOutput, calls=%fused_computation.6 | convolution fusion | flops 3221225472 | bytes 16252928 | tf_op jit(solution)/shard_map/dot_general | solution.py:106
  70.0 3.4 %fusion.10 = f32[256,512]{1,0:T(8,128)S(1)} fusion(bf16[256,4096]{1,0:T(8,128)(2,1)S(1)} %copy-done, bf16[4096,10240]{1,0:T(8,128)(2,1)} %param.10), kind=kOutput, calls=%fused_computation.10 | convolution fusion | flops 1073741824 | bytes 6815744 | tf_op jit(solution)/shard_map/dot_general | solution.py:106
  73.5 2.0 collective-permute-start.21
  77.5 1.6 add_convert_fusion.11
  79.1 1.3 collective-permute-start.1
  82.2 2.2 dynamic-slice_convert_fusion.3
  84.4 7.6 %collective-permute-start.12 = (bf16[192,2048]{1,0:T(8,128)(2,1)}, bf16[192,2048]{1,0:T(8,128)(2,1)}, u32[]{:S(2)}, u32[]{:S(2)}) collective-permute-start(bf16[192,2048]{1,0:T(8,128)(2,1)} %dynamic-slice_convert_fusion.1), channel_id=1, source_target_pairs={{0,1},{3,2},{4,5},{7,6},{8,9},{11,10},{12,13},{15,14},{16,17},{19,... | collective-permute-start | bytes 2359304 | tf_op jit(solution)/shard_map/ppermute | solution.py:61
  91.9 1.5 add_convert_fusion.13
  93.4 2.2 collective-permute-start.15
  96.2 1.4 collective-permute-start.18
  97.7 1.4 bitcast_add_fusion
  99.2 1.4 collective-permute-start.2
  100.6 1.8 add_convert_fusion.4
  102.4 34.8 %collective-permute-done.18 = bf16[192,1536]{1,0:T(8,128)(2,1)S(1)} collective-permute-done((bf16[192,1536]{1,0:T(8,128)(2,1)}, bf16[192,1536]{1,0:T(8,128)(2,1)S(1)}, u32[]{:S(2)}, u32[]{:S(2)}) %collective-permute-start.18) | collective-permute-done | bytes 589856 | tf_op jit(solution)/shard_map/ppermute | solution.py:61
  137.2 1.5 collective-permute-start.4
  139.5 3.7 %collective-permute-done.4 = bf16[1,8,14336]{2,1,0:T(8,128)(2,1)S(1)} collective-permute-done((bf16[1,8,14336]{2,1,0:T(8,128)(2,1)S(1)}, bf16[1,8,14336]{2,1,0:T(8,128)(2,1)S(1)}, u32[]{:S(2)}, u32[]{:S(2)}) %collective-permute-start.4) | collective-permute-done | bytes 229408 | tf_op jit(solution)/shard_map/ppermute | solution.py:38
  143.3 1.3 collective-permute-start.23
  146.9 2.2 fusion.48
  149.1 18.0 %reduce-scatter.4.cloned.1.call-done = f32[64,8]{1,0:T(8,128)} async-done(((f32[256,8]{1,0:T(8,128)}), f32[64,8]{1,0:T(8,128)}) %reduce-scatter.4.cloned.1.call-update) | async-done | bytes 2064
  167.9 5.3 %all_gather.6 = f32[64,32]{0,1:T(8,128)S(1)} all-gather(f32[64,8]{0,1:T(8,128)S(1)} %copy.18), channel_id=1, replica_groups=mesh['groups'=2,'rep'=4,'tp'=4] {'rep'}, dimensions={1}, use_global_device_ids=true | all-gather | bytes 10240 | tf_op jit(solution)/shard_map/all_gather | solution.py:123
  174.1 1.5 add_convert_fusion.2
  177.4 1.6 collective-permute-start.5
  180.9 45.0 %all_gather.7 = bf16[32,10240]{1,0:T(8,128)(2,1)S(1)} all-gather(bf16[8,10240]{1,0:T(8,128)(2,1)S(1)} %collective-permute-done.5), channel_id=1, replica_groups=mesh['groups'=2,'rep'=4,'tp'=4] {'tp'}, dimensions={0}, use_global_device_ids=true | all-gather | bytes 819200 | tf_op jit(solution)/shard_map/all_gather | solution.py:128
  226.9 1.2 add_add_fusion
  229.2 1.3 collective-permute-start.8
  230.6 8.2 %collective-permute-done.8 = bf16[64,1536]{1,0:T(8,128)(2,1)S(1)} collective-permute-done((bf16[64,1536]{1,0:T(8,128)(2,1)S(1)}, bf16[64,1536]{1,0:T(8,128)(2,1)S(1)}, u32[]{:S(2)}, u32[]{:S(2)}) %collective-permute-start.8) | collective-permute-done | bytes 196640 | tf_op jit(solution)/shard_map/ppermute | solution.py:61
  238.8 1.3 collective-permute-start.20
  241.4 1.3 collective-permute-start.11
  242.8 1.3 collective-permute-start.14
  244.2 1.3 collective-permute-start.17
  245.5 8.4 %collective-permute-done.11 = bf16[64,2048]{1,0:T(8,128)(2,1)S(1)} collective-permute-done((bf16[64,2048]{1,0:T(8,128)(2,1)S(1)}, bf16[64,2048]{1,0:T(8,128)(2,1)S(1)}, u32[]{:S(2)}, u32[]{:S(2)}) %collective-permute-start.11) | collective-permute-done | bytes 262176 | tf_op jit(solution)/shard_map/ppermute | solution.py:61
  253.8 1.2 add_dynamic-update-slice_fusion.2
  255.0 4.4 %collective-permute-done.14 = bf16[64,2048]{1,0:T(8,128)(2,1)S(1)} collective-permute-done((bf16[64,2048]{1,0:T(8,128)(2,1)S(1)}, bf16[64,2048]{1,0:T(8,128)(2,1)S(1)}, u32[]{:S(2)}, u32[]{:S(2)}) %collective-permute-start.14) | collective-permute-done | bytes 262176 | tf_op jit(solution)/shard_map/ppermute | solution.py:61
  259.4 1.2 add_dynamic-update-slice_fusion.1
  260.7 4.4 %collective-permute-done.17 = bf16[64,2048]{1,0:T(8,128)(2,1)S(1)} collective-permute-done((bf16[64,2048]{1,0:T(8,128)(2,1)S(1)}, bf16[64,2048]{1,0:T(8,128)(2,1)S(1)}, u32[]{:S(2)}, u32[]{:S(2)}) %collective-permute-start.17) | collective-permute-done | bytes 262176 | tf_op jit(solution)/shard_map/ppermute | solution.py:61
  265.1 1.2 add_dynamic-update-slice_fusion
  268.6 1.5 copy-done.12
  (102 shorter events, 21.7 us)
Async XLA Ops:
  7.2 1.6 copy-start
  7.2 159.9 %reduce-scatter.4.cloned.1.call-start = ((), (), s32[]{:S(2)}) async-start(), calls=%async_computation.1 | async-start | bytes 163840
  8.8 3.6 %copy-start.13 = (f32[1,32,10240]{2,1,0:T(8,128)S(1)}, f32[1,32,10240]{2,1,0:T(8,128)}, u32[]{:S(2)}) copy-start(f32[1,32,10240]{2,1,0:T(8,128)} %param.19) | copy-start | bytes 3932164
  8.8 3.6 %copy-start.16 = (f32[1,4096,32]{1,2,0:T(8,128)S(1)}, f32[1,4096,32]{1,2,0:T(8,128)}, u32[]{:S(2)}) copy-start(f32[1,4096,32]{1,2,0:T(8,128)} %param.18) | copy-start | bytes 1572868
  12.3 79.6 %copy-start.14 = (f32[256,512]{1,0:T(8,128)}, f32[256,512]{1,0:T(8,128)S(1)}, u32[]{:S(2)}) copy-start(f32[256,512]{1,0:T(8,128)S(1)} %fusion.12) | copy-start | bytes 1572868
  15.8 80.4 %collective-permute-start.3 = (bf16[2,8,14336]{2,1,0:T(8,128)(2,1)}, bf16[2,8,14336]{2,1,0:T(8,128)(2,1)}, u32[]{:S(2)}, u32[]{:S(2)}) collective-permute-start(bf16[2,8,14336]{2,1,0:T(8,128)(2,1)} %fusion.14), channel_id=1, source_target_pairs={{0,4},{4,0},{8,12},{12,8},{1,5},{5,1},{9,13},{13,9},{2,6},{6,2},{1... | collective-permute-start | bytes 1376264 | tf_op jit(solution)/shard_map/ppermute | solution.py:38
  16.2 61.2 %collective-permute-start = (bf16[192,512]{1,0:T(8,128)(2,1)S(1)}, bf16[192,512]{1,0:T(8,128)(2,1)}, u32[]{:S(2)}, u32[]{:S(2)}) collective-permute-start(bf16[192,512]{1,0:T(8,128)(2,1)S(1)} %dynamic-slice_convert_fusion.8), channel_id=1, source_target_pairs={{0,1},{3,2},{4,5},{7,6},{8,9},{11,10},{12,13},{15,14},{16,17},{19,... | collective-permute-start | bytes 589832 | tf_op jit(solution)/shard_map/ppermute | solution.py:61
  29.2 69.9 %collective-permute-start.6 = (bf16[192,1536]{1,0:T(8,128)(2,1)}, bf16[192,1536]{1,0:T(8,128)(2,1)}, u32[]{:S(2)}, u32[]{:S(2)}) collective-permute-start(bf16[192,1536]{1,0:T(8,128)(2,1)} %dynamic-slice_convert_fusion.4), channel_id=1, source_target_pairs={{0,1},{3,2},{4,5},{7,6},{8,9},{11,10},{12,13},{15,14},{16,17},{19,... | collective-permute-start | bytes 1769480 | tf_op jit(solution)/shard_map/ppermute | solution.py:61
  39.5 3.3 %copy-start.5 = (f32[256,2048]{1,0:T(8,128)}, f32[256,2048]{1,0:T(8,128)S(1)}, u32[]{:S(2)}) copy-start(f32[256,2048]{1,0:T(8,128)S(1)} %fusion.4) | copy-start | bytes 6291460
  40.7 132.6 %collective-permute-start.9 = (bf16[192,2048]{1,0:T(8,128)(2,1)}, bf16[192,2048]{1,0:T(8,128)(2,1)}, u32[]{:S(2)}, u32[]{:S(2)}) collective-permute-start(bf16[192,2048]{1,0:T(8,128)(2,1)} %dynamic-slice_convert_fusion.2), channel_id=1, source_target_pairs={{0,1},{3,2},{4,5},{7,6},{8,9},{11,10},{12,13},{15,14},{16,17},{19,... | collective-permute-start | bytes 2359304 | tf_op jit(solution)/shard_map/ppermute | solution.py:61
  51.1 24.3 %copy-start.3 = (f32[256,2048]{1,0:T(8,128)}, f32[256,2048]{1,0:T(8,128)S(1)}, u32[]{:S(2)}) copy-start(f32[256,2048]{1,0:T(8,128)S(1)} %fusion.2) | copy-start | bytes 6291460
  60.0 16.4 %copy-start.1 = (f32[256,2048]{1,0:T(8,128)}, f32[256,2048]{1,0:T(8,128)S(1)}, u32[]{:S(2)}) copy-start(f32[256,2048]{1,0:T(8,128)S(1)} %fusion) | copy-start | bytes 6291460
  73.5 6.9 %collective-permute-start.21 = (bf16[192,512]{1,0:T(8,128)(2,1)S(1)}, bf16[192,512]{1,0:T(8,128)(2,1)}, u32[]{:S(2)}, u32[]{:S(2)}) collective-permute-start(bf16[192,512]{1,0:T(8,128)(2,1)S(1)} %dynamic-slice_convert_fusion.7), channel_id=1, source_target_pairs={{0,1},{3,2},{4,5},{7,6},{8,9},{11,10},{12,13},{15,14},{16,17},{19,... | collective-permute-start | bytes 589832 | tf_op jit(solution)/shard_map/ppermute | solution.py:61
  79.1 5.3 %collective-permute-start.1 = (bf16[128,512]{1,0:T(8,128)(2,1)}, bf16[128,512]{1,0:T(8,128)(2,1)}, u32[]{:S(2)}, u32[]{:S(2)}) collective-permute-start(bf16[128,512]{1,0:T(8,128)(2,1)} %add_convert_fusion.11), channel_id=1, source_target_pairs={{1,2},{2,1},{5,6},{6,5},{9,10},{10,9},{13,14},{14,13},{17,18},{18,... | collective-permute-start | bytes 393224 | tf_op jit(solution)/shard_map/ppermute | solution.py:61
  81.3 12.1 %collective-permute-start.22 = (bf16[128,512]{1,0:T(8,128)(2,1)S(1)}, bf16[128,512]{1,0:T(8,128)(2,1)S(1)}, u32[]{:S(2)}, u32[]{:S(2)}) collective-permute-start(bf16[128,512]{1,0:T(8,128)(2,1)S(1)} %add_convert_fusion.10), channel_id=1, source_target_pairs={{1,2},{2,1},{5,6},{6,5},{9,10},{10,9},{13,14},{14,13},{17,18},{18,... | collective-permute-start | bytes 393224 | tf_op jit(solution)/shard_map/ppermute | solution.py:61
  84.4 16.2 %copy-start.10 = (f32[256,1536]{1,0:T(8,128)S(1)}, f32[256,1536]{1,0:T(8,128)}, u32[]{:S(2)}) copy-start(f32[256,1536]{1,0:T(8,128)} %copy-done.9) | copy-start | bytes 4718596
  84.4 91.2 %collective-permute-start.12 = (bf16[192,2048]{1,0:T(8,128)(2,1)}, bf16[192,2048]{1,0:T(8,128)(2,1)}, u32[]{:S(2)}, u32[]{:S(2)}) collective-permute-start(bf16[192,2048]{1,0:T(8,128)(2,1)} %dynamic-slice_convert_fusion.1), channel_id=1, source_target_pairs={{0,1},{3,2},{4,5},{7,6},{8,9},{11,10},{12,13},{15,14},{16,17},{19,... | collective-permute-start | bytes 2359304 | tf_op jit(solution)/shard_map/ppermute | solution.py:61
  93.4 9.0 %copy-start.22 = (bf16[128,512]{1,0:T(8,128)(2,1)}, bf16[128,512]{1,0:T(8,128)(2,1)S(1)}, u32[]{:S(2)}) copy-start(bf16[128,512]{1,0:T(8,128)(2,1)S(1)} %collective-permute-done.22) | copy-start | bytes 393220
  93.4 84.0 %collective-permute-start.15 = (bf16[192,2048]{1,0:T(8,128)(2,1)}, bf16[192,2048]{1,0:T(8,128)(2,1)}, u32[]{:S(2)}, u32[]{:S(2)}) collective-permute-start(bf16[192,2048]{1,0:T(8,128)(2,1)} %dynamic-slice_convert_fusion), channel_id=1, source_target_pairs={{0,1},{3,2},{4,5},{7,6},{8,9},{11,10},{12,13},{15,14},{16,17},{19,... | collective-permute-start | bytes 2359304 | tf_op jit(solution)/shard_map/ppermute | solution.py:61
  96.2 42.5 %copy-start.7 = (f32[256,1536]{1,0:T(8,128)S(1)}, f32[256,1536]{1,0:T(8,128)}, u32[]{:S(2)}) copy-start(f32[256,1536]{1,0:T(8,128)} %fusion.6) | copy-start | bytes 4718596
  96.2 41.0 %collective-permute-start.18 = (bf16[192,1536]{1,0:T(8,128)(2,1)}, bf16[192,1536]{1,0:T(8,128)(2,1)S(1)}, u32[]{:S(2)}, u32[]{:S(2)}) collective-permute-start(bf16[192,1536]{1,0:T(8,128)(2,1)} %dynamic-slice_convert_fusion.3), channel_id=1, source_target_pairs={{0,1},{3,2},{4,5},{7,6},{8,9},{11,10},{12,13},{15,14},{16,17},{19,... | collective-permute-start | bytes 1769480 | tf_op jit(solution)/shard_map/ppermute | solution.py:61
  99.1 45.5 %copy-start.19 = (f32[4096,8]{0,1:T(8,128)S(1)}, f32[4096,8]{0,1:T(8,128)}, u32[]{:S(2)}) copy-start(f32[4096,8]{0,1:T(8,128)} %param.15) | copy-start | bytes 393220
  99.1 45.5 %copy-start.20 = (f32[4096,8]{0,1:T(8,128)S(1)}, f32[4096,8]{0,1:T(8,128)}, u32[]{:S(2)}) copy-start(f32[4096,8]{0,1:T(8,128)} %param.14) | copy-start | bytes 393220
  99.1 45.5 %copy-start.21 = (f32[4096,8]{0,1:T(8,128)S(1)}, f32[4096,8]{0,1:T(8,128)}, u32[]{:S(2)}) copy-start(f32[4096,8]{0,1:T(8,128)} %param.12) | copy-start | bytes 393220
  99.2 126.9 %collective-permute-start.2 = (bf16[64,512]{1,0:T(8,128)(2,1)}, bf16[64,512]{1,0:T(8,128)(2,1)}, u32[]{:S(2)}, u32[]{:S(2)}) collective-permute-start(bf16[64,512]{1,0:T(8,128)(2,1)} %add_convert_fusion.13), channel_id=1, source_target_pairs={{2,3},{1,0},{6,7},{5,4},{10,11},{9,8},{14,15},{13,12},{18,19},{17,... | collective-permute-start | bytes 196616 | tf_op jit(solution)/shard_map/ppermute | solution.py:61
  137.2 7.4 %copy-start.15 = (bf16[192,1536]{1,0:T(8,128)(2,1)}, bf16[192,1536]{1,0:T(8,128)(2,1)S(1)}, u32[]{:S(2)}) copy-start(bf16[192,1536]{1,0:T(8,128)(2,1)S(1)} %collective-permute-done.18) | copy-start | bytes 1769476
  137.2 6.0 %collective-permute-start.4 = (bf16[1,8,14336]{2,1,0:T(8,128)(2,1)S(1)}, bf16[1,8,14336]{2,1,0:T(8,128)(2,1)S(1)}, u32[]{:S(2)}, u32[]{:S(2)}) collective-permute-start(bf16[1,8,14336]{2,1,0:T(8,128)(2,1)S(1)} %dynamic-slice_convert_fusion.6), channel_id=1, source_target_pairs={{0,8},{4,12},{8,0},{12,4},{1,9},{5,13},{9,1},{13,5},{2,10},{6,14},... | collective-permute-start | bytes 688136 | tf_op jit(solution)/shard_map/ppermute | solution.py:38
  139.5 7.4 %copy-start.18 = (f32[8,10240]{1,0:T(8,128)S(1)}, f32[8,10240]{1,0:T(8,128)}, u32[]{:S(2)}) copy-start(f32[8,10240]{1,0:T(8,128)} %param.13) | copy-start | bytes 983044
  143.3 124.2 %collective-permute-start.23 = (bf16[64,512]{1,0:T(8,128)(2,1)}, bf16[64,512]{1,0:T(8,128)(2,1)}, u32[]{:S(2)}, u32[]{:S(2)}) collective-permute-start(bf16[64,512]{1,0:T(8,128)(2,1)} %add_convert_fusion.12), channel_id=1, source_target_pairs={{2,3},{1,0},{6,7},{5,4},{10,11},{9,8},{14,15},{13,12},{18,19},{17,... | collective-permute-start | bytes 196616 | tf_op jit(solution)/shard_map/ppermute | solution.py:61
  145.4 3.6 %copy-start.17 = (f32[8,4096]{1,0:T(8,128)}, f32[8,4096]{1,0:T(8,128)S(1)}, u32[]{:S(2)}) copy-start(f32[8,4096]{1,0:T(8,128)S(1)} %get-tuple-element.26) | copy-start | bytes 393220
  167.9 8.3 %copy-start.4 = (f32[256,2048]{1,0:T(8,128)S(1)}, f32[256,2048]{1,0:T(8,128)}, u32[]{:S(2)}) copy-start(f32[256,2048]{1,0:T(8,128)} %copy-done.3) | copy-start | bytes 6291460
  173.2 5.8 %copy-start.2 = (f32[256,2048]{1,0:T(8,128)S(1)}, f32[256,2048]{1,0:T(8,128)}, u32[]{:S(2)}) copy-start(f32[256,2048]{1,0:T(8,128)} %copy-done.1) | copy-start | bytes 6291460
  173.3 55.1 %collective-permute-start.7 = (bf16[128,1536]{1,0:T(8,128)(2,1)}, bf16[128,1536]{1,0:T(8,128)(2,1)S(1)}, u32[]{:S(2)}, u32[]{:S(2)}) collective-permute-start(bf16[128,1536]{1,0:T(8,128)(2,1)} %add_convert_fusion.4), channel_id=1, source_target_pairs={{1,2},{2,1},{5,6},{6,5},{9,10},{10,9},{13,14},{14,13},{17,18},{18,... | collective-permute-start | bytes 1179656 | tf_op jit(solution)/shard_map/ppermute | solution.py:61
  175.6 53.7 %collective-permute-start.19 = (bf16[128,1536]{1,0:T(8,128)(2,1)}, bf16[128,1536]{1,0:T(8,128)(2,1)S(1)}, u32[]{:S(2)}, u32[]{:S(2)}) collective-permute-start(bf16[128,1536]{1,0:T(8,128)(2,1)} %add_convert_fusion.3), channel_id=1, source_target_pairs={{1,2},{2,1},{5,6},{6,5},{9,10},{10,9},{13,14},{14,13},{17,18},{18,... | collective-permute-start | bytes 1179656 | tf_op jit(solution)/shard_map/ppermute | solution.py:61
  177.4 2.7 collective-permute-start.5
  180.2 61.1 %collective-permute-start.10 = (bf16[128,2048]{1,0:T(8,128)(2,1)S(1)}, bf16[128,2048]{1,0:T(8,128)(2,1)S(1)}, u32[]{:S(2)}, u32[]{:S(2)}) collective-permute-start(bf16[128,2048]{1,0:T(8,128)(2,1)S(1)} %add_convert_fusion.2), channel_id=1, source_target_pairs={{1,2},{2,1},{5,6},{6,5},{9,10},{10,9},{13,14},{14,13},{17,18},{18,... | collective-permute-start | bytes 1572872 | tf_op jit(solution)/shard_map/ppermute | solution.py:61
  226.0 3.2 %copy-start.11 = (f32[256,1536]{1,0:T(8,128)S(1)}, f32[256,1536]{1,0:T(8,128)}, u32[]{:S(2)}) copy-start(f32[256,1536]{1,0:T(8,128)} %copy-done.9) | copy-start | bytes 4718596
  226.0 4.5 %copy-start.8 = (f32[256,1536]{1,0:T(8,128)S(1)}, f32[256,1536]{1,0:T(8,128)}, u32[]{:S(2)}) copy-start(f32[256,1536]{1,0:T(8,128)} %fusion.6) | copy-start | bytes 4718596
  226.0 16.7 %collective-permute-start.13 = (bf16[128,2048]{1,0:T(8,128)(2,1)S(1)}, bf16[128,2048]{1,0:T(8,128)(2,1)S(1)}, u32[]{:S(2)}, u32[]{:S(2)}) collective-permute-start(bf16[128,2048]{1,0:T(8,128)(2,1)S(1)} %add_convert_fusion.1), channel_id=1, source_target_pairs={{1,2},{2,1},{5,6},{6,5},{9,10},{10,9},{13,14},{14,13},{17,18},{18,... | collective-permute-start | bytes 1572872 | tf_op jit(solution)/shard_map/ppermute | solution.py:61
  228.3 13.0 %copy-start.6 = (f32[256,2048]{1,0:T(8,128)S(1)}, f32[256,2048]{1,0:T(8,128)}, u32[]{:S(2)}) copy-start(f32[256,2048]{1,0:T(8,128)} %copy-done.5) | copy-start | bytes 6291460
  228.3 15.8 %collective-permute-start.16 = (bf16[128,2048]{1,0:T(8,128)(2,1)S(1)}, bf16[128,2048]{1,0:T(8,128)(2,1)S(1)}, u32[]{:S(2)}, u32[]{:S(2)}) collective-permute-start(bf16[128,2048]{1,0:T(8,128)(2,1)S(1)} %add_convert_fusion), channel_id=1, source_target_pairs={{1,2},{2,1},{5,6},{6,5},{9,10},{10,9},{13,14},{14,13},{17,18},{18,... | collective-permute-start | bytes 1572872 | tf_op jit(solution)/shard_map/ppermute | solution.py:61
  229.2 9.6 %collective-permute-start.8 = (bf16[64,1536]{1,0:T(8,128)(2,1)S(1)}, bf16[64,1536]{1,0:T(8,128)(2,1)S(1)}, u32[]{:S(2)}, u32[]{:S(2)}) collective-permute-start(bf16[64,1536]{1,0:T(8,128)(2,1)S(1)} %add_convert_fusion.9), channel_id=1, source_target_pairs={{2,3},{1,0},{6,7},{5,4},{10,11},{9,8},{14,15},{13,12},{18,19},{17,... | collective-permute-start | bytes 589832 | tf_op jit(solution)/shard_map/ppermute | solution.py:61
  238.8 27.4 %collective-permute-start.20 = (bf16[64,1536]{1,0:T(8,128)(2,1)S(1)}, bf16[64,1536]{1,0:T(8,128)(2,1)S(1)}, u32[]{:S(2)}, u32[]{:S(2)}) collective-permute-start(bf16[64,1536]{1,0:T(8,128)(2,1)S(1)} %add_convert_fusion.8), channel_id=1, source_target_pairs={{2,3},{1,0},{6,7},{5,4},{10,11},{9,8},{14,15},{13,12},{18,19},{17,... | collective-permute-start | bytes 589832 | tf_op jit(solution)/shard_map/ppermute | solution.py:61
  241.4 12.4 %collective-permute-start.11 = (bf16[64,2048]{1,0:T(8,128)(2,1)S(1)}, bf16[64,2048]{1,0:T(8,128)(2,1)S(1)}, u32[]{:S(2)}, u32[]{:S(2)}) collective-permute-start(bf16[64,2048]{1,0:T(8,128)(2,1)S(1)} %add_convert_fusion.7), channel_id=1, source_target_pairs={{2,3},{1,0},{6,7},{5,4},{10,11},{9,8},{14,15},{13,12},{18,19},{17,... | collective-permute-start | bytes 786440 | tf_op jit(solution)/shard_map/ppermute | solution.py:61
  242.8 16.7 %collective-permute-start.14 = (bf16[64,2048]{1,0:T(8,128)(2,1)S(1)}, bf16[64,2048]{1,0:T(8,128)(2,1)S(1)}, u32[]{:S(2)}, u32[]{:S(2)}) collective-permute-start(bf16[64,2048]{1,0:T(8,128)(2,1)S(1)} %add_convert_fusion.6), channel_id=1, source_target_pairs={{2,3},{1,0},{6,7},{5,4},{10,11},{9,8},{14,15},{13,12},{18,19},{17,... | collective-permute-start | bytes 786440 | tf_op jit(solution)/shard_map/ppermute | solution.py:61
  244.2 20.9 %collective-permute-start.17 = (bf16[64,2048]{1,0:T(8,128)(2,1)S(1)}, bf16[64,2048]{1,0:T(8,128)(2,1)S(1)}, u32[]{:S(2)}, u32[]{:S(2)}) collective-permute-start(bf16[64,2048]{1,0:T(8,128)(2,1)S(1)} %add_convert_fusion.5), channel_id=1, source_target_pairs={{2,3},{1,0},{6,7},{5,4},{10,11},{9,8},{14,15},{13,12},{18,19},{17,... | collective-permute-start | bytes 786440 | tf_op jit(solution)/shard_map/ppermute | solution.py:61
  260.7 6.8 %copy-start.23 = (bf16[128,512]{1,0:T(8,128)(2,1)S(1)}, bf16[128,512]{1,0:T(8,128)(2,1)}, u32[]{:S(2)}) copy-start(bf16[128,512]{1,0:T(8,128)(2,1)} %copy-done.22) | copy-start | bytes 393220
  268.6 1.5 copy-start.12
  (1 other events, 1.4 us)
Sparse Core Ops, SparseCore 0:
  147.0 20.0 reduce-scatter.3

commit v2 on v1

v2 whole, which is shorter than its diff:
```python
import jax
import jax.numpy as jnp
from jax import lax
from jax.experimental import pallas as pl
from jax.experimental.pallas import tpu as pltpu
from jax.sharding import PartitionSpec as P

ADAM_STEP = 200


beta_one = 0.9
beta_two = 0.999
learn_rate = 0.003
adam_eps = 1e-08
factor_scale = 2.0

CHUNKS = (1, 3, 6, 6, 3, 1)
VMEM_BYTES = 40 * 1024 * 1024


def apply_adam_rule(weights, moment, second, grads):
    moment_new = beta_one * moment + (1.0 - beta_one) * grads
    second_new = beta_two * second + (1.0 - beta_two) * grads * grads
    first_fix = 1.0 - beta_one**ADAM_STEP
    second_fix = 1.0 - beta_two**ADAM_STEP
    step_size = moment_new / first_fix / (jnp.sqrt(second_new / second_fix) + adam_eps)
    return (weights - learn_rate * step_size, moment_new, second_new)


def scatter_sum_rep(part):
    reps = lax.axis_size("rep")
    me = lax.axis_index("rep")
    share = part.shape[0] // reps
    blocks = part.reshape(reps, share, part.shape[1])
    bit = 1
    while bit < reps:
        pairs = blocks.reshape(blocks.shape[0] // 2, 2, share, part.shape[1])
        mine_bit = (me // bit) % 2
        keep = lax.dynamic_index_in_dim(pairs, mine_bit, 1, keepdims=False)
        send = lax.dynamic_index_in_dim(pairs, 1 - mine_bit, 1, keepdims=False)
        got = lax.ppermute(send.astype(jnp.bfloat16), "rep", [(i, i ^ bit) for i in range(reps)])
        blocks = keep + got.astype(jnp.float32)
        bit *= 2
    return blocks[0]


def split_high_low(values):
    high = values.astype(jnp.bfloat16)
    low = (values - high.astype(jnp.float32)).astype(jnp.bfloat16)
    return high, low


def local_any(
    base,
    decoded_row_activations,
    input_factor,
    output_factor,
    input_first_moment,
    input_second_moment,
    output_first_moment,
    output_second_moment,
    replica_input_gradient,
    replica_output_gradient,
):
    x = decoded_row_activations
    width = base.shape[1]
    features = base.shape[0]
    reps = lax.axis_size("rep")
    part = jnp.concatenate([replica_input_gradient[0].T, replica_output_gradient[0]], axis=1)
    grads = scatter_sum_rep(part)
    grads_in, grads_out = grads[:, :features], grads[:, features:]
    new_in, first_in, second_in = apply_adam_rule(input_factor.T, input_first_moment.T, input_second_moment.T, grads_in)
    new_out, first_out, second_out = apply_adam_rule(output_factor, output_first_moment, output_second_moment, grads_out)
    half_in = new_in.astype(jnp.bfloat16)
    half_out = new_out.astype(jnp.bfloat16)
    inner = lax.dot_general(x, half_in, (((1,), (1,)), ((), ())), preferred_element_type=jnp.float32)
    inner = lax.psum_scatter(inner, "tp", scatter_dimension=0, tiled=True)
    inner = lax.all_gather(inner, "rep", axis=1, tiled=True)
    gathered = lax.all_gather(half_out, ("rep", "tp"), axis=1, tiled=True)
    stacked = gathered.reshape(half_out.shape[0], reps, -1)
    full_out = jnp.transpose(stacked, (1, 0, 2)).reshape(half_out.shape[0] * reps, -1)
    full_out = lax.dynamic_slice_in_dim(full_out, lax.axis_index("rep") * width, width, 1)
    high, low = split_high_low(factor_scale * inner)
    spread = jnp.concatenate([high, low], axis=1)
    doubled = jnp.concatenate([full_out, full_out], axis=0)
    partial = jnp.dot(x, base, preferred_element_type=jnp.float32)
    summed = lax.psum_scatter(partial, "tp", scatter_dimension=0, tiled=True)
    decoded = summed + jnp.dot(spread, doubled, preferred_element_type=jnp.float32)
    return (decoded, new_in.T, new_out, first_in.T, second_in.T, first_out, second_out)


LINE = (((0, 1), (3, 2)), ((1, 2), (2, 1)), ((2, 3), (1, 0)))
(SEND_ROW, SECOND_AT, THIRD_AT, THIRD_FROM, OWN, FIRST_OWN, SECOND_OWN, ORDER, CORE_BIT, CHIP_BIT) = (
    0, 1, 2, 3, 4, 5, 6, 7, 11, 12)


def place_numbers(share):
    me, rep = lax.axis_index("tp"), lax.axis_index("rep")
    low = me < 2
    order = [me, me ^ 1, jnp.where(low, 2, 1), jnp.where(low, 3, 0)]
    numbers = [
        jnp.where(me == 0, share, 0),
        jnp.where(me == 1, 1, 0),
        jnp.where(me == 2, 3, 0),
        jnp.where(me == 2, 1, 0),
        me,
        jnp.where(me == 1, 0, 2),
        jnp.where(me == 2, 0, 1),
    ]
    numbers += [rank ^ rep for rank in order] + [rep & 1, rep >> 1]
    return jnp.stack([jnp.asarray(n, jnp.int32) for n in numbers])


def call(body, place, operands, specs, earlier, out_shapes, out_specs, grid=(1,), flops=0, moved=0, aliases=None):
    count = len(operands)

    def kernel(place_ref, *refs):
        body(place_ref, *refs[:count], *refs[count + len(earlier):])

    return pl.pallas_call(
        kernel,
        grid_spec=pltpu.PrefetchScalarGridSpec(
            num_scalar_prefetch=1,
            grid=grid,
            in_specs=list(specs) + [pl.BlockSpec(memory_space=pl.ANY)] * len(earlier),
            out_specs=out_specs,
        ),
        out_shape=out_shapes,
        input_output_aliases={} if aliases is None else aliases,
        compiler_params=pltpu.CompilerParams(vmem_limit_bytes=VMEM_BYTES),
        cost_estimate=pl.CostEstimate(flops=flops, bytes_accessed=moved, transcendentals=0),
    )(place, *operands, *earlier)


def whole(shape):
    return pl.BlockSpec(shape, lambda *_: (0,) * len(shape))


def block_width(start, width, most):
    block = most
    while start % block or width % block:
        block //= 2
    return block


def matmul_chunk(place, x, base, start, width, share, earlier, most):
    rows, depth = x.shape
    block = block_width(start, width, most)
    sent = rows - share

    def body(place_ref, x_ref, base_ref, partial_ref, send_ref):
        partial_ref[...] = jnp.dot(x_ref[...], base_ref[...], preferred_element_type=jnp.float32)
        row = pl.multiple_of(place_ref[SEND_ROW], share)
        send_ref[...] = partial_ref[pl.ds(row, sent), :].astype(jnp.bfloat16)

    return call(
        body,
        place,
        [x, base],
        [whole(x.shape), pl.BlockSpec((depth, block), lambda j, p: (0, start // block + j))],
        earlier,
        [jax.ShapeDtypeStruct((rows, width), jnp.float32), jax.ShapeDtypeStruct((sent, width), jnp.bfloat16)],
        [pl.BlockSpec((rows, block), lambda j, p: (0, j)), pl.BlockSpec((sent, block), lambda j, p: (0, j))],
        grid=(width // block,),
        flops=2 * rows * depth * width,
        moved=2 * depth * width,
    )


def add_second(place, partial, arrived, share, earlier):
    width = partial.shape[1]
    block = block_width(0, width, 1024) if width % 128 == 0 else width

    def body(place_ref, partial_ref, upper_ref, lower_ref, out_ref):
        out_ref[:share, :] = (partial_ref[:share, :] + upper_ref[...].astype(jnp.float32)).astype(out_ref.dtype)
        out_ref[share:, :] = (partial_ref[share:, :] + lower_ref[...].astype(jnp.float32)).astype(out_ref.dtype)

    return call(
        body,
        place,
        [partial, arrived, arrived],
        [
            pl.BlockSpec((2 * share, block), lambda j, p: (p[SECOND_AT], j)),
            pl.BlockSpec((share, block), lambda j, p: (p[SECOND_AT], j)),
            pl.BlockSpec((share, block), lambda j, p: (p[SECOND_AT] + 1, j)),
        ],
        earlier,
        jax.ShapeDtypeStruct((2 * share, width), arrived.dtype),
        pl.BlockSpec((2 * share, block), lambda j, p: (0, j)),
        grid=(width // block,),
        moved=16 * share * width,
    )


def add_third(place, partial, arrived, share, earlier):
    width = partial.shape[1]
    block = block_width(0, width, 1024) if width % 128 == 0 else width

    def body(place_ref, partial_ref, arrived_ref, out_ref):
        out_ref[...] = (partial_ref[...] + arrived_ref[...].astype(jnp.float32)).astype(out_ref.dtype)

    return call(
        body,
        place,
        [partial, arrived],
        [
            pl.BlockSpec((share, block), lambda j, p: (p[THIRD_AT], j)),
            pl.BlockSpec((share, block), lambda j, p: (p[THIRD_FROM], j)),
        ],
        earlier,
        jax.ShapeDtypeStruct((share, width), arrived.dtype),
        pl.BlockSpec((share, block), lambda j, p: (0, j)),
        grid=(width // block,),
        moved=8 * share * width,
    )


def own_block_specs(share, block):
    return [
        pl.BlockSpec((share, block), lambda j, p: (p[OWN], j)),
        pl.BlockSpec((share, block), lambda j, p: (p[FIRST_OWN], j)),
        pl.BlockSpec((share, block), lambda j, p: (p[SECOND_OWN], j)),
        pl.BlockSpec((share, block), lambda j, p: (0, j)),
    ]


def own_total(refs):
    total = refs[0][...]
    for ref in refs[1:]:
        total = total + ref[...].astype(jnp.float32)
    return total


def finish_chunk(place, terms, spread, factors, decoded, start, width, share, full_width, earlier):
    block = block_width(start, width, 1024)
    first = start // block
    operands = [*terms, spread, *factors]

    def body(place_ref, own_ref, one_ref, two_ref, three_ref, spread_ref, pair_ref, near_ref, far_ref, *rest):
        other = near_ref[...] + far_ref[...]
        ranks = jnp.concatenate([pair_ref[...], other, pair_ref[...], other], axis=0)
        change = jnp.dot(spread_ref[...], ranks, preferred_element_type=jnp.float32)
        rest[-1][...] = own_total((own_ref, one_ref, two_ref, three_ref)) + change

    half = factors[0].shape[0]
    specs = own_block_specs(share, block) + [whole(spread.shape)]
    specs += [pl.BlockSpec((half, block), lambda j, p: (0, first + j))] * 3
    aliases = None
    if decoded is not None:
        aliases = {1 + len(operands): 0}
        operands.append(decoded)
        specs.append(pl.BlockSpec(memory_space=pl.ANY))
    return call(
        body,
        place,
        operands,
        specs,
        earlier,
        jax.ShapeDtypeStruct((share, full_width), jnp.float32),
        pl.BlockSpec((share, block), lambda j, p: (0, first + j)),
        grid=(width // block,),
        moved=14 * share * width,
        aliases=aliases,
    )


def gradients_out(place, part_in, part_out, earlier):
    features, columns = part_in.shape[3], part_out.shape[3]
    rows = 2 * part_in.shape[2]

    def body(place_ref, in_ref, out_ref, send_ref):
        send_ref[:, :features] = in_ref[...].reshape(rows, features).astype(jnp.bfloat16)
        send_ref[:, features:] = out_ref[...].reshape(rows, columns).astype(jnp.bfloat16)

    shape = (rows, features + columns)
    return call(
        body,
        place,
        [part_in, part_out],
        [
            pl.BlockSpec((2, 1, rows // 2, n), lambda j, p: (0, 1 - p[CORE_BIT], 0, 0))
            for n in (features, columns)
        ],
        earlier,
        jax.ShapeDtypeStruct(shape, jnp.bfloat16),
        whole(shape),
        moved=6 * shape[0] * shape[1],
    )


def gradients_on(place, part_in, part_out, arrived, earlier):
    features, columns = part_in.shape[3], part_out.shape[3]
    ranks = part_in.shape[2]

    def body(place_ref, in_ref, out_ref, arrived_ref, send_ref, keep_ref):
        upper = place_ref[CHIP_BIT] == 0
        for ref, at, n in ((in_ref, 0, features), (out_ref, features, columns)):
            total = ref[...].reshape(2 * ranks, n) + arrived_ref[:, at:at + n].astype(jnp.float32)
            keep_ref[:, at:at + n] = jnp.where(upper, total[:ranks], total[ranks:])
            send_ref[:, at:at + n] = jnp.where(upper, total[ranks:], total[:ranks]).astype(jnp.bfloat16)

    shape = (ranks, features + columns)
    return call(
        body,
        place,
        [part_in, part_out, arrived],
        [pl.BlockSpec((2, 1, ranks, n), lambda j, p: (0, p[CORE_BIT], 0, 0)) for n in (features, columns)]
        + [whole(arrived.shape)],
        earlier,
        [jax.ShapeDtypeStruct(shape, jnp.bfloat16), jax.ShapeDtypeStruct(shape, jnp.float32)],
        [whole(shape)] * 2,
        moved=20 * shape[0] * shape[1],
    )


def update_factors(place, keep, arrived, in_state, out_state, earlier):
    features, columns = in_state[0].shape[1], out_state[0].shape[1]
    ranks = keep.shape[0]

    def body(place_ref, keep_ref, arrived_ref, *refs):
        for side, at, n in ((0, 0, features), (1, features, columns)):
            weights, first, second = refs[3 * side:3 * side + 3]
            outs = refs[6 + 4 * side:10 + 4 * side]
            grads = keep_ref[:, at:at + n] + arrived_ref[:, at:at + n].astype(jnp.float32)
            values = apply_adam_rule(weights[...], first[...], second[...], grads)
            for out, value in zip(outs, values):
                out[...] = value
            outs[3][...] = values[0].astype(jnp.bfloat16)

    operands = [keep, arrived, *in_state, *out_state]
    shapes = []
    for n in (features, columns):
        shapes += [jax.ShapeDtypeStruct((ranks, n), jnp.float32)] * 3 + [jax.ShapeDtypeStruct((ranks, n), jnp.bfloat16)]
    return call(
        body,
        place,
        operands,
        [whole(o.shape) for o in operands],
        earlier,
        shapes,
        [whole(s.shape) for s in shapes],
        moved=32 * ranks * (features + columns),
    )


def inner_products(place, x, near, far, share, earlier):
    rows, ranks = x.shape[0], 2 * near.shape[0]
    sent = rows - share

    def body(place_ref, x_ref, near_ref, far_ref, inner_ref, send_ref):
        half = ranks // 2
        for at, ref in ((0, near_ref), (half, far_ref)):
            inner_ref[:, at:at + half] = lax.dot_general(
                x_ref[...], ref[...], (((1,), (1,)), ((), ())), preferred_element_type=jnp.float32
            )
        send_ref[...] = inner_ref[pl.ds(pl.multiple_of(place_ref[SEND_ROW], share), sent), :]

    return call(
        body,
        place,
        [x, near, far],
        [whole(x.shape), whole(near.shape), whole(far.shape)],
        earlier,
        [jax.ShapeDtypeStruct((rows, ranks), jnp.float32), jax.ShapeDtypeStruct((sent, ranks), jnp.float32)],
        [whole((rows, ranks)), whole((sent, ranks))],
        flops=2 * rows * ranks * x.shape[1],
        moved=2 * rows * x.shape[1],
    )


def spread_inner(place, terms, share, earlier):
    ranks = terms[0].shape[1]
    portion = ranks // 4

    def body(place_ref, own_ref, one_ref, two_ref, three_ref, out_ref):
        inner = factor_scale * own_total((own_ref, one_ref, two_ref, three_ref))
        block = lax.broadcasted_iota(jnp.int32, (ranks, ranks), 1) // portion
        source = jnp.full((ranks, ranks), 0, jnp.int32)
        for i in range(4):
            source = jnp.where(block == i, place_ref[ORDER + i], source)
        column = lax.broadcasted_iota(jnp.int32, (ranks, ranks), 1) % portion
        chosen = lax.broadcasted_iota(jnp.int32, (ranks, ranks), 0) == source * portion + column
        chosen = jnp.where(chosen, 1.0, 0.0).astype(jnp.bfloat16)
        halves = [
            jnp.dot(half, chosen, preferred_element_type=jnp.float32) for half in split_high_low(inner)
        ]
        out_ref[...] = jnp.concatenate(halves, axis=1).astype(jnp.bfloat16)

    return call(
        body,
        place,
        list(terms),
        own_block_specs(share, ranks),
        earlier,
        jax.ShapeDtypeStruct((share, 2 * ranks), jnp.bfloat16),
        whole((share, 2 * ranks)),
    )


def local_line(
    base,
    decoded_row_activations,
    input_factor,
    output_factor,
    input_first_moment,
    input_second_moment,
    output_first_moment,
    output_second_moment,
    replica_input_gradient,
    replica_output_gradient,
):
    x = decoded_row_activations
    width = base.shape[1]
    share = x.shape[0] // 4
    ranks = input_factor.shape[1]
    place = place_numbers(share)
    part_in = replica_input_gradient[0].T.reshape(2, 2, ranks, -1)
    part_out = replica_output_gradient[0].reshape(2, 2, ranks, -1)

    unit = width // sum(CHUNKS)
    widths = [unit * c for c in CHUNKS]
    starts = [sum(widths[:i]) for i in range(len(widths))]
    count = len(widths)
    partials, seconds, thirds, arrived = {}, {}, {}, {}

    def line(step, values):
        return lax.ppermute(values, "tp", LINE[step])

    def chip(bit, values):
        return lax.ppermute(values, "rep", [(i, i ^ bit) for i in range(4)])

    def matmul(c, *earlier):
        most = 256 if c == 0 else 512
        partials[c], send = matmul_chunk(place, x, base, starts[c], widths[c], share, earlier, most)
        arrived[c, 0] = line(0, send)
        return send

    def second(c, *earlier):
        seconds[c] = add_second(place, partials[c], arrived[c, 0], share, earlier)
        arrived[c, 1] = line(1, seconds[c])
        return seconds[c]

    def third(c, *earlier):
        thirds[c] = add_third(place, partials[c], arrived[c, 1], share, earlier)
        arrived[c, 2] = line(2, thirds[c])
        return thirds[c]

    last = matmul(0)
    last = matmul(1, last)
    last = matmul(2, last)
    last = gradients_out(place, part_in, part_out, [last])
    from_core = chip(1, last)
    last = second(0, last)
    last = matmul(3, last)
    across, keep = gradients_on(place, part_in, part_out, from_core, [last])
    from_chip = chip(2, across)
    last = second(1, keep)
    last = third(0, last)
    in_state = (input_factor.T, input_first_moment.T, input_second_moment.T)
    out_state = (output_factor, output_first_moment, output_second_moment)
    states = update_factors(place, keep, from_chip, in_state, out_state, [last])
    new_in, first_in, second_in, half_in, new_out, first_out, second_out, half_out = states
    near_in = jnp.concatenate([half_in, chip(1, half_in)], axis=0)
    far_in = chip(2, near_in)
    turned = lax.ppermute(half_out, ("rep", "tp"), [(4 * a + b, 4 * b + a) for a in range(4) for b in range(4)])
    last = second(2, half_out)
    last = matmul(4, last)
    last = matmul(5, last)
    last = third(1, last)
    inner, inner_send = inner_products(place, x, near_in, far_in, share, [last])
    inner_arrived = [line(0, inner_send)]
    last = third(2, inner_send)
    pair = jnp.concatenate([turned, lax.ppermute(turned, "tp", [(i, i ^ 1) for i in range(4)])], axis=0)
    near_out = line(1, pair)
    inner_second = add_second(place, inner, inner_arrived[0], share, [last])
    inner_arrived.append(line(1, inner_second))
    far_out = line(2, near_out)
    last = second(3, inner_second)
    inner_third = add_third(place, inner, inner_arrived[1], share, [last])
    inner_arrived.append(line(2, inner_third))
    last = second(4, inner_third)
    last = third(3, last)
    spread = spread_inner(place, (inner, *inner_arrived), share, [last])

    decoded = None

    def finish(c, decoded, *earlier):
        terms = (partials[c], arrived[c, 0], arrived[c, 1], arrived[c, 2])
        return finish_chunk(
            place, terms, spread, (pair, near_out, far_out), decoded, starts[c], widths[c], share, width, earlier
        )

    decoded = finish(0, None)
    decoded = finish(1, decoded)
    last = second(5, decoded)
    last = third(4, last)
    decoded = finish(2, decoded, last)
    last = third(5, decoded)
    for c in range(3, count):
        decoded = finish(c, decoded, last)
    return (decoded, new_in.T, new_out, first_in.T, second_in.T, first_out, second_out)


def solution(mesh):
    line = mesh.shape["rep"] == 4 and mesh.shape["tp"] == 4
    return jax.shard_map(
        local_line if line else local_any,
        mesh=mesh,
        in_specs=(
            P("tp", "rep"),
            P("groups", "tp"),
            P(("groups", "tp"), "rep"),
            P("rep", ("groups", "tp")),
            P(("groups", "tp"), "rep"),
            P(("groups", "tp"), "rep"),
            P("rep", ("groups", "tp")),
            P("rep", ("groups", "tp")),
            P("rep", ("groups", "tp"), None),
            P("rep", None, ("groups", "tp")),
        ),
        out_specs=(
            P(("groups", "tp"), "rep"),
            P(("groups", "tp"), "rep"),
            P("rep", ("groups", "tp")),
            P(("groups", "tp"), "rep"),
            P(("groups", "tp"), "rep"),
            P("rep", ("groups", "tp")),
            P("rep", ("groups", "tp")),
        ),
        check_vma=False,
    )
```

time: 278 us -> 198 us (0.71)
  Pallas kernels: 0 us -> 77.4 us
  matrix products: 57.6 us -> 0 us
  blocking collectives: 50.3 us -> 0 us
  waiting for transfers between devices: 82 us -> 38.8 us
  starting transfers between devices: 41.3 us -> 71.5 us
  other arithmetic: 17.2 us -> 0 us
  between operations: 14.7 us -> 1.38 us
  local copies, waits for them, and re-layouts: 13.8 us -> 5.25 us
    pallas_call x0 -> x31, Pallas kernels: none -> 77.4 us  [call(): pl.pallas_call(kernel, grid_spec=pltpu.PrefetchScalarGridSpec(num_scalar_...]
    dot_general x15 -> x0, matrix products: 57.6 us -> none  [the longest x7 48.7 us: local(): jnp.dot(rows, base[:, start:stop], preferred_element_type=jnp.float32)]
    all_gather x2 -> x0, blocking collectives: 50.3 us -> none  [the longest x1 45 us: local(): full_out = lax.all_gather(turned, 'tp', axis=0, tiled=True)]
    ppermute x24 -> x29, starting transfers between devices: 41.3 us -> 71.5 us  [the longest x23 41.2 us: line(): return lax.ppermute(values, 'tp', LINE[step])]
    ppermute x24 -> x29, waiting for transfers between devices: 64 us -> 38.8 us  [the longest x23 38.2 us: line(): return lax.ppermute(values, 'tp', LINE[step])]
    unnamed x2 -> x0, waiting for transfers between devices: 18 us -> none
    convert_element_type x16 -> x0, other arithmetic: 13.5 us -> none  [the longest x14 11.3 us: line_step(): outgoing.astype(jnp.bfloat16)]
    convert_element_type x9 -> x0, local copies, waits for them, and re-layouts: 8.37 us -> none  [the longest x7 6.35 us: line_step(): outgoing.astype(jnp.bfloat16)]
  transfers between devices with their start and end apart: 25 -> 29, of which waited for: 7 -> 5; matrix products, arithmetic and copies ran while one was open for 28% -> 0% of each run, Pallas kernels for 0% -> 37%
where the time goes in v2:
time: 198 us; the launch traced here: 194 us
  Pallas kernels  77.4 us (39%)
  starting transfers between devices  71.5 us (36%)
  waiting for transfers between devices  38.8 us (20%)
  local copies, waits for them, and re-layouts  5.25 us (3%)
    pallas_call x31, Pallas kernels, call(): pl.pallas_call(kernel, grid_spec=pltpu.PrefetchScalarGridSpec(num_scalar_...  77.4 us
    ppermute x23, starting transfers between devices, line(): return lax.ppermute(values, 'tp', LINE[step])  41.2 us
    ppermute x23, waiting for transfers between devices, line(): return lax.ppermute(values, 'tp', LINE[step])  38.2 us
    ppermute x1, starting transfers between devices, local_line(): lax.ppermute(turned, 'tp', [(i, i ^ 1) for i in range(4)])  23.8 us
    ppermute x4, starting transfers between devices, chip(): return lax.ppermute(values, 'rep', [(i, i ^ bit) for i in range(4)])  5.85 us
    unnamed x26, local copies, waits for them, and re-layouts  5.14 us
  transfers between devices with their start and end apart: 29, of which 5 were waited for; matrix products, arithmetic and copies ran while one was open for 0% of the time, Pallas kernels for 37%

profile of v2, /device:TPU:0, one launch (start us, length us, event | category | flops | bytes accessed | tf_op | source)
XLA Modules:
  0.0 194.3 jit_solution(6740617413606435129)
XLA Ops:
  0.8 1.6 copy-done.2
  2.4 3.7 %shard_map.153 = (f32[256,512]{1,0:T(8,128)S(1)}, bf16[192,512]{1,0:T(8,128)(2,1)S(1)}) custom-call(s32[13]{0:T(128)S(1)} %stack.55.place_ref, bf16[256,4096]{1,0:T(8,128)(2,1)S(1)} %copy-done.2, bf16[4096,10240]{1,0:T(8,128)(2,1)} %refs_1_.11), custom_call_target="tpu_custom_call" | custom-call | flops 1073741824 | bytes 4194304 | tf_op jit(solution)/shard_map/pallas_call | solution.py:120
  6.1 4.9 %collective-permute-start.2 = (bf16[192,512]{1,0:T(8,128)(2,1)S(1)}, bf16[192,512]{1,0:T(8,128)(2,1)S(1)}, u32[]{:S(2)}, u32[]{:S(2)}) collective-permute-start(bf16[192,512]{1,0:T(8,128)(2,1)S(1)} %get-tuple-element.31.refs_2_), channel_id=1, source_target_pairs={{0,1},{3,2},{4,5},{7,6},{8,9},{11,10},{12,13},{15,14},{16,17},{19,... | collective-permute-start | bytes 589832 | tf_op jit(solution)/shard_map/ppermute | solution.py:427
  11.0 7.7 %shard_map.154 = (f32[256,1536]{1,0:T(8,128)S(1)}, bf16[192,1536]{1,0:T(8,128)(2,1)S(1)}) custom-call(s32[13]{0:T(128)S(1)} %stack.55.place_ref, bf16[256,4096]{1,0:T(8,128)(2,1)S(1)} %copy-done.2, bf16[4096,10240]{1,0:T(8,128)(2,1)} %refs_1_.11, bf16[192,512]{1,0:T(8,128)(2,1)S(1)} %get-tuple-element.31.refs_2_), custom_call_target="tpu_custom_call" | custom-call | flops 3221225472 | bytes 12582912 | tf_op jit(solution)/shard_map/pallas_call | solution.py:120
  18.7 1.5 collective-permute-start.5
  20.2 12.9 %shard_map.155 = (f32[256,3072]{1,0:T(8,128)S(1)}, bf16[192,3072]{1,0:T(8,128)(2,1)S(1)}) custom-call(s32[13]{0:T(128)S(1)} %stack.55.place_ref, bf16[256,4096]{1,0:T(8,128)(2,1)S(1)} %copy-done.2, bf16[4096,10240]{1,0:T(8,128)(2,1)} %refs_1_.11, bf16[192,1536]{1,0:T(8,128)(2,1)S(1)} %get-tuple-element.32.refs_2_), custom_call_target="tpu_custom_call" | custom-call | flops 6442450944 | bytes 25165824 | tf_op jit(solution)/shard_map/pallas_call | solution.py:120
  33.2 1.5 collective-permute-start
  36.0 12.9 %shard_map.158 = (f32[256,3072]{1,0:T(8,128)S(1)}, bf16[192,3072]{1,0:T(8,128)(2,1)S(1)}) custom-call(s32[13]{0:T(128)S(1)} %stack.55.place_ref, bf16[256,4096]{1,0:T(8,128)(2,1)S(1)} %copy-done.3, bf16[4096,10240]{1,0:T(8,128)(2,1)} %refs_1_.11, bf16[128,512]{1,0:T(8,128)(2,1)S(1)} %shard_map.157.refs_2_), custom_call_target="tpu_custom_call" | custom-call | flops 6442450944 | bytes 25165824 | tf_op jit(solution)/shard_map/pallas_call | solution.py:120
  49.7 1.6 collective-permute-start.3
  51.9 4.1 %collective-permute-start.14 = (bf16[192,3072]{1,0:T(8,128)(2,1)S(1)}, bf16[192,3072]{1,0:T(8,128)(2,1)S(1)}, u32[]{:S(2)}, u32[]{:S(2)}) collective-permute-start(bf16[192,3072]{1,0:T(8,128)(2,1)S(1)} %get-tuple-element.36.refs_3_), channel_id=1, source_target_pairs={{0,1},{3,2},{4,5},{7,6},{8,9},{11,10},{12,13},{15,14},{16,17},{19,... | collective-permute-start | bytes 3538952 | tf_op jit(solution)/shard_map/ppermute | solution.py:427
  56.0 0.9 shard_map.160.refs_2_
  58.2 1.9 shard_map.162
  61.3 4.2 %collective-permute-start.10 = (bf16[16,4096]{1,0:T(8,128)(2,1)S(1)}, bf16[16,4096]{1,0:T(8,128)(2,1)S(1)}, u32[]{:S(2)}, u32[]{:S(2)}) collective-permute-start(bf16[16,4096]{1,0:T(8,128)(2,1)S(1)} %constant_dynamic-update-slice_fusion.refs_1_), channel_id=1, source_target_pairs={{0,8},{4,12},{8,0},{12,4},{1,9},{5,13},{9,1},{13,5},{2,10},{6,14},... | collective-permute-start | bytes 393224 | tf_op jit(solution)/shard_map/ppermute | solution.py:430
  65.5 23.8 %collective-permute-start.19 = (bf16[8,10240]{1,0:T(8,128)(2,1)S(1)}, bf16[8,10240]{1,0:T(8,128)(2,1)S(1)}, u32[]{:S(2)}, u32[]{:S(2)}) collective-permute-start(bf16[8,10240]{1,0:T(8,128)(2,1)S(1)} %collective-permute-done.18), channel_id=1, source_target_pairs={{0,1},{1,0},{2,3},{3,2},{4,5},{5,4},{6,7},{7,6},{8,9},{9,8},{10,11... | collective-permute-start | bytes 491528 | tf_op jit(solution)/shard_map/ppermute | solution.py:473
  89.3 1.0 shard_map.163.refs_2_
  91.1 7.7 %shard_map.164 = (f32[256,1536]{1,0:T(8,128)S(1)}, bf16[192,1536]{1,0:T(8,128)(2,1)S(1)}) custom-call(s32[13]{0:T(128)S(1)} %stack.55.place_ref, bf16[256,4096]{1,0:T(8,128)(2,1)S(1)} %copy-done.3, bf16[4096,10240]{1,0:T(8,128)(2,1)} %refs_1_.11, bf16[128,3072]{1,0:T(8,128)(2,1)S(1)} %shard_map.163.refs_2_), custom_call_target="tpu_custom_call" | custom-call | flops 3221225472 | bytes 12582912 | tf_op jit(solution)/shard_map/pallas_call | solution.py:120
  98.8 4.0 %shard_map.165 = (f32[256,512]{1,0:T(8,128)S(1)}, bf16[192,512]{1,0:T(8,128)(2,1)S(1)}) custom-call(s32[13]{0:T(128)S(1)} %stack.55.place_ref, bf16[256,4096]{1,0:T(8,128)(2,1)S(1)} %copy-done.3, bf16[4096,10240]{1,0:T(8,128)(2,1)} %refs_1_.11, bf16[192,1536]{1,0:T(8,128)(2,1)S(1)} %get-tuple-element.41.refs_2_), custom_call_target="tpu_custom_call" | custom-call | flops 1073741824 | bytes 4194304 | tf_op jit(solution)/shard_map/pallas_call | solution.py:120
  102.8 0.8 shard_map.166.refs_3_
  103.6 1.8 shard_map.167
  105.5 7.5 %collective-permute-start.11 = (f32[192,32]{1,0:T(8,128)S(1)}, f32[192,32]{1,0:T(8,128)S(1)}, u32[]{:S(2)}, u32[]{:S(2)}) collective-permute-start(f32[192,32]{1,0:T(8,128)S(1)} %get-tuple-element.46.refs_2_), channel_id=1, source_target_pairs={{0,1},{3,2},{4,5},{7,6},{8,9},{11,10},{12,13},{15,14},{16,17},{19,... | collective-permute-start | bytes 73736 | tf_op jit(solution)/shard_map/ppermute | solution.py:427
  113.0 1.3 collective-permute-start.17
  114.4 0.8 shard_map.168.refs_3_
  115.2 1.0 collective-permute-done.11.refs_1_.refs_2_
  116.8 1.0 shard_map.170.refs_2_
  117.8 0.7 collective-permute-start.16
  119.3 1.3 collective-permute-start.21
  121.8 3.1 %collective-permute-done.17.refs_1_.refs_2_ = bf16[192,1536]{1,0:T(8,128)(2,1)S(1)} collective-permute-done((bf16[192,1536]{1,0:T(8,128)(2,1)S(1)}, bf16[192,1536]{1,0:T(8,128)(2,1)S(1)}, u32[]{:S(2)}, u32[]{:S(2)}) %collective-permute-start.17) | collective-permute-done | bytes 589856 | tf_op jit(solution)/shard_map/ppermute | solution.py:427
  124.9 0.9 shard_map.172.refs_2_
  126.5 1.3 collective-permute-start.22
  127.8 1.3 collective-permute-start.24
  129.1 30.3 %collective-permute-done.22.refs_3_ = bf16[64,512]{1,0:T(8,128)(2,1)S(1)} collective-permute-done((bf16[64,512]{1,0:T(8,128)(2,1)S(1)}, bf16[64,512]{1,0:T(8,128)(2,1)S(1)}, u32[]{:S(2)}, u32[]{:S(2)}) %collective-permute-start.22) | collective-permute-done | bytes 65568 | tf_op jit(solution)/shard_map/ppermute | solution.py:427
  159.4 1.3 collective-permute-start.15
  160.7 1.3 collective-permute-start.8
  162.0 4.6 %collective-permute-start.6 = (bf16[192,512]{1,0:T(8,128)(2,1)S(1)}, bf16[192,512]{1,0:T(8,128)(2,1)S(1)}, u32[]{:S(2)}, u32[]{:S(2)}) collective-permute-start(bf16[192,512]{1,0:T(8,128)(2,1)S(1)} %get-tuple-element.43.refs_2_), channel_id=1, source_target_pairs={{0,1},{3,2},{4,5},{7,6},{8,9},{11,10},{12,13},{15,14},{16,17},{19,... | collective-permute-start | bytes 589832 | tf_op jit(solution)/shard_map/ppermute | solution.py:427
  166.6 0.8 shard_map.173.refs_4_
  167.4 1.3 collective-permute-start.28
  169.4 1.4 shard_map.175.refs_8_
  170.8 2.3 %shard_map.176.refs_3_.refs_8_ = f32[64,10240]{1,0:T(8,128)} custom-call(s32[13]{0:T(128)S(1)} %stack.55.place_ref, f32[256,1536]{1,0:T(8,128)S(1)} %get-tuple-element.39.refs_0_, bf16[192,1536]{1,0:T(8,128)(2,1)S(1)} %collective-permute-done.5.refs_1_.refs_2_, ...), custom_call_target="tpu_custom_call", output_to_operand_aliasing={{}: (9, {})} | custom-call | bytes 1376256 | tf_op jit(solution)/shard_map/pallas_call | solution.py:120
  173.2 1.7 copy-done
  175.5 0.8 shard_map.178.refs_9_
  176.3 1.3 collective-permute-start.27
  178.3 2.5 %shard_map.179.refs_2_.refs_8_ = f32[64,10240]{1,0:T(8,128)} custom-call(s32[13]{0:T(128)S(1)} %stack.55.place_ref, f32[256,3072]{1,0:T(8,128)S(1)} %get-tuple-element.33.refs_0_, bf16[192,3072]{1,0:T(8,128)(2,1)S(1)} %collective-permute-done.refs_1_.refs_2_, ...), custom_call_target="tpu_custom_call", output_to_operand_aliasing={{}: (9, {})} | custom-call | bytes 2752512 | tf_op jit(solution)/shard_map/pallas_call | solution.py:120
  180.8 1.7 copy-done.1
  183.1 1.3 collective-permute-start.26
  184.4 2.5 %shard_map.181.refs_8_ = f32[64,10240]{1,0:T(8,128)} custom-call(s32[13]{0:T(128)S(1)} %stack.55.place_ref, f32[256,3072]{1,0:T(8,128)S(1)} %get-tuple-element.47.refs_0_, bf16[192,3072]{1,0:T(8,128)(2,1)S(1)} %collective-permute-done.14.refs_1_.refs_2_, ...), custom_call_target="tpu_custom_call", output_to_operand_aliasing={{}: (9, {})} | custom-call | bytes 2752512 | tf_op jit(solution)/shard_map/pallas_call | solution.py:120
  186.9 2.3 %shard_map.182.refs_8_ = f32[64,10240]{1,0:T(8,128)} custom-call(s32[13]{0:T(128)S(1)} %stack.55.place_ref, f32[256,1536]{1,0:T(8,128)S(1)} %get-tuple-element.48.refs_0_, bf16[192,1536]{1,0:T(8,128)(2,1)S(1)} %collective-permute-done.17.refs_1_.refs_2_, ...), custom_call_target="tpu_custom_call", output_to_operand_aliasing={{}: (9, {})} | custom-call | bytes 1376256 | tf_op jit(solution)/shard_map/pallas_call | solution.py:120
  189.2 3.7 %collective-permute-done.26.refs_3_ = bf16[64,512]{1,0:T(8,128)(2,1)S(1)} collective-permute-done((bf16[64,512]{1,0:T(8,128)(2,1)S(1)}, bf16[64,512]{1,0:T(8,128)(2,1)S(1)}, u32[]{:S(2)}, u32[]{:S(2)}) %collective-permute-start.26) | collective-permute-done | bytes 65568 | tf_op jit(solution)/shard_map/ppermute | solution.py:427
  192.9 1.3 shard_map.183
  (70 shorter events, 11.6 us)
Async XLA Ops:
  0.8 1.6 copy-start.2
  6.1 29.3 %collective-permute-start.2 = (bf16[192,512]{1,0:T(8,128)(2,1)S(1)}, bf16[192,512]{1,0:T(8,128)(2,1)S(1)}, u32[]{:S(2)}, u32[]{:S(2)}) collective-permute-start(bf16[192,512]{1,0:T(8,128)(2,1)S(1)} %get-tuple-element.31.refs_2_), channel_id=1, source_target_pairs={{0,1},{3,2},{4,5},{7,6},{8,9},{11,10},{12,13},{15,14},{16,17},{19,... | collective-permute-start | bytes 589832 | tf_op jit(solution)/shard_map/ppermute | solution.py:427
  18.7 16.0 %copy-start.4 = (f32[1,32,10240]{2,1,0:T(8,128)S(1)}, f32[1,32,10240]{2,1,0:T(8,128)}, u32[]{:S(2)}) copy-start(f32[1,32,10240]{2,1,0:T(8,128)} %param.19) | copy-start | bytes 3932164
  18.7 16.0 %copy-start.5 = (f32[1,4096,32]{1,2,0:T(8,128)S(1)}, f32[1,4096,32]{1,2,0:T(8,128)}, u32[]{:S(2)}) copy-start(f32[1,4096,32]{1,2,0:T(8,128)} %param.18) | copy-start | bytes 1572868
  18.7 37.2 %collective-permute-start.5 = (bf16[192,1536]{1,0:T(8,128)(2,1)S(1)}, bf16[192,1536]{1,0:T(8,128)(2,1)S(1)}, u32[]{:S(2)}, u32[]{:S(2)}) collective-permute-start(bf16[192,1536]{1,0:T(8,128)(2,1)S(1)} %get-tuple-element.32.refs_2_), channel_id=1, source_target_pairs={{0,1},{3,2},{4,5},{7,6},{8,9},{11,10},{12,13},{15,14},{16,17},{19,... | collective-permute-start | bytes 1769480 | tf_op jit(solution)/shard_map/ppermute | solution.py:427
  33.2 2.8 %copy-start.3 = (bf16[256,4096]{1,0:T(8,128)(2,1)S(1)}, bf16[256,4096]{1,0:T(8,128)(2,1)}, u32[]{:S(2)}) copy-start(bf16[256,4096]{1,0:T(8,128)(2,1)} %refs_0_.13) | copy-start | bytes 6291460
  33.2 56.2 %collective-permute-start = (bf16[192,3072]{1,0:T(8,128)(2,1)S(1)}, bf16[192,3072]{1,0:T(8,128)(2,1)S(1)}, u32[]{:S(2)}, u32[]{:S(2)}) collective-permute-start(bf16[192,3072]{1,0:T(8,128)(2,1)S(1)} %get-tuple-element.34.refs_2_), channel_id=1, source_target_pairs={{0,1},{3,2},{4,5},{7,6},{8,9},{11,10},{12,13},{15,14},{16,17},{19,... | collective-permute-start | bytes 3538952 | tf_op jit(solution)/shard_map/ppermute | solution.py:427
  35.3 13.6 %collective-permute-start.1 = (bf16[16,14336]{1,0:T(8,128)(2,1)S(1)}, bf16[16,14336]{1,0:T(8,128)(2,1)S(1)}, u32[]{:S(2)}, u32[]{:S(2)}) collective-permute-start(bf16[16,14336]{1,0:T(8,128)(2,1)S(1)} %shard_map.156.refs_3_), channel_id=1, source_target_pairs={{0,4},{4,0},{8,12},{12,8},{1,5},{5,1},{9,13},{13,9},{2,6},{6,2},{1... | collective-permute-start | bytes 1376264 | tf_op jit(solution)/shard_map/ppermute | solution.py:430
  49.6 8.5 %copy-start.6 = (f32[8,10240]{1,0:T(8,128)S(1)}, f32[8,10240]{1,0:T(8,128)}, u32[]{:S(2)}) copy-start(f32[8,10240]{1,0:T(8,128)} %refs_5_.1) | copy-start | bytes 983044
  49.6 8.5 %copy-start.7 = (f32[8,10240]{1,0:T(8,128)S(1)}, f32[8,10240]{1,0:T(8,128)}, u32[]{:S(2)}) copy-start(f32[8,10240]{1,0:T(8,128)} %refs_6_.1) | copy-start | bytes 983044
  49.6 8.5 %copy-start.8 = (f32[8,10240]{1,0:T(8,128)S(1)}, f32[8,10240]{1,0:T(8,128)}, u32[]{:S(2)}) copy-start(f32[8,10240]{1,0:T(8,128)} %refs_7_.1) | copy-start | bytes 983044
  49.6 8.5 %copy-start.9 = (f32[4096,8]{0,1:T(8,128)S(1)}, f32[4096,8]{0,1:T(8,128)}, u32[]{:S(2)}) copy-start(f32[4096,8]{0,1:T(8,128)} %param.12) | copy-start | bytes 393220
  49.6 8.5 %copy-start.10 = (f32[4096,8]{0,1:T(8,128)S(1)}, f32[4096,8]{0,1:T(8,128)}, u32[]{:S(2)}) copy-start(f32[4096,8]{0,1:T(8,128)} %param.14) | copy-start | bytes 393220
  49.7 8.5 %copy-start.11 = (f32[4096,8]{0,1:T(8,128)S(1)}, f32[4096,8]{0,1:T(8,128)}, u32[]{:S(2)}) copy-start(f32[4096,8]{0,1:T(8,128)} %param.15) | copy-start | bytes 393220
  49.7 8.5 %collective-permute-start.3 = (bf16[8,14336]{1,0:T(8,128)(2,1)S(1)}, bf16[8,14336]{1,0:T(8,128)(2,1)S(1)}, u32[]{:S(2)}, u32[]{:S(2)}) collective-permute-start(bf16[8,14336]{1,0:T(8,128)(2,1)S(1)} %get-tuple-element.38), channel_id=1, source_target_pairs={{0,8},{4,12},{8,0},{12,4},{1,9},{5,13},{9,1},{13,5},{2,10},{6,14},... | collective-permute-start | bytes 688136 | tf_op jit(solution)/shard_map/ppermute | solution.py:430
  51.2 6.3 %collective-permute-start.4 = (bf16[128,512]{1,0:T(8,128)(2,1)S(1)}, bf16[128,512]{1,0:T(8,128)(2,1)S(1)}, u32[]{:S(2)}, u32[]{:S(2)}) collective-permute-start(bf16[128,512]{1,0:T(8,128)(2,1)S(1)} %shard_map.157.refs_2_), channel_id=1, source_target_pairs={{1,2},{2,1},{5,6},{6,5},{9,10},{10,9},{13,14},{14,13},{17,18},{18,... | collective-permute-start | bytes 393224 | tf_op jit(solution)/shard_map/ppermute | solution.py:427
  51.9 64.9 %collective-permute-start.14 = (bf16[192,3072]{1,0:T(8,128)(2,1)S(1)}, bf16[192,3072]{1,0:T(8,128)(2,1)S(1)}, u32[]{:S(2)}, u32[]{:S(2)}) collective-permute-start(bf16[192,3072]{1,0:T(8,128)(2,1)S(1)} %get-tuple-element.36.refs_3_), channel_id=1, source_target_pairs={{0,1},{3,2},{4,5},{7,6},{8,9},{11,10},{12,13},{15,14},{16,17},{19,... | collective-permute-start | bytes 3538952 | tf_op jit(solution)/shard_map/ppermute | solution.py:427
  56.8 46.0 %collective-permute-start.7 = (bf16[128,1536]{1,0:T(8,128)(2,1)S(1)}, bf16[128,1536]{1,0:T(8,128)(2,1)S(1)}, u32[]{:S(2)}, u32[]{:S(2)}) collective-permute-start(bf16[128,1536]{1,0:T(8,128)(2,1)S(1)} %shard_map.160.refs_2_), channel_id=1, source_target_pairs={{1,2},{2,1},{5,6},{6,5},{9,10},{10,9},{13,14},{14,13},{17,18},{18,... | collective-permute-start | bytes 1179656 | tf_op jit(solution)/shard_map/ppermute | solution.py:427
  60.1 1.3 collective-permute-start.9
  60.1 5.5 %collective-permute-start.18 = (bf16[8,10240]{1,0:T(8,128)(2,1)S(1)}, bf16[8,10240]{1,0:T(8,128)(2,1)S(1)}, u32[]{:S(2)}, u32[]{:S(2)}) collective-permute-start(bf16[8,10240]{1,0:T(8,128)(2,1)S(1)} %get-tuple-element.40.refs_3_), channel_id=1, source_target_pairs={{0,0},{1,4},{2,8},{3,12},{4,1},{5,5},{6,9},{7,13},{8,2},{9,6},{10,... | collective-permute-start | bytes 491528 | tf_op jit(solution)/shard_map/ppermute | solution.py:465
  61.3 42.3 %collective-permute-start.10 = (bf16[16,4096]{1,0:T(8,128)(2,1)S(1)}, bf16[16,4096]{1,0:T(8,128)(2,1)S(1)}, u32[]{:S(2)}, u32[]{:S(2)}) collective-permute-start(bf16[16,4096]{1,0:T(8,128)(2,1)S(1)} %constant_dynamic-update-slice_fusion.refs_1_), channel_id=1, source_target_pairs={{0,8},{4,12},{8,0},{12,4},{1,9},{5,13},{9,1},{13,5},{2,10},{6,14},... | collective-permute-start | bytes 393224 | tf_op jit(solution)/shard_map/ppermute | solution.py:430
  65.5 53.0 %collective-permute-start.19 = (bf16[8,10240]{1,0:T(8,128)(2,1)S(1)}, bf16[8,10240]{1,0:T(8,128)(2,1)S(1)}, u32[]{:S(2)}, u32[]{:S(2)}) collective-permute-start(bf16[8,10240]{1,0:T(8,128)(2,1)S(1)} %collective-permute-done.18), channel_id=1, source_target_pairs={{0,1},{1,0},{2,3},{3,2},{4,5},{5,4},{6,7},{7,6},{8,9},{9,8},{10,11... | collective-permute-start | bytes 491528 | tf_op jit(solution)/shard_map/ppermute | solution.py:473
  90.4 24.0 %collective-permute-start.12 = (bf16[128,3072]{1,0:T(8,128)(2,1)S(1)}, bf16[128,3072]{1,0:T(8,128)(2,1)S(1)}, u32[]{:S(2)}, u32[]{:S(2)}) collective-permute-start(bf16[128,3072]{1,0:T(8,128)(2,1)S(1)} %shard_map.163.refs_2_), channel_id=1, source_target_pairs={{1,2},{2,1},{5,6},{6,5},{9,10},{10,9},{13,14},{14,13},{17,18},{18,... | collective-permute-start | bytes 2359304 | tf_op jit(solution)/shard_map/ppermute | solution.py:427
  105.5 10.8 %collective-permute-start.11 = (f32[192,32]{1,0:T(8,128)S(1)}, f32[192,32]{1,0:T(8,128)S(1)}, u32[]{:S(2)}, u32[]{:S(2)}) collective-permute-start(f32[192,32]{1,0:T(8,128)S(1)} %get-tuple-element.46.refs_2_), channel_id=1, source_target_pairs={{0,1},{3,2},{4,5},{7,6},{8,9},{11,10},{12,13},{15,14},{16,17},{19,... | collective-permute-start | bytes 73736 | tf_op jit(solution)/shard_map/ppermute | solution.py:427
  113.0 11.9 %collective-permute-start.17 = (bf16[192,1536]{1,0:T(8,128)(2,1)S(1)}, bf16[192,1536]{1,0:T(8,128)(2,1)S(1)}, u32[]{:S(2)}, u32[]{:S(2)}) collective-permute-start(bf16[192,1536]{1,0:T(8,128)(2,1)S(1)} %get-tuple-element.41.refs_2_), channel_id=1, source_target_pairs={{0,1},{3,2},{4,5},{7,6},{8,9},{11,10},{12,13},{15,14},{16,17},{19,... | collective-permute-start | bytes 1769480 | tf_op jit(solution)/shard_map/ppermute | solution.py:427
  117.8 44.2 %collective-permute-start.16 = (bf16[128,3072]{1,0:T(8,128)(2,1)S(1)}, bf16[128,3072]{1,0:T(8,128)(2,1)S(1)}, u32[]{:S(2)}, u32[]{:S(2)}) collective-permute-start(bf16[128,3072]{1,0:T(8,128)(2,1)S(1)} %shard_map.170.refs_2_), channel_id=1, source_target_pairs={{1,2},{2,1},{5,6},{6,5},{9,10},{10,9},{13,14},{14,13},{17,18},{18,... | collective-permute-start | bytes 2359304 | tf_op jit(solution)/shard_map/ppermute | solution.py:427
  118.6 0.7 collective-permute-start.20
  119.3 41.4 %collective-permute-start.21 = (bf16[16,10240]{1,0:T(8,128)(2,1)S(1)}, bf16[16,10240]{1,0:T(8,128)(2,1)S(1)}, u32[]{:S(2)}, u32[]{:S(2)}) collective-permute-start(bf16[16,10240]{1,0:T(8,128)(2,1)S(1)} %collective-permute-done.20.refs_6_), channel_id=1, source_target_pairs={{2,3},{1,0},{6,7},{5,4},{10,11},{9,8},{14,15},{13,12},{18,19},{17,... | collective-permute-start | bytes 983048 | tf_op jit(solution)/shard_map/ppermute | solution.py:427
  120.6 0.7 collective-permute-start.13
  125.8 49.7 %collective-permute-start.25 = (bf16[128,1536]{1,0:T(8,128)(2,1)S(1)}, bf16[128,1536]{1,0:T(8,128)(2,1)S(1)}, u32[]{:S(2)}, u32[]{:S(2)}) collective-permute-start(bf16[128,1536]{1,0:T(8,128)(2,1)S(1)} %shard_map.172.refs_2_), channel_id=1, source_target_pairs={{1,2},{2,1},{5,6},{6,5},{9,10},{10,9},{13,14},{14,13},{17,18},{18,... | collective-permute-start | bytes 1179656 | tf_op jit(solution)/shard_map/ppermute | solution.py:427
  126.5 32.9 %collective-permute-start.22 = (bf16[64,512]{1,0:T(8,128)(2,1)S(1)}, bf16[64,512]{1,0:T(8,128)(2,1)S(1)}, u32[]{:S(2)}, u32[]{:S(2)}) collective-permute-start(bf16[64,512]{1,0:T(8,128)(2,1)S(1)} %shard_map.161.refs_8_), channel_id=1, source_target_pairs={{2,3},{1,0},{6,7},{5,4},{10,11},{9,8},{14,15},{13,12},{18,19},{17,... | collective-permute-start | bytes 196616 | tf_op jit(solution)/shard_map/ppermute | solution.py:427
  127.8 50.5 %collective-permute-start.24 = (bf16[64,3072]{1,0:T(8,128)(2,1)S(1)}, bf16[64,3072]{1,0:T(8,128)(2,1)S(1)}, u32[]{:S(2)}, u32[]{:S(2)}) collective-permute-start(bf16[64,3072]{1,0:T(8,128)(2,1)S(1)} %shard_map.168.refs_3_), channel_id=1, source_target_pairs={{2,3},{1,0},{6,7},{5,4},{10,11},{9,8},{14,15},{13,12},{18,19},{17,... | collective-permute-start | bytes 1179656 | tf_op jit(solution)/shard_map/ppermute | solution.py:427
  159.4 8.0 %collective-permute-start.15 = (f32[64,32]{1,0:T(8,128)S(1)}, f32[64,32]{1,0:T(8,128)S(1)}, u32[]{:S(2)}, u32[]{:S(2)}) collective-permute-start(f32[64,32]{1,0:T(8,128)S(1)} %shard_map.171.refs_3_), channel_id=1, source_target_pairs={{2,3},{1,0},{6,7},{5,4},{10,11},{9,8},{14,15},{13,12},{18,19},{17,... | collective-permute-start | bytes 24584 | tf_op jit(solution)/shard_map/ppermute | solution.py:427
  160.7 10.1 %collective-permute-start.8 = (bf16[64,1536]{1,0:T(8,128)(2,1)S(1)}, bf16[64,1536]{1,0:T(8,128)(2,1)S(1)}, u32[]{:S(2)}, u32[]{:S(2)}) collective-permute-start(bf16[64,1536]{1,0:T(8,128)(2,1)S(1)} %shard_map.166.refs_3_), channel_id=1, source_target_pairs={{2,3},{1,0},{6,7},{5,4},{10,11},{9,8},{14,15},{13,12},{18,19},{17,... | collective-permute-start | bytes 589832 | tf_op jit(solution)/shard_map/ppermute | solution.py:427
  162.0 11.2 %collective-permute-start.6 = (bf16[192,512]{1,0:T(8,128)(2,1)S(1)}, bf16[192,512]{1,0:T(8,128)(2,1)S(1)}, u32[]{:S(2)}, u32[]{:S(2)}) collective-permute-start(bf16[192,512]{1,0:T(8,128)(2,1)S(1)} %get-tuple-element.43.refs_2_), channel_id=1, source_target_pairs={{0,1},{3,2},{4,5},{7,6},{8,9},{11,10},{12,13},{15,14},{16,17},{19,... | collective-permute-start | bytes 589832 | tf_op jit(solution)/shard_map/ppermute | solution.py:427
  167.4 16.9 %collective-permute-start.28 = (bf16[64,3072]{1,0:T(8,128)(2,1)S(1)}, bf16[64,3072]{1,0:T(8,128)(2,1)S(1)}, u32[]{:S(2)}, u32[]{:S(2)}) collective-permute-start(bf16[64,3072]{1,0:T(8,128)(2,1)S(1)} %shard_map.173.refs_4_), channel_id=1, source_target_pairs={{2,3},{1,0},{6,7},{5,4},{10,11},{9,8},{14,15},{13,12},{18,19},{17,... | collective-permute-start | bytes 1179656 | tf_op jit(solution)/shard_map/ppermute | solution.py:427
  173.2 1.7 copy-start
  176.3 10.6 %collective-permute-start.27 = (bf16[64,1536]{1,0:T(8,128)(2,1)S(1)}, bf16[64,1536]{1,0:T(8,128)(2,1)S(1)}, u32[]{:S(2)}, u32[]{:S(2)}) collective-permute-start(bf16[64,1536]{1,0:T(8,128)(2,1)S(1)} %shard_map.178.refs_9_), channel_id=1, source_target_pairs={{2,3},{1,0},{6,7},{5,4},{10,11},{9,8},{14,15},{13,12},{18,19},{17,... | collective-permute-start | bytes 589832 | tf_op jit(solution)/shard_map/ppermute | solution.py:427
  177.6 3.2 %collective-permute-start.23 = (bf16[128,512]{1,0:T(8,128)(2,1)S(1)}, bf16[128,512]{1,0:T(8,128)(2,1)S(1)}, u32[]{:S(2)}, u32[]{:S(2)}) collective-permute-start(bf16[128,512]{1,0:T(8,128)(2,1)S(1)} %shard_map.177.refs_2_), channel_id=1, source_target_pairs={{1,2},{2,1},{5,6},{6,5},{9,10},{10,9},{13,14},{14,13},{17,18},{18,... | collective-permute-start | bytes 393224 | tf_op jit(solution)/shard_map/ppermute | solution.py:427
  180.8 1.7 copy-start.1
  183.1 9.9 %collective-permute-start.26 = (bf16[64,512]{1,0:T(8,128)(2,1)S(1)}, bf16[64,512]{1,0:T(8,128)(2,1)S(1)}, u32[]{:S(2)}, u32[]{:S(2)}) collective-permute-start(bf16[64,512]{1,0:T(8,128)(2,1)S(1)} %shard_map.180.refs_9_), channel_id=1, source_target_pairs={{2,3},{1,0},{6,7},{5,4},{10,11},{9,8},{14,15},{13,12},{18,19},{17,... | collective-permute-start | bytes 196616 | tf_op jit(solution)/shard_map/ppermute | solution.py:427

commit v3 on v2

--- a/solution.py
+++ b/solution.py
@@ -14,8 +14,9 @@
 adam_eps = 1e-08
 factor_scale = 2.0
 
-CHUNKS = (1, 3, 6, 6, 3, 1)
+CHUNKS = ((16, 2), (12, 3), (0, 4), (4, 4), (8, 4), (18, 2), (15, 1))
 VMEM_BYTES = 40 * 1024 * 1024
+WEIGHT = 5
 
 
 def apply_adam_rule(weights, moment, second, grads):
@@ -92,6 +93,7 @@
 LINE = (((0, 1), (3, 2)), ((1, 2), (2, 1)), ((2, 3), (1, 0)))
 (SEND_ROW, SECOND_AT, THIRD_AT, THIRD_FROM, OWN, FIRST_OWN, SECOND_OWN, ORDER, CORE_BIT, CHIP_BIT) = (
     0, 1, 2, 3, 4, 5, 6, 7, 11, 12)
+MOST = 2048
 
 
 def place_numbers(share):
@@ -111,7 +113,7 @@
     return jnp.stack([jnp.asarray(n, jnp.int32) for n in numbers])
 
 
-def call(body, place, operands, specs, earlier, out_shapes, out_specs, grid=(1,), flops=0, moved=0, aliases=None):
+def call(body, place, operands, specs, earlier, out_shapes, out_specs, grid=(1,), flops=0, moved=0, scratch=()):
     count = len(operands)
 
     def kernel(place_ref, *refs):
@@ -124,11 +126,11 @@
             grid=grid,
             in_specs=list(specs) + [pl.BlockSpec(memory_space=pl.ANY)] * len(earlier),
             out_specs=out_specs,
+            scratch_shapes=scratch,
         ),
         out_shape=out_shapes,
-        input_output_aliases={} if aliases is None else aliases,
         compiler_params=pltpu.CompilerParams(vmem_limit_bytes=VMEM_BYTES),
-        cost_estimate=pl.CostEstimate(flops=flops, bytes_accessed=moved, transcendentals=0),
+        cost_estimate=pl.CostEstimate(flops=WEIGHT * flops, bytes_accessed=WEIGHT * moved, transcendentals=0),
     )(place, *operands, *earlier)
 
 
@@ -137,7 +139,7 @@
 
 
 def block_width(start, width, most):
-    block = most
+    block = min(most, width)
     while start % block or width % block:
         block //= 2
     return block
@@ -169,7 +171,7 @@
 
 def add_second(place, partial, arrived, share, earlier):
     width = partial.shape[1]
-    block = block_width(0, width, 1024) if width % 128 == 0 else width
+    block = block_width(0, width, MOST)
 
     def body(place_ref, partial_ref, upper_ref, lower_ref, out_ref):
         out_ref[:share, :] = (partial_ref[:share, :] + upper_ref[...].astype(jnp.float32)).astype(out_ref.dtype)
@@ -194,7 +196,7 @@
 
 def add_third(place, partial, arrived, share, earlier):
     width = partial.shape[1]
-    block = block_width(0, width, 1024) if width % 128 == 0 else width
+    block = block_width(0, width, MOST)
 
     def body(place_ref, partial_ref, arrived_ref, out_ref):
         out_ref[...] = (partial_ref[...] + arrived_ref[...].astype(jnp.float32)).astype(out_ref.dtype)
@@ -231,36 +233,71 @@
     return total
 
 
-def finish_chunk(place, terms, spread, factors, decoded, start, width, share, full_width, earlier):
-    block = block_width(start, width, 1024)
-    first = start // block
-    operands = [*terms, spread, *factors]
-
-    def body(place_ref, own_ref, one_ref, two_ref, three_ref, spread_ref, pair_ref, near_ref, far_ref, *rest):
-        other = near_ref[...] + far_ref[...]
-        ranks = jnp.concatenate([pair_ref[...], other, pair_ref[...], other], axis=0)
-        change = jnp.dot(spread_ref[...], ranks, preferred_element_type=jnp.float32)
-        rest[-1][...] = own_total((own_ref, one_ref, two_ref, three_ref)) + change
-
+def finish_specs(share, block, first, spread, factors):
     half = factors[0].shape[0]
-    specs = own_block_specs(share, block) + [whole(spread.shape)]
-    specs += [pl.BlockSpec((half, block), lambda j, p: (0, first + j))] * 3
-    aliases = None
-    if decoded is not None:
-        aliases = {1 + len(operands): 0}
-        operands.append(decoded)
-        specs.append(pl.BlockSpec(memory_space=pl.ANY))
-    return call(
-        body,
-        place,
-        operands,
-        specs,
-        earlier,
-        jax.ShapeDtypeStruct((share, full_width), jnp.float32),
-        pl.BlockSpec((share, block), lambda j, p: (0, first + j)),
+    return own_block_specs(share, block) + [whole(spread.shape)] + [
+        pl.BlockSpec((half, block), lambda j, p: (0, first + j))
+    ] * 3
+
+
+def finish_value(refs):
+    spread_ref, pair_ref, near_ref, far_ref = refs[4:8]
+    other = near_ref[...] + far_ref[...]
+    ranks = jnp.concatenate([pair_ref[...], other, pair_ref[...], other], axis=0)
+    return own_total(refs[:4]) + jnp.dot(spread_ref[...], ranks, preferred_element_type=jnp.float32)
+
+
+def finish_chunk(place, terms, spread, factors, start, width, share, earlier):
+    block = block_width(start, width, MOST)
+
+    def body(place_ref, *refs):
+        refs[-1][...] = finish_value(refs)
+
+    return call(
+        body,
+        place,
+        [*terms, spread, *factors],
+        finish_specs(share, block, start // block, spread, factors),
+        earlier,
+        jax.ShapeDtypeStruct((share, width), jnp.float32),
+        pl.BlockSpec((share, block), lambda j, p: (0, j)),
         grid=(width // block,),
         moved=14 * share * width,
-        aliases=aliases,
+    )
+
+
+def finish_all(place, terms, spread, factors, start, width, share, full_width, done):
+    chunks = [chunk for _, chunk in done]
+
+    def body(place_ref, *refs):
+        others = refs[8:8 + len(chunks)]
+        out_ref, held, semaphores = refs[8 + len(chunks):]
+        copies = []
+        for i, ((at, chunk), ref) in enumerate(zip(done, others)):
+            copies.append(
+                pltpu.make_async_copy(ref, out_ref.at[:, at:at + chunk.shape[1]], semaphores.at[i])
+            )
+        for copy in copies:
+            copy.start()
+        held[...] = finish_value(refs)
+        last = pltpu.make_async_copy(held, out_ref.at[:, start:start + width], semaphores.at[len(chunks)])
+        last.start()
+        for copy in copies + [last]:
+            copy.wait()
+
+    return call(
+        body,
+        place,
+        [*terms, spread, *factors, *chunks],
+        finish_specs(share, width, start // width, spread, factors) + [pl.BlockSpec(memory_space=pl.ANY)] * len(chunks),
+        [],
+        jax.ShapeDtypeStruct((share, full_width), jnp.float32),
+        pl.BlockSpec(memory_space=pl.ANY),
+        moved=8 * share * full_width,
+        scratch=[
+            pltpu.VMEM((share, width), jnp.float32),
+            pltpu.SemaphoreType.DMA((len(chunks) + 1,)),
+        ],
     )
 
 
@@ -343,17 +380,35 @@
     )
 
 
-def inner_products(place, x, near, far, share, earlier):
-    rows, ranks = x.shape[0], 2 * near.shape[0]
-    sent = rows - share
-
-    def body(place_ref, x_ref, near_ref, far_ref, inner_ref, send_ref):
-        half = ranks // 2
+def join_ranks(place, upper, lower, earlier):
+    ranks, width = upper.shape
+    block = block_width(0, width, MOST)
+
+    def body(place_ref, upper_ref, lower_ref, out_ref):
+        both = [ref[...].astype(jnp.float32) for ref in (upper_ref, lower_ref)]
+        out_ref[...] = jnp.concatenate(both, axis=0).astype(jnp.bfloat16)
+
+    return call(
+        body,
+        place,
+        [upper, lower],
+        [pl.BlockSpec((ranks, block), lambda j, p: (0, j))] * 2,
+        earlier,
+        jax.ShapeDtypeStruct((2 * ranks, width), jnp.bfloat16),
+        pl.BlockSpec((2 * ranks, block), lambda j, p: (0, j)),
+        grid=(width // block,),
+        moved=8 * ranks * width,
+    )
+
+
+def inner_products(place, x, near, far, earlier):
+    rows, half = x.shape[0], near.shape[0]
+
+    def body(place_ref, x_ref, near_ref, far_ref, inner_ref):
         for at, ref in ((0, near_ref), (half, far_ref)):
-            inner_ref[:, at:at + half] = lax.dot_general(
-                x_ref[...], ref[...], (((1,), (1,)), ((), ())), preferred_element_type=jnp.float32
+            inner_ref[at:at + half, :] = lax.dot_general(
+                ref[...], x_ref[...], (((1,), (1,)), ((), ())), preferred_element_type=jnp.float32
             )
-        send_ref[...] = inner_ref[pl.ds(pl.multiple_of(place_ref[SEND_ROW], share), sent), :]
 
     return call(
         body,
@@ -361,19 +416,37 @@
         [x, near, far],
         [whole(x.shape), whole(near.shape), whole(far.shape)],
         earlier,
-        [jax.ShapeDtypeStruct((rows, ranks), jnp.float32), jax.ShapeDtypeStruct((sent, ranks), jnp.float32)],
-        [whole((rows, ranks)), whole((sent, ranks))],
-        flops=2 * rows * ranks * x.shape[1],
+        jax.ShapeDtypeStruct((2 * half, rows), jnp.float32),
+        whole((2 * half, rows)),
+        flops=4 * rows * half * x.shape[1],
         moved=2 * rows * x.shape[1],
     )
 
 
-def spread_inner(place, terms, share, earlier):
-    ranks = terms[0].shape[1]
+def inner_sum(place, inner, arrived, earlier):
+    def body(place_ref, inner_ref, arrived_ref, out_ref):
+        out_ref[...] = inner_ref[...] + arrived_ref[...]
+
+    return call(
+        body,
+        place,
+        [inner, arrived],
+        [whole(inner.shape)] * 2,
+        earlier,
+        jax.ShapeDtypeStruct(inner.shape, jnp.float32),
+        whole(inner.shape),
+    )
+
+
+def spread_inner(place, inner, arrived, share, earlier):
+    ranks, rows = inner.shape
     portion = ranks // 4
 
-    def body(place_ref, own_ref, one_ref, two_ref, three_ref, out_ref):
-        inner = factor_scale * own_total((own_ref, one_ref, two_ref, three_ref))
+    def body(place_ref, inner_ref, arrived_ref, out_ref):
+        total = factor_scale * (inner_ref[...] + arrived_ref[...])
+        shape = (share, rows)
+        mine = lax.broadcasted_iota(jnp.int32, shape, 0) + place_ref[OWN] * share
+        mine = jnp.where(lax.broadcasted_iota(jnp.int32, shape, 1) == mine, 1.0, 0.0).astype(jnp.bfloat16)
         block = lax.broadcasted_iota(jnp.int32, (ranks, ranks), 1) // portion
         source = jnp.full((ranks, ranks), 0, jnp.int32)
         for i in range(4):
@@ -381,16 +454,17 @@
         column = lax.broadcasted_iota(jnp.int32, (ranks, ranks), 1) % portion
         chosen = lax.broadcasted_iota(jnp.int32, (ranks, ranks), 0) == source * portion + column
         chosen = jnp.where(chosen, 1.0, 0.0).astype(jnp.bfloat16)
-        halves = [
-            jnp.dot(half, chosen, preferred_element_type=jnp.float32) for half in split_high_low(inner)
-        ]
+        halves = []
+        for half in split_high_low(total):
+            turned = lax.dot_general(mine, half, (((1,), (1,)), ((), ())), preferred_element_type=jnp.float32)
+            halves.append(jnp.dot(turned.astype(jnp.bfloat16), chosen, preferred_element_type=jnp.float32))
         out_ref[...] = jnp.concatenate(halves, axis=1).astype(jnp.bfloat16)
 
     return call(
         body,
         place,
-        list(terms),
-        own_block_specs(share, ranks),
+        [inner, arrived],
+        [whole(inner.shape)] * 2,
         earlier,
         jax.ShapeDtypeStruct((share, 2 * ranks), jnp.bfloat16),
         whole((share, 2 * ranks)),
@@ -417,10 +491,9 @@
     part_in = replica_input_gradient[0].T.reshape(2, 2, ranks, -1)
     part_out = replica_output_gradient[0].reshape(2, 2, ranks, -1)
 
-    unit = width // sum(CHUNKS)
-    widths = [unit * c for c in CHUNKS]
-    starts = [sum(widths[:i]) for i in range(len(widths))]
-    count = len(widths)
+    unit = width // 20
+    starts = [unit * at for at, _ in CHUNKS]
+    widths = [unit * wide for _, wide in CHUNKS]
     partials, seconds, thirds, arrived = {}, {}, {}, {}
 
     def line(step, values):
@@ -430,8 +503,7 @@
         return lax.ppermute(values, "rep", [(i, i ^ bit) for i in range(4)])
 
     def matmul(c, *earlier):
-        most = 256 if c == 0 else 512
-        partials[c], send = matmul_chunk(place, x, base, starts[c], widths[c], share, earlier, most)
+        partials[c], send = matmul_chunk(place, x, base, starts[c], widths[c], share, earlier, 512)
         arrived[c, 0] = line(0, send)
         return send
 
@@ -445,59 +517,67 @@
         arrived[c, 2] = line(2, thirds[c])
         return thirds[c]
 
+    def terms(c):
+        return (partials[c], arrived[c, 0], arrived[c, 1], arrived[c, 2])
+
+    def finish(c, *earlier):
+        finished.append((starts[c], finish_chunk(
+            place, terms(c), spread, (pair, near_out, far_out), starts[c], widths[c], share, earlier
+        )))
+        return finished[-1][1]
+
+    finished = []
     last = matmul(0)
-    last = matmul(1, last)
-    last = matmul(2, last)
     last = gradients_out(place, part_in, part_out, [last])
     from_core = chip(1, last)
+    last = matmul(1, last)
+    across, last = gradients_on(place, part_in, part_out, from_core, [last])
+    keep = last
+    from_chip = chip(2, across)
+    last = matmul(2, last)
     last = second(0, last)
-    last = matmul(3, last)
-    across, keep = gradients_on(place, part_in, part_out, from_core, [last])
-    from_chip = chip(2, across)
-    last = second(1, keep)
-    last = third(0, last)
     in_state = (input_factor.T, input_first_moment.T, input_second_moment.T)
     out_state = (output_factor, output_first_moment, output_second_moment)
     states = update_factors(place, keep, from_chip, in_state, out_state, [last])
     new_in, first_in, second_in, half_in, new_out, first_out, second_out, half_out = states
+    turned = lax.ppermute(half_out, ("rep", "tp"), [(4 * a + b, 4 * b + a) for a in range(4) for b in range(4)])
     near_in = jnp.concatenate([half_in, chip(1, half_in)], axis=0)
     far_in = chip(2, near_in)
-    turned = lax.ppermute(half_out, ("rep", "tp"), [(4 * a + b, 4 * b + a) for a in range(4) for b in range(4)])
-    last = second(2, half_out)
+    last = matmul(3, half_out)
+    last = second(1, last)
+    last = third(0, last, turned)
+    swapped = lax.ppermute(turned, "tp", [(i, i ^ 1) for i in range(4)])
+    last = second(2, last)
     last = matmul(4, last)
+    last = inner = inner_products(place, x, near_in, far_in, [last])
+    inner_arrived = lax.ppermute(inner, "tp", [(i, i ^ 1) for i in range(4)])
+    last = third(1, last)
+    last = second(3, last)
     last = matmul(5, last)
-    last = third(1, last)
-    inner, inner_send = inner_products(place, x, near_in, far_in, share, [last])
-    inner_arrived = [line(0, inner_send)]
-    last = third(2, inner_send)
-    pair = jnp.concatenate([turned, lax.ppermute(turned, "tp", [(i, i ^ 1) for i in range(4)])], axis=0)
+    last = pair = join_ranks(place, turned, swapped, [last])
     near_out = line(1, pair)
-    inner_second = add_second(place, inner, inner_arrived[0], share, [last])
-    inner_arrived.append(line(1, inner_second))
+    last = inner = inner_sum(place, inner, inner_arrived, [last])
+    inner_arrived = lax.ppermute(inner, "tp", [(i, i ^ 2) for i in range(4)])
+    last = third(2, last)
+    last = matmul(6, last)
+    last = second(4, last)
+    last = third(3, last)
+    last = spread = spread_inner(place, inner, inner_arrived, share, [last, near_out])
     far_out = line(2, near_out)
-    last = second(3, inner_second)
-    inner_third = add_third(place, inner, inner_arrived[1], share, [last])
-    inner_arrived.append(line(2, inner_third))
-    last = second(4, inner_third)
-    last = third(3, last)
-    spread = spread_inner(place, (inner, *inner_arrived), share, [last])
-
-    decoded = None
-
-    def finish(c, decoded, *earlier):
-        terms = (partials[c], arrived[c, 0], arrived[c, 1], arrived[c, 2])
-        return finish_chunk(
-            place, terms, spread, (pair, near_out, far_out), decoded, starts[c], widths[c], share, width, earlier
-        )
-
-    decoded = finish(0, None)
-    decoded = finish(1, decoded)
-    last = second(5, decoded)
+    last = second(5, last)
+    last = finish(0, last, far_out)
+    last = finish(1, last)
     last = third(4, last)
-    decoded = finish(2, decoded, last)
-    last = third(5, decoded)
-    for c in range(3, count):
-        decoded = finish(c, decoded, last)
+    last = second(6, last)
+    last = third(5, last)
+    last = finish(2, last)
+    last = finish(3, last)
+    last = third(6, last)
+    last = finish(4, last)
+    last = finish(5, last)
+    decoded = finish_all(
+        place, terms(6), spread, (pair, near_out, far_out), starts[6], widths[6], share, width, finished
+    )
     return (decoded, new_in.T, new_out, first_in.T, second_in.T, first_out, second_out)
 
 

time: 198 us -> 163 us (0.82); the launches traced: 194 us -> 163 us
  starting transfers between devices: 71.5 us -> 58.4 us
  waiting for transfers between devices: 38.8 us -> 28.7 us
  Pallas kernels: 77.4 us -> 72.3 us
  local copies, waits for them, and re-layouts: 5.25 us -> 1.74 us
    ppermute x23, waiting for transfers between devices: 38.2 us -> 13.5 us  [line(): return lax.ppermute(values, 'tp', LINE[step])]
    ppermute x1 -> x3, starting transfers between devices: 23.8 us -> 7.13 us  [the longest x1 6.56 us: local_line(): inner_arrived = lax.ppermute(inner, 'tp', [(i, i ^ 2) for i in range(4)])]
    ppermute x1 -> x3, waiting for transfers between devices: 0.01 us -> 15.2 us  [the longest x1 12.3 us: local_line(): inner_arrived = lax.ppermute(inner, 'tp', [(i, i ^ 2) for i in range(4)])]
    ppermute x23, starting transfers between devices: 41.2 us -> 46.7 us  [line(): return lax.ppermute(values, 'tp', LINE[step])]
    pallas_call x31 -> x35, Pallas kernels: 77.4 us -> 72.3 us  [call(): pl.pallas_call(kernel, grid_spec=pltpu.PrefetchScalarGridSpec(num_scalar_...]
    unnamed x26 -> x21, local copies, waits for them, and re-layouts: 5.14 us -> 1.65 us
    ppermute x4, starting transfers between devices: 5.85 us -> 3.86 us  [chip(): return lax.ppermute(values, 'rep', [(i, i ^ bit) for i in range(4)])]
  transfers between devices with their start and end apart: 29 -> 31, of which waited for: 5 -> 7; matrix products, arithmetic and copies ran while one was open for 0% -> 0% of each run, Pallas kernels for 37% -> 40%
where the time goes in v3:
time: 163 us
  Pallas kernels  72.3 us (44%)
  starting transfers between devices  58.4 us (36%)
  waiting for transfers between devices  28.7 us (18%)
  local copies, waits for them, and re-layouts  1.74 us (1%)
    pallas_call x35, Pallas kernels, call(): pl.pallas_call(kernel, grid_spec=pltpu.PrefetchScalarGridSpec(num_scalar_...  72.3 us
    ppermute x23, starting transfers between devices, line(): return lax.ppermute(values, 'tp', LINE[step])  46.7 us
    ppermute x23, waiting for transfers between devices, line(): return lax.ppermute(values, 'tp', LINE[step])  13.5 us
    ppermute x1, waiting for transfers between devices, local_line(): inner_arrived = lax.ppermute(inner, 'tp', [(i, i ^ 2) for i in range(4)])  12.3 us
    ppermute x1, starting transfers between devices, local_line(): inner_arrived = lax.ppermute(inner, 'tp', [(i, i ^ 2) for i in range(4)])  6.56 us
    ppermute x4, starting transfers between devices, chip(): return lax.ppermute(values, 'rep', [(i, i ^ bit) for i in range(4)])  3.86 us
  transfers between devices with their start and end apart: 31, of which 7 were waited for; matrix products, arithmetic and copies ran while one was open for 0% of the time, Pallas kernels for 40%

profile of v3, /device:TPU:0, one launch (start us, length us, event | category | flops | bytes accessed | tf_op | source)
XLA Modules:
  0.0 162.6 jit_solution(15162740813645987301)
XLA Ops:
  0.8 1.6 copy-done
  2.4 5.5 %shard_map.153 = (f32[256,1024]{1,0:T(8,128)S(1)}, bf16[192,1024]{1,0:T(8,128)(2,1)S(1)}) custom-call(s32[13]{0:T(128)S(1)} %stack.55.place_ref, bf16[256,4096]{1,0:T(8,128)(2,1)S(1)} %copy-done, bf16[4096,10240]{1,0:T(8,128)(2,1)} %refs_1_.13), custom_call_target="tpu_custom_call" | custom-call | flops 10737418240 | bytes 41943040 | tf_op jit(solution)/shard_map/pallas_call | solution.py:122
  7.9 5.1 %collective-permute-start.2 = (bf16[192,1024]{1,0:T(8,128)(2,1)S(1)}, bf16[192,1024]{1,0:T(8,128)(2,1)S(1)}, u32[]{:S(2)}, u32[]{:S(2)}) collective-permute-start(bf16[192,1024]{1,0:T(8,128)(2,1)S(1)} %get-tuple-element.31.refs_2_), channel_id=1, source_target_pairs={{0,1},{3,2},{4,5},{7,6},{8,9},{11,10},{12,13},{15,14},{16,17},{19,... | collective-permute-start | bytes 1179656 | tf_op jit(solution)/shard_map/ppermute | solution.py:500
  13.7 7.7 %shard_map.155 = (f32[256,1536]{1,0:T(8,128)S(1)}, bf16[192,1536]{1,0:T(8,128)(2,1)S(1)}) custom-call(s32[13]{0:T(128)S(1)} %stack.55.place_ref, bf16[256,4096]{1,0:T(8,128)(2,1)S(1)} %copy-done.1, bf16[4096,10240]{1,0:T(8,128)(2,1)} %refs_1_.13, bf16[16,14336]{1,0:T(8,128)(2,1)S(1)} %shard_map.154.refs_2_), custom_call_target="tpu_custom_call" | custom-call | flops 16106127360 | bytes 62914560 | tf_op jit(solution)/shard_map/pallas_call | solution.py:122
  21.3 1.3 collective-permute-start.4
  23.3 1.6 collective-permute-start.5
  24.9 9.2 %shard_map.157 = (f32[256,2048]{1,0:T(8,128)S(1)}, bf16[192,2048]{1,0:T(8,128)(2,1)S(1)}) custom-call(s32[13]{0:T(128)S(1)} %stack.55.place_ref, bf16[256,4096]{1,0:T(8,128)(2,1)S(1)} %copy-done.1, bf16[4096,10240]{1,0:T(8,128)(2,1)} %refs_1_.13, f32[8,14336]{1,0:T(8,128)S(1)} %get-tuple-element.33.refs_2_.refs_0_), custom_call_target="tpu_custom_call" | custom-call | flops 21474836480 | bytes 83886080 | tf_op jit(solution)/shard_map/pallas_call | solution.py:122
  34.2 1.5 collective-permute-start.1
  37.1 1.9 %shard_map.159 = (f32[8,4096]{1,0:T(8,128)}, f32[8,4096]{1,0:T(8,128)}, f32[8,4096]{1,0:T(8,128)}, bf16[8,4096]{1,0:T(8,128)(2,1)S(1)}, f32[8,10240]{1,0:T(8,128...) custom-call(s32[13]{0:T(128)S(1)} %stack.55.place_ref, ...), custom_call_target="tpu_custom_call" | custom-call | bytes 18350080 | tf_op jit(solution)/shard_map/pallas_call | solution.py:122
  39.1 9.2 %shard_map.160 = (f32[256,2048]{1,0:T(8,128)S(1)}, bf16[192,2048]{1,0:T(8,128)(2,1)S(1)}) custom-call(s32[13]{0:T(128)S(1)} %stack.55.place_ref, bf16[256,4096]{1,0:T(8,128)(2,1)S(1)} %copy-done.1, bf16[4096,10240]{1,0:T(8,128)(2,1)} %refs_1_.13, bf16[8,10240]{1,0:T(8,128)(2,1)S(1)} %get-tuple-element.39.refs_2_), custom_call_target="tpu_custom_call" | custom-call | flops 21474836480 | bytes 83886080 | tf_op jit(solution)/shard_map/pallas_call | solution.py:122
  49.0 5.1 %collective-permute-start.12 = (bf16[192,2048]{1,0:T(8,128)(2,1)S(1)}, bf16[192,2048]{1,0:T(8,128)(2,1)S(1)}, u32[]{:S(2)}, u32[]{:S(2)}) collective-permute-start(bf16[192,2048]{1,0:T(8,128)(2,1)S(1)} %get-tuple-element.40.refs_3_), channel_id=1, source_target_pairs={{0,1},{3,2},{4,5},{7,6},{8,9},{11,10},{12,13},{15,14},{16,17},{19,... | collective-permute-start | bytes 2359304 | tf_op jit(solution)/shard_map/ppermute | solution.py:500
  54.8 0.7 collective-permute-start.13
  55.5 2.0 %collective-permute-start.9 = (bf16[16,4096]{1,0:T(8,128)(2,1)S(1)}, bf16[16,4096]{1,0:T(8,128)(2,1)S(1)}, u32[]{:S(2)}, u32[]{:S(2)}) collective-permute-start(bf16[16,4096]{1,0:T(8,128)(2,1)S(1)} %constant_dynamic-update-slice_fusion.refs_1_), channel_id=1, source_target_pairs={{0,8},{4,12},{8,0},{12,4},{1,9},{5,13},{9,1},{13,5},{2,10},{6,14},... | collective-permute-start | bytes 393224 | tf_op jit(solution)/shard_map/ppermute | solution.py:503
  59.4 0.7 collective-permute-start.7
  60.1 9.2 %shard_map.164 = (f32[256,2048]{1,0:T(8,128)S(1)}, bf16[192,2048]{1,0:T(8,128)(2,1)S(1)}) custom-call(s32[13]{0:T(128)S(1)} %stack.55.place_ref, bf16[256,4096]{1,0:T(8,128)(2,1)S(1)} %copy-done.1, bf16[4096,10240]{1,0:T(8,128)(2,1)} %refs_1_.13, bf16[128,2048]{1,0:T(8,128)(2,1)S(1)} %shard_map.163.refs_2_), custom_call_target="tpu_custom_call" | custom-call | flops 21474836480 | bytes 83886080 | tf_op jit(solution)/shard_map/pallas_call | solution.py:122
  69.3 8.2 %collective-permute-start.15 = (bf16[192,2048]{1,0:T(8,128)(2,1)S(1)}, bf16[192,2048]{1,0:T(8,128)(2,1)S(1)}, u32[]{:S(2)}, u32[]{:S(2)}) collective-permute-start(bf16[192,2048]{1,0:T(8,128)(2,1)S(1)} %get-tuple-element.42.refs_3_), channel_id=1, source_target_pairs={{0,1},{3,2},{4,5},{7,6},{8,9},{11,10},{12,13},{15,14},{16,17},{19,... | collective-permute-start | bytes 2359304 | tf_op jit(solution)/shard_map/ppermute | solution.py:500
  77.5 1.7 %shard_map.165.refs_2_.refs_0_ = f32[32,256]{1,0:T(8,128)S(1)} custom-call(s32[13]{0:T(128)S(1)} %stack.55.place_ref, bf16[256,4096]{1,0:T(8,128)(2,1)S(1)} %copy-done.1, bf16[16,4096]{1,0:T(8,128)(2,1)S(1)} %constant_dynamic-update-slice_fusion.refs_1_, bf16[16,4096]{1,0:T(8,128)(2,1)S(1)} %collective-permute-done.9.refs_2_, ...), custom_call_target="tpu_custom_call" | custom-call | flops 335544320 | bytes 10485760 | tf_op jit(solution)/shard_map/pallas_call | solution.py:122
  80.5 0.7 collective-permute-start.19
  81.2 5.5 %shard_map.168 = (f32[256,1024]{1,0:T(8,128)S(1)}, bf16[192,1024]{1,0:T(8,128)(2,1)S(1)}) custom-call(s32[13]{0:T(128)S(1)} %stack.55.place_ref, bf16[256,4096]{1,0:T(8,128)(2,1)S(1)} %copy-done.1, bf16[4096,10240]{1,0:T(8,128)(2,1)} %refs_1_.13, bf16[128,2048]{1,0:T(8,128)(2,1)S(1)} %shard_map.167.refs_2_), custom_call_target="tpu_custom_call" | custom-call | flops 10737418240 | bytes 41943040 | tf_op jit(solution)/shard_map/pallas_call | solution.py:122
  86.7 5.2 %collective-permute-start.23 = (bf16[192,1024]{1,0:T(8,128)(2,1)S(1)}, bf16[192,1024]{1,0:T(8,128)(2,1)S(1)}, u32[]{:S(2)}, u32[]{:S(2)}) collective-permute-start(bf16[192,1024]{1,0:T(8,128)(2,1)S(1)} %get-tuple-element.44.refs_2_), channel_id=1, source_target_pairs={{0,1},{3,2},{4,5},{7,6},{8,9},{11,10},{12,13},{15,14},{16,17},{19,... | collective-permute-start | bytes 1179656 | tf_op jit(solution)/shard_map/ppermute | solution.py:500
  91.9 0.7 shard_map.169.refs_2_.refs_5_
  92.6 2.9 %collective-permute-done.10.refs_1_ = f32[32,256]{1,0:T(8,128)S(1)} collective-permute-done((f32[32,256]{1,0:T(8,128)S(1)}, f32[32,256]{1,0:T(8,128)S(1)}, u32[]{:S(2)}, u32[]{:S(2)}) %collective-permute-start.10) | collective-permute-done | bytes 32800 | tf_op jit(solution)/shard_map/ppermute | solution.py:553
  97.3 4.0 %shard_map.172 = (f32[256,512]{1,0:T(8,128)S(1)}, bf16[192,512]{1,0:T(8,128)(2,1)S(1)}) custom-call(s32[13]{0:T(128)S(1)} %stack.55.place_ref, bf16[256,4096]{1,0:T(8,128)(2,1)S(1)} %copy-done.1, bf16[4096,10240]{1,0:T(8,128)(2,1)} %refs_1_.13, bf16[64,2048]{1,0:T(8,128)(2,1)S(1)} %shard_map.171.refs_2_), custom_call_target="tpu_custom_call" | custom-call | flops 5368709120 | bytes 20971520 | tf_op jit(solution)/shard_map/pallas_call | solution.py:122
  102.0 0.7 collective-permute-start.16
  102.7 1.3 collective-permute-start.21
  104.0 6.6 %collective-permute-start.18 = (f32[32,256]{1,0:T(8,128)S(1)}, f32[32,256]{1,0:T(8,128)S(1)}, u32[]{:S(2)}, u32[]{:S(2)}) collective-permute-start(f32[32,256]{1,0:T(8,128)S(1)} %shard_map.170.refs_2_.refs_0_), channel_id=1, source_target_pairs={{0,2},{1,3},{2,0},{3,1},{4,6},{5,7},{6,4},{7,5},{8,10},{9,11},{10,... | collective-permute-start | bytes 98312 | tf_op jit(solution)/shard_map/ppermute | solution.py:560
  110.6 12.3 %collective-permute-done.18.refs_1_ = f32[32,256]{1,0:T(8,128)S(1)} collective-permute-done((f32[32,256]{1,0:T(8,128)S(1)}, f32[32,256]{1,0:T(8,128)S(1)}, u32[]{:S(2)}, u32[]{:S(2)}) %collective-permute-start.18) | collective-permute-done | bytes 32800 | tf_op jit(solution)/shard_map/ppermute | solution.py:560
  122.9 1.3 collective-permute-start.17
  124.2 1.3 collective-permute-start.22
  126.1 1.0 shard_map.175.refs_3_.refs_4_
  127.1 4.6 %collective-permute-start.14 = (bf16[192,512]{1,0:T(8,128)(2,1)S(1)}, bf16[192,512]{1,0:T(8,128)(2,1)S(1)}, u32[]{:S(2)}, u32[]{:S(2)}) collective-permute-start(bf16[192,512]{1,0:T(8,128)(2,1)S(1)} %get-tuple-element.46.refs_3_), channel_id=1, source_target_pairs={{0,1},{3,2},{4,5},{7,6},{8,9},{11,10},{12,13},{15,14},{16,17},{19,... | collective-permute-start | bytes 589832 | tf_op jit(solution)/shard_map/ppermute | solution.py:500
  132.3 2.3 %collective-permute-done.22.refs_3_ = bf16[64,1024]{1,0:T(8,128)(2,1)S(1)} collective-permute-done((bf16[64,1024]{1,0:T(8,128)(2,1)S(1)}, bf16[64,1024]{1,0:T(8,128)(2,1)S(1)}, u32[]{:S(2)}, u32[]{:S(2)}) %collective-permute-start.22) | collective-permute-done | bytes 131104 | tf_op jit(solution)/shard_map/ppermute | solution.py:500
  135.3 1.3 collective-permute-start.26
  136.6 1.3 collective-permute-start.25
  137.9 0.7 shard_map.177.refs_8_
  138.6 0.8 shard_map.178.refs_2_.refs_9_
  140.1 1.3 collective-permute-start.29
  143.2 1.3 collective-permute-start.30
  144.5 2.3 %collective-permute-done.26.refs_3_ = bf16[64,2048]{1,0:T(8,128)(2,1)S(1)} collective-permute-done((bf16[64,2048]{1,0:T(8,128)(2,1)S(1)}, bf16[64,2048]{1,0:T(8,128)(2,1)S(1)}, u32[]{:S(2)}, u32[]{:S(2)}) %collective-permute-start.26) | collective-permute-done | bytes 262176 | tf_op jit(solution)/shard_map/ppermute | solution.py:500
  146.8 0.7 shard_map.182.refs_8_.refs_10_
  147.6 4.9 %collective-permute-done.25.refs_3_ = bf16[64,2048]{1,0:T(8,128)(2,1)S(1)} collective-permute-done((bf16[64,2048]{1,0:T(8,128)(2,1)S(1)}, bf16[64,2048]{1,0:T(8,128)(2,1)S(1)}, u32[]{:S(2)}, u32[]{:S(2)}) %collective-permute-start.25) | collective-permute-done | bytes 262176 | tf_op jit(solution)/shard_map/ppermute | solution.py:500
  152.5 0.7 shard_map.183.refs_2_.refs_11_
  153.8 1.3 collective-permute-start.28
  155.1 3.0 %collective-permute-done.29.refs_3_ = bf16[64,2048]{1,0:T(8,128)(2,1)S(1)} collective-permute-done((bf16[64,2048]{1,0:T(8,128)(2,1)S(1)}, bf16[64,2048]{1,0:T(8,128)(2,1)S(1)}, u32[]{:S(2)}, u32[]{:S(2)}) %collective-permute-start.29) | collective-permute-done | bytes 262176 | tf_op jit(solution)/shard_map/ppermute | solution.py:500
  158.1 0.7 shard_map.185.refs_8_.refs_12_
  158.8 1.0 collective-permute-done.30.refs_3_
  159.8 0.7 shard_map.186.refs_13_
  160.5 2.1 %shard_map.187 = f32[64,10240]{1,0:T(8,128)} custom-call(s32[13]{0:T(128)S(1)} %stack.55.place_ref, f32[256,512]{1,0:T(8,128)S(1)} %get-tuple-element.45.refs_0_, bf16[192,512]{1,0:T(8,128)(2,1)S(1)} %collective-permute-done.14.refs_1_.refs_2_, bf16[128,512]{1,0:T(8,128)(2,1)S(1)} %collective-permute-done.24.refs_1_.refs_2_, ...), custom_call_target="tpu_custom_call" | custom-call | bytes 26214400 | tf_op jit(solution)/shard_map/pallas_call | solution.py:122
  (72 shorter events, 14.6 us)
Async XLA Ops:
  0.8 1.6 copy-start
  2.4 10.6 %copy-start.2 = (f32[1,32,10240]{2,1,0:T(8,128)S(1)}, f32[1,32,10240]{2,1,0:T(8,128)}, u32[]{:S(2)}) copy-start(f32[1,32,10240]{2,1,0:T(8,128)} %param.19) | copy-start | bytes 3932164
  2.4 10.6 %copy-start.3 = (f32[1,4096,32]{1,2,0:T(8,128)S(1)}, f32[1,4096,32]{1,2,0:T(8,128)}, u32[]{:S(2)}) copy-start(f32[1,4096,32]{1,2,0:T(8,128)} %param.18) | copy-start | bytes 1572868
  7.8 5.8 %copy-start.1 = (bf16[256,4096]{1,0:T(8,128)(2,1)S(1)}, bf16[256,4096]{1,0:T(8,128)(2,1)}, u32[]{:S(2)}) copy-start(bf16[256,4096]{1,0:T(8,128)(2,1)} %refs_0_.15) | copy-start | bytes 6291460
  7.9 27.8 %collective-permute-start.2 = (bf16[192,1024]{1,0:T(8,128)(2,1)S(1)}, bf16[192,1024]{1,0:T(8,128)(2,1)S(1)}, u32[]{:S(2)}, u32[]{:S(2)}) collective-permute-start(bf16[192,1024]{1,0:T(8,128)(2,1)S(1)} %get-tuple-element.31.refs_2_), channel_id=1, source_target_pairs={{0,1},{3,2},{4,5},{7,6},{8,9},{11,10},{12,13},{15,14},{16,17},{19,... | collective-permute-start | bytes 1179656 | tf_op jit(solution)/shard_map/ppermute | solution.py:500
  13.6 9.1 %collective-permute-start = (bf16[16,14336]{1,0:T(8,128)(2,1)S(1)}, bf16[16,14336]{1,0:T(8,128)(2,1)S(1)}, u32[]{:S(2)}, u32[]{:S(2)}) collective-permute-start(bf16[16,14336]{1,0:T(8,128)(2,1)S(1)} %shard_map.154.refs_2_), channel_id=1, source_target_pairs={{0,4},{4,0},{8,12},{12,8},{1,5},{5,1},{9,13},{13,9},{2,6},{6,2},{1... | collective-permute-start | bytes 1376264 | tf_op jit(solution)/shard_map/ppermute | solution.py:503
  21.3 27.7 %collective-permute-start.4 = (bf16[192,1536]{1,0:T(8,128)(2,1)S(1)}, bf16[192,1536]{1,0:T(8,128)(2,1)S(1)}, u32[]{:S(2)}, u32[]{:S(2)}) collective-permute-start(bf16[192,1536]{1,0:T(8,128)(2,1)S(1)} %get-tuple-element.32.refs_3_), channel_id=1, source_target_pairs={{0,1},{3,2},{4,5},{7,6},{8,9},{11,10},{12,13},{15,14},{16,17},{19,... | collective-permute-start | bytes 1769480 | tf_op jit(solution)/shard_map/ppermute | solution.py:500
  23.3 13.7 %collective-permute-start.5 = (bf16[8,14336]{1,0:T(8,128)(2,1)S(1)}, bf16[8,14336]{1,0:T(8,128)(2,1)S(1)}, u32[]{:S(2)}, u32[]{:S(2)}) collective-permute-start(bf16[8,14336]{1,0:T(8,128)(2,1)S(1)} %get-tuple-element.38), channel_id=1, source_target_pairs={{0,8},{4,12},{8,0},{12,4},{1,9},{5,13},{9,1},{13,5},{2,10},{6,14},... | collective-permute-start | bytes 688136 | tf_op jit(solution)/shard_map/ppermute | solution.py:503
  34.1 2.9 %copy-start.4 = (f32[8,10240]{1,0:T(8,128)S(1)}, f32[8,10240]{1,0:T(8,128)}, u32[]{:S(2)}) copy-start(f32[8,10240]{1,0:T(8,128)} %refs_5_.1) | copy-start | bytes 983044
  34.1 2.9 %copy-start.5 = (f32[8,10240]{1,0:T(8,128)S(1)}, f32[8,10240]{1,0:T(8,128)}, u32[]{:S(2)}) copy-start(f32[8,10240]{1,0:T(8,128)} %refs_6_.1) | copy-start | bytes 983044
  34.2 2.9 %copy-start.6 = (f32[8,10240]{1,0:T(8,128)S(1)}, f32[8,10240]{1,0:T(8,128)}, u32[]{:S(2)}) copy-start(f32[8,10240]{1,0:T(8,128)} %refs_7_.1) | copy-start | bytes 983044
  34.2 2.9 %copy-start.7 = (f32[4096,8]{0,1:T(8,128)S(1)}, f32[4096,8]{0,1:T(8,128)}, u32[]{:S(2)}) copy-start(f32[4096,8]{0,1:T(8,128)} %param.12) | copy-start | bytes 393220
  34.2 2.9 %copy-start.8 = (f32[4096,8]{0,1:T(8,128)S(1)}, f32[4096,8]{0,1:T(8,128)}, u32[]{:S(2)}) copy-start(f32[4096,8]{0,1:T(8,128)} %param.14) | copy-start | bytes 393220
  34.2 2.9 %copy-start.9 = (f32[4096,8]{0,1:T(8,128)S(1)}, f32[4096,8]{0,1:T(8,128)}, u32[]{:S(2)}) copy-start(f32[4096,8]{0,1:T(8,128)} %param.15) | copy-start | bytes 393220
  34.2 24.5 %collective-permute-start.1 = (bf16[192,2048]{1,0:T(8,128)(2,1)S(1)}, bf16[192,2048]{1,0:T(8,128)(2,1)S(1)}, u32[]{:S(2)}, u32[]{:S(2)}) collective-permute-start(bf16[192,2048]{1,0:T(8,128)(2,1)S(1)} %get-tuple-element.35.refs_3_), channel_id=1, source_target_pairs={{0,1},{3,2},{4,5},{7,6},{8,9},{11,10},{12,13},{15,14},{16,17},{19,... | collective-permute-start | bytes 2359304 | tf_op jit(solution)/shard_map/ppermute | solution.py:500
  36.3 19.2 %collective-permute-start.3 = (bf16[128,1024]{1,0:T(8,128)(2,1)S(1)}, bf16[128,1024]{1,0:T(8,128)(2,1)S(1)}, u32[]{:S(2)}, u32[]{:S(2)}) collective-permute-start(bf16[128,1024]{1,0:T(8,128)(2,1)S(1)} %shard_map.158.refs_8_), channel_id=1, source_target_pairs={{1,2},{2,1},{5,6},{6,5},{9,10},{10,9},{13,14},{14,13},{17,18},{18,... | collective-permute-start | bytes 786440 | tf_op jit(solution)/shard_map/ppermute | solution.py:500
  38.9 15.9 %collective-permute-start.8 = (bf16[8,4096]{1,0:T(8,128)(2,1)S(1)}, bf16[8,4096]{1,0:T(8,128)(2,1)S(1)}, u32[]{:S(2)}, u32[]{:S(2)}) collective-permute-start(bf16[8,4096]{1,0:T(8,128)(2,1)S(1)} %get-tuple-element.41), channel_id=1, source_target_pairs={{0,4},{4,0},{8,12},{12,8},{1,5},{5,1},{9,13},{13,9},{2,6},{6,2},{1... | collective-permute-start | bytes 196616 | tf_op jit(solution)/shard_map/ppermute | solution.py:503
  48.4 9.2 %collective-permute-start.6 = (bf16[8,10240]{1,0:T(8,128)(2,1)S(1)}, bf16[8,10240]{1,0:T(8,128)(2,1)S(1)}, u32[]{:S(2)}, u32[]{:S(2)}) collective-permute-start(bf16[8,10240]{1,0:T(8,128)(2,1)S(1)} %get-tuple-element.39.refs_2_), channel_id=1, source_target_pairs={{0,0},{1,4},{2,8},{3,12},{4,1},{5,5},{6,9},{7,13},{8,2},{9,6},{10,... | collective-permute-start | bytes 491528 | tf_op jit(solution)/shard_map/ppermute | solution.py:543
  49.0 30.8 %collective-permute-start.12 = (bf16[192,2048]{1,0:T(8,128)(2,1)S(1)}, bf16[192,2048]{1,0:T(8,128)(2,1)S(1)}, u32[]{:S(2)}, u32[]{:S(2)}) collective-permute-start(bf16[192,2048]{1,0:T(8,128)(2,1)S(1)} %get-tuple-element.40.refs_3_), channel_id=1, source_target_pairs={{0,1},{3,2},{4,5},{7,6},{8,9},{11,10},{12,13},{15,14},{16,17},{19,... | collective-permute-start | bytes 2359304 | tf_op jit(solution)/shard_map/ppermute | solution.py:500
  54.8 24.4 %collective-permute-start.13 = (bf16[128,1536]{1,0:T(8,128)(2,1)S(1)}, bf16[128,1536]{1,0:T(8,128)(2,1)S(1)}, u32[]{:S(2)}, u32[]{:S(2)}) collective-permute-start(bf16[128,1536]{1,0:T(8,128)(2,1)S(1)} %shard_map.161.refs_2_), channel_id=1, source_target_pairs={{1,2},{2,1},{5,6},{6,5},{9,10},{10,9},{13,14},{14,13},{17,18},{18,... | collective-permute-start | bytes 1179656 | tf_op jit(solution)/shard_map/ppermute | solution.py:500
  55.5 13.8 %collective-permute-start.9 = (bf16[16,4096]{1,0:T(8,128)(2,1)S(1)}, bf16[16,4096]{1,0:T(8,128)(2,1)S(1)}, u32[]{:S(2)}, u32[]{:S(2)}) collective-permute-start(bf16[16,4096]{1,0:T(8,128)(2,1)S(1)} %constant_dynamic-update-slice_fusion.refs_1_), channel_id=1, source_target_pairs={{0,8},{4,12},{8,0},{12,4},{1,9},{5,13},{9,1},{13,5},{2,10},{6,14},... | collective-permute-start | bytes 393224 | tf_op jit(solution)/shard_map/ppermute | solution.py:503
  57.6 29.2 %collective-permute-start.11 = (bf16[8,10240]{1,0:T(8,128)(2,1)S(1)}, bf16[8,10240]{1,0:T(8,128)(2,1)S(1)}, u32[]{:S(2)}, u32[]{:S(2)}) collective-permute-start(bf16[8,10240]{1,0:T(8,128)(2,1)S(1)} %collective-permute-done.6.refs_3_.refs_0_), channel_id=1, source_target_pairs={{0,1},{1,0},{2,3},{3,2},{4,5},{5,4},{6,7},{7,6},{8,9},{9,8},{10,11... | collective-permute-start | bytes 491528 | tf_op jit(solution)/shard_map/ppermute | solution.py:549
  59.4 37.3 %collective-permute-start.7 = (bf16[128,2048]{1,0:T(8,128)(2,1)S(1)}, bf16[128,2048]{1,0:T(8,128)(2,1)S(1)}, u32[]{:S(2)}, u32[]{:S(2)}) collective-permute-start(bf16[128,2048]{1,0:T(8,128)(2,1)S(1)} %shard_map.163.refs_2_), channel_id=1, source_target_pairs={{1,2},{2,1},{5,6},{6,5},{9,10},{10,9},{13,14},{14,13},{17,18},{18,... | collective-permute-start | bytes 1572872 | tf_op jit(solution)/shard_map/ppermute | solution.py:500
  69.3 32.0 %collective-permute-start.15 = (bf16[192,2048]{1,0:T(8,128)(2,1)S(1)}, bf16[192,2048]{1,0:T(8,128)(2,1)S(1)}, u32[]{:S(2)}, u32[]{:S(2)}) collective-permute-start(bf16[192,2048]{1,0:T(8,128)(2,1)S(1)} %get-tuple-element.42.refs_3_), channel_id=1, source_target_pairs={{0,1},{3,2},{4,5},{7,6},{8,9},{11,10},{12,13},{15,14},{16,17},{19,... | collective-permute-start | bytes 2359304 | tf_op jit(solution)/shard_map/ppermute | solution.py:500
  79.2 16.3 %collective-permute-start.10 = (f32[32,256]{1,0:T(8,128)S(1)}, f32[32,256]{1,0:T(8,128)S(1)}, u32[]{:S(2)}, u32[]{:S(2)}) collective-permute-start(f32[32,256]{1,0:T(8,128)S(1)} %shard_map.165.refs_2_.refs_0_), channel_id=1, source_target_pairs={{0,1},{1,0},{2,3},{3,2},{4,5},{5,4},{6,7},{7,6},{8,9},{9,8},{10,11... | collective-permute-start | bytes 98312 | tf_op jit(solution)/shard_map/ppermute | solution.py:553
  80.5 43.7 %collective-permute-start.19 = (bf16[128,2048]{1,0:T(8,128)(2,1)S(1)}, bf16[128,2048]{1,0:T(8,128)(2,1)S(1)}, u32[]{:S(2)}, u32[]{:S(2)}) collective-permute-start(bf16[128,2048]{1,0:T(8,128)(2,1)S(1)} %shard_map.167.refs_2_), channel_id=1, source_target_pairs={{1,2},{2,1},{5,6},{6,5},{9,10},{10,9},{13,14},{14,13},{17,18},{18,... | collective-permute-start | bytes 1572872 | tf_op jit(solution)/shard_map/ppermute | solution.py:500
  86.7 40.4 %collective-permute-start.23 = (bf16[192,1024]{1,0:T(8,128)(2,1)S(1)}, bf16[192,1024]{1,0:T(8,128)(2,1)S(1)}, u32[]{:S(2)}, u32[]{:S(2)}) collective-permute-start(bf16[192,1024]{1,0:T(8,128)(2,1)S(1)} %get-tuple-element.44.refs_2_), channel_id=1, source_target_pairs={{0,1},{3,2},{4,5},{7,6},{8,9},{11,10},{12,13},{15,14},{16,17},{19,... | collective-permute-start | bytes 1179656 | tf_op jit(solution)/shard_map/ppermute | solution.py:500
  95.5 7.2 %collective-permute-start.20 = (bf16[16,10240]{1,0:T(8,128)(2,1)S(1)}, bf16[16,10240]{1,0:T(8,128)(2,1)S(1)}, u32[]{:S(2)}, u32[]{:S(2)}) collective-permute-start(bf16[16,10240]{1,0:T(8,128)(2,1)S(1)} %shard_map.169.refs_2_.refs_5_), channel_id=1, source_target_pairs={{1,2},{2,1},{5,6},{6,5},{9,10},{10,9},{13,14},{14,13},{17,18},{18,... | collective-permute-start | bytes 983048 | tf_op jit(solution)/shard_map/ppermute | solution.py:500
  102.0 37.4 %collective-permute-start.16 = (bf16[128,2048]{1,0:T(8,128)(2,1)S(1)}, bf16[128,2048]{1,0:T(8,128)(2,1)S(1)}, u32[]{:S(2)}, u32[]{:S(2)}) collective-permute-start(bf16[128,2048]{1,0:T(8,128)(2,1)S(1)} %shard_map.173.refs_2_), channel_id=1, source_target_pairs={{1,2},{2,1},{5,6},{6,5},{9,10},{10,9},{13,14},{14,13},{17,18},{18,... | collective-permute-start | bytes 1572872 | tf_op jit(solution)/shard_map/ppermute | solution.py:500
  102.7 33.8 %collective-permute-start.21 = (bf16[16,10240]{1,0:T(8,128)(2,1)S(1)}, bf16[16,10240]{1,0:T(8,128)(2,1)S(1)}, u32[]{:S(2)}, u32[]{:S(2)}) collective-permute-start(bf16[16,10240]{1,0:T(8,128)(2,1)S(1)} %collective-permute-done.20.refs_3_.refs_6_), channel_id=1, source_target_pairs={{2,3},{1,0},{6,7},{5,4},{10,11},{9,8},{14,15},{13,12},{18,19},{17,... | collective-permute-start | bytes 983048 | tf_op jit(solution)/shard_map/ppermute | solution.py:500
  104.0 18.9 %collective-permute-start.18 = (f32[32,256]{1,0:T(8,128)S(1)}, f32[32,256]{1,0:T(8,128)S(1)}, u32[]{:S(2)}, u32[]{:S(2)}) collective-permute-start(f32[32,256]{1,0:T(8,128)S(1)} %shard_map.170.refs_2_.refs_0_), channel_id=1, source_target_pairs={{0,2},{1,3},{2,0},{3,1},{4,6},{5,7},{6,4},{7,5},{8,10},{9,11},{10,... | collective-permute-start | bytes 98312 | tf_op jit(solution)/shard_map/ppermute | solution.py:560
  122.9 12.3 %collective-permute-start.17 = (bf16[64,1536]{1,0:T(8,128)(2,1)S(1)}, bf16[64,1536]{1,0:T(8,128)(2,1)S(1)}, u32[]{:S(2)}, u32[]{:S(2)}) collective-permute-start(bf16[64,1536]{1,0:T(8,128)(2,1)S(1)} %shard_map.166.refs_3_), channel_id=1, source_target_pairs={{2,3},{1,0},{6,7},{5,4},{10,11},{9,8},{14,15},{13,12},{18,19},{17,... | collective-permute-start | bytes 589832 | tf_op jit(solution)/shard_map/ppermute | solution.py:500
  124.2 10.4 %collective-permute-start.22 = (bf16[64,1024]{1,0:T(8,128)(2,1)S(1)}, bf16[64,1024]{1,0:T(8,128)(2,1)S(1)}, u32[]{:S(2)}, u32[]{:S(2)}) collective-permute-start(bf16[64,1024]{1,0:T(8,128)(2,1)S(1)} %shard_map.162.refs_3_), channel_id=1, source_target_pairs={{2,3},{1,0},{6,7},{5,4},{10,11},{9,8},{14,15},{13,12},{18,19},{17,... | collective-permute-start | bytes 393224 | tf_op jit(solution)/shard_map/ppermute | solution.py:500
  127.1 14.2 %collective-permute-start.14 = (bf16[192,512]{1,0:T(8,128)(2,1)S(1)}, bf16[192,512]{1,0:T(8,128)(2,1)S(1)}, u32[]{:S(2)}, u32[]{:S(2)}) collective-permute-start(bf16[192,512]{1,0:T(8,128)(2,1)S(1)} %get-tuple-element.46.refs_3_), channel_id=1, source_target_pairs={{0,1},{3,2},{4,5},{7,6},{8,9},{11,10},{12,13},{15,14},{16,17},{19,... | collective-permute-start | bytes 589832 | tf_op jit(solution)/shard_map/ppermute | solution.py:500
  134.6 8.0 %collective-permute-start.27 = (bf16[128,1024]{1,0:T(8,128)(2,1)S(1)}, bf16[128,1024]{1,0:T(8,128)(2,1)S(1)}, u32[]{:S(2)}, u32[]{:S(2)}) collective-permute-start(bf16[128,1024]{1,0:T(8,128)(2,1)S(1)} %shard_map.176.refs_8_), channel_id=1, source_target_pairs={{1,2},{2,1},{5,6},{6,5},{9,10},{10,9},{13,14},{14,13},{17,18},{18,... | collective-permute-start | bytes 786440 | tf_op jit(solution)/shard_map/ppermute | solution.py:500
  135.3 11.5 %collective-permute-start.26 = (bf16[64,2048]{1,0:T(8,128)(2,1)S(1)}, bf16[64,2048]{1,0:T(8,128)(2,1)S(1)}, u32[]{:S(2)}, u32[]{:S(2)}) collective-permute-start(bf16[64,2048]{1,0:T(8,128)(2,1)S(1)} %shard_map.171.refs_2_), channel_id=1, source_target_pairs={{2,3},{1,0},{6,7},{5,4},{10,11},{9,8},{14,15},{13,12},{18,19},{17,... | collective-permute-start | bytes 786440 | tf_op jit(solution)/shard_map/ppermute | solution.py:500
  136.6 15.8 %collective-permute-start.25 = (bf16[64,2048]{1,0:T(8,128)(2,1)S(1)}, bf16[64,2048]{1,0:T(8,128)(2,1)S(1)}, u32[]{:S(2)}, u32[]{:S(2)}) collective-permute-start(bf16[64,2048]{1,0:T(8,128)(2,1)S(1)} %shard_map.174.refs_2_), channel_id=1, source_target_pairs={{2,3},{1,0},{6,7},{5,4},{10,11},{9,8},{14,15},{13,12},{18,19},{17,... | collective-permute-start | bytes 786440 | tf_op jit(solution)/shard_map/ppermute | solution.py:500
  140.1 18.0 %collective-permute-start.29 = (bf16[64,2048]{1,0:T(8,128)(2,1)S(1)}, bf16[64,2048]{1,0:T(8,128)(2,1)S(1)}, u32[]{:S(2)}, u32[]{:S(2)}) collective-permute-start(bf16[64,2048]{1,0:T(8,128)(2,1)S(1)} %shard_map.179.refs_3_), channel_id=1, source_target_pairs={{2,3},{1,0},{6,7},{5,4},{10,11},{9,8},{14,15},{13,12},{18,19},{17,... | collective-permute-start | bytes 786440 | tf_op jit(solution)/shard_map/ppermute | solution.py:500
  142.0 11.2 %collective-permute-start.24 = (bf16[128,512]{1,0:T(8,128)(2,1)S(1)}, bf16[128,512]{1,0:T(8,128)(2,1)S(1)}, u32[]{:S(2)}, u32[]{:S(2)}) collective-permute-start(bf16[128,512]{1,0:T(8,128)(2,1)S(1)} %shard_map.180.refs_2_), channel_id=1, source_target_pairs={{1,2},{2,1},{5,6},{6,5},{9,10},{10,9},{13,14},{14,13},{17,18},{18,... | collective-permute-start | bytes 393224 | tf_op jit(solution)/shard_map/ppermute | solution.py:500
  143.2 16.6 %collective-permute-start.30 = (bf16[64,1024]{1,0:T(8,128)(2,1)S(1)}, bf16[64,1024]{1,0:T(8,128)(2,1)S(1)}, u32[]{:S(2)}, u32[]{:S(2)}) collective-permute-start(bf16[64,1024]{1,0:T(8,128)(2,1)S(1)} %shard_map.181.refs_8_), channel_id=1, source_target_pairs={{2,3},{1,0},{6,7},{5,4},{10,11},{9,8},{14,15},{13,12},{18,19},{17,... | collective-permute-start | bytes 393224 | tf_op jit(solution)/shard_map/ppermute | solution.py:500
  153.8 6.8 %collective-permute-start.28 = (bf16[64,512]{1,0:T(8,128)(2,1)S(1)}, bf16[64,512]{1,0:T(8,128)(2,1)S(1)}, u32[]{:S(2)}, u32[]{:S(2)}) collective-permute-start(bf16[64,512]{1,0:T(8,128)(2,1)S(1)} %shard_map.184.refs_8_), channel_id=1, source_target_pairs={{2,3},{1,0},{6,7},{5,4},{10,11},{9,8},{14,15},{13,12},{18,19},{17,... | collective-permute-start | bytes 196616 | tf_op jit(solution)/shard_map/ppermute | solution.py:500

commit v4 on v2

--- a/solution.py
+++ b/solution.py
@@ -14,8 +14,9 @@
 adam_eps = 1e-08
 factor_scale = 2.0
 
-CHUNKS = (1, 3, 6, 6, 3, 1)
+CHUNKS = ((16, 2), (12, 3), (0, 4), (4, 4), (8, 4), (18, 2), (15, 1))
 VMEM_BYTES = 40 * 1024 * 1024
+WEIGHT = 5
 
 
 def apply_adam_rule(weights, moment, second, grads):
@@ -92,6 +93,7 @@
 LINE = (((0, 1), (3, 2)), ((1, 2), (2, 1)), ((2, 3), (1, 0)))
 (SEND_ROW, SECOND_AT, THIRD_AT, THIRD_FROM, OWN, FIRST_OWN, SECOND_OWN, ORDER, CORE_BIT, CHIP_BIT) = (
     0, 1, 2, 3, 4, 5, 6, 7, 11, 12)
+MOST = 2048
 
 
 def place_numbers(share):
@@ -111,7 +113,7 @@
     return jnp.stack([jnp.asarray(n, jnp.int32) for n in numbers])
 
 
-def call(body, place, operands, specs, earlier, out_shapes, out_specs, grid=(1,), flops=0, moved=0, aliases=None):
+def call(body, place, operands, specs, earlier, out_shapes, out_specs, grid=(1,), flops=0, moved=0):
     count = len(operands)
 
     def kernel(place_ref, *refs):
@@ -126,9 +128,8 @@
             out_specs=out_specs,
         ),
         out_shape=out_shapes,
-        input_output_aliases={} if aliases is None else aliases,
         compiler_params=pltpu.CompilerParams(vmem_limit_bytes=VMEM_BYTES),
-        cost_estimate=pl.CostEstimate(flops=flops, bytes_accessed=moved, transcendentals=0),
+        cost_estimate=pl.CostEstimate(flops=WEIGHT * flops, bytes_accessed=WEIGHT * moved, transcendentals=0),
     )(place, *operands, *earlier)
 
 
@@ -137,7 +138,7 @@
 
 
 def block_width(start, width, most):
-    block = most
+    block = min(most, width)
     while start % block or width % block:
         block //= 2
     return block
@@ -167,100 +168,100 @@
     )
 
 
-def add_second(place, partial, arrived, share, earlier):
-    width = partial.shape[1]
-    block = block_width(0, width, 1024) if width % 128 == 0 else width
-
-    def body(place_ref, partial_ref, upper_ref, lower_ref, out_ref):
-        out_ref[:share, :] = (partial_ref[:share, :] + upper_ref[...].astype(jnp.float32)).astype(out_ref.dtype)
-        out_ref[share:, :] = (partial_ref[share:, :] + lower_ref[...].astype(jnp.float32)).astype(out_ref.dtype)
-
-    return call(
-        body,
-        place,
-        [partial, arrived, arrived],
-        [
-            pl.BlockSpec((2 * share, block), lambda j, p: (p[SECOND_AT], j)),
-            pl.BlockSpec((share, block), lambda j, p: (p[SECOND_AT], j)),
-            pl.BlockSpec((share, block), lambda j, p: (p[SECOND_AT] + 1, j)),
-        ],
-        earlier,
-        jax.ShapeDtypeStruct((2 * share, width), arrived.dtype),
-        pl.BlockSpec((2 * share, block), lambda j, p: (0, j)),
-        grid=(width // block,),
-        moved=16 * share * width,
-    )
-
-
-def add_third(place, partial, arrived, share, earlier):
-    width = partial.shape[1]
-    block = block_width(0, width, 1024) if width % 128 == 0 else width
-
-    def body(place_ref, partial_ref, arrived_ref, out_ref):
-        out_ref[...] = (partial_ref[...] + arrived_ref[...].astype(jnp.float32)).astype(out_ref.dtype)
-
-    return call(
-        body,
-        place,
-        [partial, arrived],
-        [
-            pl.BlockSpec((share, block), lambda j, p: (p[THIRD_AT], j)),
-            pl.BlockSpec((share, block), lambda j, p: (p[THIRD_FROM], j)),
-        ],
-        earlier,
-        jax.ShapeDtypeStruct((share, width), arrived.dtype),
-        pl.BlockSpec((share, block), lambda j, p: (0, j)),
-        grid=(width // block,),
-        moved=8 * share * width,
-    )
-
-
-def own_block_specs(share, block):
-    return [
-        pl.BlockSpec((share, block), lambda j, p: (p[OWN], j)),
-        pl.BlockSpec((share, block), lambda j, p: (p[FIRST_OWN], j)),
-        pl.BlockSpec((share, block), lambda j, p: (p[SECOND_OWN], j)),
-        pl.BlockSpec((share, block), lambda j, p: (0, j)),
-    ]
-
-
-def own_total(refs):
-    total = refs[0][...]
-    for ref in refs[1:]:
-        total = total + ref[...].astype(jnp.float32)
-    return total
-
-
-def finish_chunk(place, terms, spread, factors, decoded, start, width, share, full_width, earlier):
-    block = block_width(start, width, 1024)
-    first = start // block
-    operands = [*terms, spread, *factors]
-
-    def body(place_ref, own_ref, one_ref, two_ref, three_ref, spread_ref, pair_ref, near_ref, far_ref, *rest):
-        other = near_ref[...] + far_ref[...]
-        ranks = jnp.concatenate([pair_ref[...], other, pair_ref[...], other], axis=0)
-        change = jnp.dot(spread_ref[...], ranks, preferred_element_type=jnp.float32)
-        rest[-1][...] = own_total((own_ref, one_ref, two_ref, three_ref)) + change
-
+def add_second(place, pieces, share, earlier):
+    operands, specs = [], []
+    for partial, arrived in pieces:
+        width = partial.shape[1]
+        operands += [partial, arrived, arrived]
+        specs += [
+            pl.BlockSpec((2 * share, width), lambda j, p: (p[SECOND_AT], 0)),
+            pl.BlockSpec((share, width), lambda j, p: (p[SECOND_AT], 0)),
+            pl.BlockSpec((share, width), lambda j, p: (p[SECOND_AT] + 1, 0)),
+        ]
+    widths = [partial.shape[1] for partial, _ in pieces]
+
+    def body(place_ref, *refs):
+        out_ref, at = refs[-1], 0
+        for i, width in enumerate(widths):
+            partial_ref, upper_ref, lower_ref = refs[3 * i:3 * i + 3]
+            to = slice(at, at + width)
+            out_ref[:share, to] = (partial_ref[:share, :] + upper_ref[...].astype(jnp.float32)).astype(jnp.bfloat16)
+            out_ref[share:, to] = (partial_ref[share:, :] + lower_ref[...].astype(jnp.float32)).astype(jnp.bfloat16)
+            at += width
+
+    shape = (2 * share, sum(widths))
+    return call(
+        body, place, operands, specs, earlier, jax.ShapeDtypeStruct(shape, jnp.bfloat16), whole(shape),
+        moved=16 * share * shape[1],
+    )
+
+
+def add_third(place, pieces, share, earlier):
+    operands, specs = [], []
+    for partial, arrived, _ in pieces:
+        operands += [partial, arrived]
+        specs += [
+            pl.BlockSpec((share, partial.shape[1]), lambda j, p: (p[THIRD_AT], 0)),
+            pl.BlockSpec((share, arrived.shape[1]), lambda j, p: (p[THIRD_FROM], 0)),
+        ]
+    widths = [partial.shape[1] for partial, _, _ in pieces]
+    inside = [at for _, _, at in pieces]
+
+    def body(place_ref, *refs):
+        out_ref, at = refs[-1], 0
+        for i, width in enumerate(widths):
+            partial_ref, arrived_ref = refs[2 * i:2 * i + 2]
+            arrived = arrived_ref[:, inside[i]:inside[i] + width].astype(jnp.float32)
+            out_ref[:, at:at + width] = (partial_ref[...] + arrived).astype(jnp.bfloat16)
+            at += width
+
+    shape = (share, sum(widths))
+    return call(
+        body, place, operands, specs, earlier, jax.ShapeDtypeStruct(shape, jnp.bfloat16), whole(shape),
+        moved=8 * share * shape[1],
+    )
+
+
+def finish_chunks(place, pieces, spread, factors, share, earlier, full_width=None, done=()):
+    operands, specs = [spread], [whole(spread.shape)]
     half = factors[0].shape[0]
-    specs = own_block_specs(share, block) + [whole(spread.shape)]
-    specs += [pl.BlockSpec((half, block), lambda j, p: (0, first + j))] * 3
-    aliases = None
-    if decoded is not None:
-        aliases = {1 + len(operands): 0}
-        operands.append(decoded)
-        specs.append(pl.BlockSpec(memory_space=pl.ANY))
-    return call(
-        body,
-        place,
-        operands,
-        specs,
-        earlier,
-        jax.ShapeDtypeStruct((share, full_width), jnp.float32),
-        pl.BlockSpec((share, block), lambda j, p: (0, first + j)),
-        grid=(width // block,),
-        moved=14 * share * width,
-        aliases=aliases,
+    for start, partial, first, second, _, third, _ in pieces:
+        width = partial.shape[1]
+        operands += [partial, first, second, third, *factors]
+        specs += [
+            pl.BlockSpec((share, width), lambda j, p: (p[OWN], 0)),
+            pl.BlockSpec((share, width), lambda j, p: (p[FIRST_OWN], 0)),
+            pl.BlockSpec((share, second.shape[1]), lambda j, p: (p[SECOND_OWN], 0)),
+            whole(third.shape),
+        ] + [pl.BlockSpec((half, width), lambda j, p, at=start // width: (0, at))] * 3
+    for columns, _ in done:
+        operands.append(columns)
+        specs.append(whole(columns.shape))
+    places = [(start, partial.shape[1], two, three) for start, partial, _, _, two, _, three in pieces]
+    shape = (share, sum(width for _, width, _, _ in places) if full_width is None else full_width)
+
+    def body(place_ref, spread_ref, *refs):
+        out_ref, at = refs[-1], 0
+        for i, (start, width, two, three) in enumerate(places):
+            own_ref, first_ref, second_ref, third_ref, pair_ref, near_ref, far_ref = refs[7 * i:7 * i + 7]
+            other = near_ref[...] + far_ref[...]
+            ranks = jnp.concatenate([pair_ref[...], other, pair_ref[...], other], axis=0)
+            total = own_ref[...] + first_ref[...].astype(jnp.float32)
+            total = total + second_ref[:, two:two + width].astype(jnp.float32)
+            total = total + third_ref[:, three:three + width].astype(jnp.float32)
+            total = total + jnp.dot(spread_ref[...], ranks, preferred_element_type=jnp.float32)
+            to = at if full_width is None else start
+            out_ref[:, to:to + width] = total
+            at += width
+        for ref, (_, parts) in zip(refs[7 * len(places):], done):
+            at = 0
+            for start, width in parts:
+                out_ref[:, start:start + width] = ref[:, at:at + width]
+                at += width
+
+    return call(
+        body, place, operands, specs, earlier, jax.ShapeDtypeStruct(shape, jnp.float32), whole(shape),
+        moved=14 * share * shape[1],
     )
 
 
@@ -343,37 +344,76 @@
     )
 
 
-def inner_products(place, x, near, far, share, earlier):
-    rows, ranks = x.shape[0], 2 * near.shape[0]
-    sent = rows - share
-
-    def body(place_ref, x_ref, near_ref, far_ref, inner_ref, send_ref):
-        half = ranks // 2
-        for at, ref in ((0, near_ref), (half, far_ref)):
-            inner_ref[:, at:at + half] = lax.dot_general(
-                x_ref[...], ref[...], (((1,), (1,)), ((), ())), preferred_element_type=jnp.float32
+def inner_products(place, x, near, far, turned, earlier):
+    rows, ranks = x.shape[0], turned.shape[0]
+    width = turned.shape[1]
+    inner_width = 4 * rows
+
+    def body(place_ref, x_ref, near_ref, far_ref, turned_ref, inner_ref, send_ref):
+        for i, ref in enumerate((near_ref, far_ref)):
+            products = lax.dot_general(
+                ref[...], x_ref[...], (((1,), (1,)), ((), ())), preferred_element_type=jnp.float32
             )
-        send_ref[...] = inner_ref[pl.ds(pl.multiple_of(place_ref[SEND_ROW], share), sent), :]
-
-    return call(
-        body,
-        place,
-        [x, near, far],
-        [whole(x.shape), whole(near.shape), whole(far.shape)],
-        earlier,
-        [jax.ShapeDtypeStruct((rows, ranks), jnp.float32), jax.ShapeDtypeStruct((sent, ranks), jnp.float32)],
-        [whole((rows, ranks)), whole((sent, ranks))],
-        flops=2 * rows * ranks * x.shape[1],
+            for j in range(2):
+                at = (2 * i + j) * rows
+                inner_ref[:, at:at + rows] = products[j * ranks:(j + 1) * ranks]
+        high, low = split_high_low(inner_ref[...])
+        send_ref[:, :width] = turned_ref[...]
+        send_ref[:, width:width + inner_width] = high
+        send_ref[:, width + inner_width:] = low
+
+    shapes = [(ranks, inner_width), (ranks, width + 2 * inner_width)]
+    return call(
+        body,
+        place,
+        [x, near, far, turned],
+        [whole(x.shape), whole(near.shape), whole(far.shape), whole(turned.shape)],
+        earlier,
+        [jax.ShapeDtypeStruct(shapes[0], jnp.float32), jax.ShapeDtypeStruct(shapes[1], jnp.bfloat16)],
+        [whole(shape) for shape in shapes],
+        flops=8 * rows * ranks * x.shape[1],
         moved=2 * rows * x.shape[1],
     )
 
 
-def spread_inner(place, terms, share, earlier):
-    ranks = terms[0].shape[1]
-    portion = ranks // 4
-
-    def body(place_ref, own_ref, one_ref, two_ref, three_ref, out_ref):
-        inner = factor_scale * own_total((own_ref, one_ref, two_ref, three_ref))
+def join_pair(place, turned, swapped, inner, earlier):
+    ranks, width = turned.shape
+    inner_width = inner.shape[1]
+
+    def body(place_ref, turned_ref, swapped_ref, inner_ref, pair_ref, sum_ref):
+        both = [turned_ref[...].astype(jnp.float32), swapped_ref[:, :width].astype(jnp.float32)]
+        pair_ref[:, :width] = jnp.concatenate(both, axis=0).astype(jnp.bfloat16)
+        total = inner_ref[...] + swapped_ref[:, width:width + inner_width].astype(jnp.float32)
+        total = total + swapped_ref[:, width + inner_width:].astype(jnp.float32)
+        sum_ref[...] = total
+        halves = [half.astype(jnp.float32) for half in split_high_low(total)]
+        pair_ref[:, width:] = jnp.concatenate(halves, axis=0).astype(jnp.bfloat16)
+
+    shapes = [(2 * ranks, width + inner_width), (ranks, inner_width)]
+    return call(
+        body,
+        place,
+        [turned, swapped, inner],
+        [whole(turned.shape), whole(swapped.shape), whole(inner.shape)],
+        earlier,
+        [jax.ShapeDtypeStruct(shapes[0], jnp.bfloat16), jax.ShapeDtypeStruct(shapes[1], jnp.float32)],
+        [whole(shape) for shape in shapes],
+        moved=8 * ranks * width,
+    )
+
+
+def spread_inner(place, inner, near, far, width, share, earlier):
+    portion = inner.shape[0]
+    rows = inner.shape[1] // 4
+    ranks = 4 * portion
+
+    def body(place_ref, inner_ref, near_ref, far_ref, out_ref):
+        other = near_ref[:, width:].astype(jnp.float32) + far_ref[:, width:].astype(jnp.float32)
+        total = factor_scale * (inner_ref[...] + (other[:portion] + other[portion:]))
+        total = jnp.concatenate([total[:, i * rows:(i + 1) * rows] for i in range(4)], axis=0)
+        shape = (share, rows)
+        mine = lax.broadcasted_iota(jnp.int32, shape, 0) + place_ref[OWN] * share
+        mine = jnp.where(lax.broadcasted_iota(jnp.int32, shape, 1) == mine, 1.0, 0.0).astype(jnp.bfloat16)
         block = lax.broadcasted_iota(jnp.int32, (ranks, ranks), 1) // portion
         source = jnp.full((ranks, ranks), 0, jnp.int32)
         for i in range(4):
@@ -381,16 +421,17 @@
         column = lax.broadcasted_iota(jnp.int32, (ranks, ranks), 1) % portion
         chosen = lax.broadcasted_iota(jnp.int32, (ranks, ranks), 0) == source * portion + column
         chosen = jnp.where(chosen, 1.0, 0.0).astype(jnp.bfloat16)
-        halves = [
-            jnp.dot(half, chosen, preferred_element_type=jnp.float32) for half in split_high_low(inner)
-        ]
+        halves = []
+        for half in split_high_low(total):
+            turned = lax.dot_general(mine, half, (((1,), (1,)), ((), ())), preferred_element_type=jnp.float32)
+            halves.append(jnp.dot(turned.astype(jnp.bfloat16), chosen, preferred_element_type=jnp.float32))
         out_ref[...] = jnp.concatenate(halves, axis=1).astype(jnp.bfloat16)
 
     return call(
         body,
         place,
-        list(terms),
-        own_block_specs(share, ranks),
+        [inner, near, far],
+        [whole(inner.shape), whole(near.shape), whole(far.shape)],
         earlier,
         jax.ShapeDtypeStruct((share, 2 * ranks), jnp.bfloat16),
         whole((share, 2 * ranks)),
@@ -417,11 +458,10 @@
     part_in = replica_input_gradient[0].T.reshape(2, 2, ranks, -1)
     part_out = replica_output_gradient[0].reshape(2, 2, ranks, -1)
 
-    unit = width // sum(CHUNKS)
-    widths = [unit * c for c in CHUNKS]
-    starts = [sum(widths[:i]) for i in range(len(widths))]
-    count = len(widths)
-    partials, seconds, thirds, arrived = {}, {}, {}, {}
+    unit = width // 20
+    starts = [unit * at for at, _ in CHUNKS]
+    widths = [unit * wide for _, wide in CHUNKS]
+    partials, firsts, seconds, thirds = {}, {}, {}, {}
 
     def line(step, values):
         return lax.ppermute(values, "tp", LINE[step])
@@ -430,74 +470,74 @@
         return lax.ppermute(values, "rep", [(i, i ^ bit) for i in range(4)])
 
     def matmul(c, *earlier):
-        most = 256 if c == 0 else 512
-        partials[c], send = matmul_chunk(place, x, base, starts[c], widths[c], share, earlier, most)
-        arrived[c, 0] = line(0, send)
+        partials[c], send = matmul_chunk(place, x, base, starts[c], widths[c], share, earlier, 512)
+        firsts[c] = line(0, send)
         return send
 
-    def second(c, *earlier):
-        seconds[c] = add_second(place, partials[c], arrived[c, 0], share, earlier)
-        arrived[c, 1] = line(1, seconds[c])
-        return seconds[c]
-
-    def third(c, *earlier):
-        thirds[c] = add_third(place, partials[c], arrived[c, 1], share, earlier)
-        arrived[c, 2] = line(2, thirds[c])
-        return thirds[c]
-
+    def second(chunks, *earlier):
+        send = add_second(place, [(partials[c], firsts[c]) for c in chunks], share, earlier)
+        got, at = line(1, send), 0
+        for c in chunks:
+            seconds[c] = (got, at)
+            at += widths[c]
+        return send
+
+    def third(chunks, *earlier):
+        send = add_third(place, [(partials[c], *seconds[c]) for c in chunks], share, earlier)
+        got, at = line(2, send), 0
+        for c in chunks:
+            thirds[c] = (got, at)
+            at += widths[c]
+        return send
+
+    def finish(chunks, *earlier, full_width=None, done=()):
+        pieces = [(starts[c], partials[c], firsts[c], *seconds[c], *thirds[c]) for c in chunks]
+        columns = finish_chunks(place, pieces, spread, factors, share, earlier, full_width, done)
+        finished.append((columns, [(starts[c], widths[c]) for c in chunks]))
+        return columns
+
+    finished = []
     last = matmul(0)
-    last = matmul(1, last)
-    last = matmul(2, last)
     last = gradients_out(place, part_in, part_out, [last])
     from_core = chip(1, last)
-    last = second(0, last)
-    last = matmul(3, last)
+    last = matmul(1, last)
     across, keep = gradients_on(place, part_in, part_out, from_core, [last])
     from_chip = chip(2, across)
-    last = second(1, keep)
-    last = third(0, last)
+    last = matmul(2, keep)
     in_state = (input_factor.T, input_first_moment.T, input_second_moment.T)
     out_state = (output_factor, output_first_moment, output_second_moment)
     states = update_factors(place, keep, from_chip, in_state, out_state, [last])
     new_in, first_in, second_in, half_in, new_out, first_out, second_out, half_out = states
+    turned = lax.ppermute(half_out, ("rep", "tp"), [(4 * a + b, 4 * b + a) for a in range(4) for b in range(4)])
     near_in = jnp.concatenate([half_in, chip(1, half_in)], axis=0)
     far_in = chip(2, near_in)
-    turned = lax.ppermute(half_out, ("rep", "tp"), [(4 * a + b, 4 * b + a) for a in range(4) for b in range(4)])
-    last = second(2, half_out)
+    last = second((0, 1), half_out)
+    last = matmul(3, last)
+    inner, last = inner_products(place, x, near_in, far_in, turned, [last])
+    swapped = lax.ppermute(last, "tp", [(i, i ^ 1) for i in range(4)])
+    last = second((2,), last)
     last = matmul(4, last)
-    last = matmul(5, last)
-    last = third(1, last)
-    inner, inner_send = inner_products(place, x, near_in, far_in, share, [last])
-    inner_arrived = [line(0, inner_send)]
-    last = third(2, inner_send)
-    pair = jnp.concatenate([turned, lax.ppermute(turned, "tp", [(i, i ^ 1) for i in range(4)])], axis=0)
+    last = second((3,), last)
+    last = third((0, 1), last)
+    pair, inner = join_pair(place, turned, swapped, inner, [last])
     near_out = line(1, pair)
-    inner_second = add_second(place, inner, inner_arrived[0], share, [last])
-    inner_arrived.append(line(1, inner_second))
+    last = matmul(5, pair)
+    last = matmul(6, last, thirds[0][0])
+    last = second((4,), last)
+    last = third((2, 3), last)
     far_out = line(2, near_out)
-    last = second(3, inner_second)
-    inner_third = add_third(place, inner, inner_arrived[1], share, [last])
-    inner_arrived.append(line(2, inner_third))
-    last = second(4, inner_third)
-    last = third(3, last)
-    spread = spread_inner(place, (inner, *inner_arrived), share, [last])
-
-    decoded = None
-
-    def finish(c, decoded, *earlier):
-        terms = (partials[c], arrived[c, 0], arrived[c, 1], arrived[c, 2])
-        return finish_chunk(
-            place, terms, spread, (pair, near_out, far_out), decoded, starts[c], widths[c], share, width, earlier
-        )
-
-    decoded = finish(0, None)
-    decoded = finish(1, decoded)
-    last = second(5, decoded)
-    last = third(4, last)
-    decoded = finish(2, decoded, last)
-    last = third(5, decoded)
-    for c in range(3, count):
-        decoded = finish(c, decoded, last)
+    factors = (pair, near_out, far_out)
+    last = second((5,), last)
+    last = second((6,), last)
+    last = spread = spread_inner(place, inner, near_out, far_out, width, share, [last])
+    last = finish((0, 1), last)
+    last = third((4,), last)
+    last = third((5,), last)
+    last = third((6,), last)
+    last = finish((2, 3), last)
+    last = finish((4,), last)
+    last = finish((5,), last)
+    decoded = finish((6,), last, full_width=width, done=list(finished))
     return (decoded, new_in.T, new_out, first_in.T, second_in.T, first_out, second_out)
 
 

time: 198 us -> 135 us (0.68); the launches traced: 194 us -> 135 us
  waiting for transfers between devices: 38.8 us -> 12.9 us
  starting transfers between devices: 71.5 us -> 48.3 us
  Pallas kernels: 77.4 us -> 70.3 us
  local copies, waits for them, and re-layouts: 5.25 us -> 1.74 us
    ppermute x23 -> x20, waiting for transfers between devices: 38.2 us -> 12.8 us  [line(): return lax.ppermute(values, 'tp', LINE[step])]
    ppermute x1, starting transfers between devices: 23.8 us -> 0.29 us  [local_line(): swapped = lax.ppermute(last, 'tp', [(i, i ^ 1) for i in range(4)])]
    pallas_call x31 -> x29, Pallas kernels: 77.4 us -> 70.3 us  [call(): pl.pallas_call(kernel, grid_spec=pltpu.PrefetchScalarGridSpec(num_scalar_...]
    unnamed x26 -> x25, local copies, waits for them, and re-layouts: 5.14 us -> 1.65 us
    ppermute x23 -> x20, starting transfers between devices: 41.2 us -> 42.4 us  [line(): return lax.ppermute(values, 'tp', LINE[step])]
  transfers between devices with their start and end apart: 29 -> 26, of which waited for: 5 -> 6; matrix products, arithmetic and copies ran while one was open for 0% -> 0% of each run, Pallas kernels for 37% -> 47%
where the time goes in v4:
time: 135 us
  Pallas kernels  70.3 us (52%)
  starting transfers between devices  48.3 us (36%)
  waiting for transfers between devices  12.9 us (10%)
  local copies, waits for them, and re-layouts  1.74 us (1%)
    pallas_call x29, Pallas kernels, call(): pl.pallas_call(kernel, grid_spec=pltpu.PrefetchScalarGridSpec(num_scalar_...  70.3 us
    ppermute x20, starting transfers between devices, line(): return lax.ppermute(values, 'tp', LINE[step])  42.4 us
    ppermute x20, waiting for transfers between devices, line(): return lax.ppermute(values, 'tp', LINE[step])  12.8 us
    ppermute x4, starting transfers between devices, chip(): return lax.ppermute(values, 'rep', [(i, i ^ bit) for i in range(4)])  4.89 us
  transfers between devices with their start and end apart: 26, of which 6 were waited for; matrix products, arithmetic and copies ran while one was open for 0% of the time, Pallas kernels for 47%

profile of v4, /device:TPU:0, one launch (start us, length us, event | category | flops | bytes accessed | tf_op | source)
XLA Modules:
  0.0 134.6 jit_solution(5909674239587377114)
XLA Ops:
  0.8 1.6 %copy-done = bf16[256,4096]{1,0:T(8,128)(2,1)S(1)} copy-done((bf16[256,4096]{1,0:T(8,128)(2,1)S(1)}, bf16[256,4096]{1,0:T(8,128)(2,1)}, u32[]{:S(2)}) %copy-start) | copy-done | bytes 2097176
  2.4 5.5 %shard_map.153 = (f32[256,1024]{1,0:T(8,128)S(1)}, bf16[192,1024]{1,0:T(8,128)(2,1)S(1)}) custom-call(s32[13]{0:T(128)S(1)} %stack.55.place_ref, bf16[256,4096]{1,0:T(8,128)(2,1)S(1)} %copy-done, bf16[4096,10240]{1,0:T(8,128)(2,1)} %refs_1_.13), custom_call_target="tpu_custom_call" | custom-call | flops 10737418240 | bytes 41943040 | tf_op jit(solution)/shard_map/pallas_call | solution.py:122
  7.9 5.1 %collective-permute-start.5 = (bf16[192,1024]{1,0:T(8,128)(2,1)S(1)}, bf16[192,1024]{1,0:T(8,128)(2,1)S(1)}, u32[]{:S(2)}, u32[]{:S(2)}) collective-permute-start(bf16[192,1024]{1,0:T(8,128)(2,1)S(1)} %get-tuple-element.35.refs_2_), channel_id=1, source_target_pairs={{0,1},{3,2},{4,5},{7,6},{8,9},{11,10},{12,13},{15,14},{16,17},{19,... | collective-permute-start | bytes 1179656 | tf_op jit(solution)/shard_map/ppermute | solution.py:467
  13.7 7.7 %shard_map.155 = (f32[256,1536]{1,0:T(8,128)S(1)}, bf16[192,1536]{1,0:T(8,128)(2,1)S(1)}) custom-call(s32[13]{0:T(128)S(1)} %stack.55.place_ref, bf16[256,4096]{1,0:T(8,128)(2,1)S(1)} %copy-done.1, bf16[4096,10240]{1,0:T(8,128)(2,1)} %refs_1_.13, bf16[16,14336]{1,0:T(8,128)(2,1)S(1)} %shard_map.154.refs_2_), custom_call_target="tpu_custom_call" | custom-call | flops 16106127360 | bytes 62914560 | tf_op jit(solution)/shard_map/pallas_call | solution.py:122
  21.3 1.3 collective-permute-start.6
  22.7 0.7 shard_map.156
  23.3 1.6 %collective-permute-start.1 = (bf16[8,14336]{1,0:T(8,128)(2,1)S(1)}, bf16[8,14336]{1,0:T(8,128)(2,1)S(1)}, u32[]{:S(2)}, u32[]{:S(2)}) collective-permute-start(bf16[8,14336]{1,0:T(8,128)(2,1)S(1)} %get-tuple-element.38), channel_id=1, source_target_pairs={{0,8},{4,12},{8,0},{12,4},{1,9},{5,13},{9,1},{13,5},{2,10},{6,14},... | collective-permute-start | bytes 688136 | tf_op jit(solution)/shard_map/ppermute | solution.py:470
  24.9 9.2 %shard_map.157 = (f32[256,2048]{1,0:T(8,128)S(1)}, bf16[192,2048]{1,0:T(8,128)(2,1)S(1)}) custom-call(s32[13]{0:T(128)S(1)} %stack.55.place_ref, bf16[256,4096]{1,0:T(8,128)(2,1)S(1)} %copy-done.1, bf16[4096,10240]{1,0:T(8,128)(2,1)} %refs_1_.13, f32[8,14336]{1,0:T(8,128)S(1)} %get-tuple-element.37.refs_2_.refs_0_), custom_call_target="tpu_custom_call" | custom-call | flops 21474836480 | bytes 83886080 | tf_op jit(solution)/shard_map/pallas_call | solution.py:122
  34.2 1.3 collective-permute-start.10
  35.6 1.9 %shard_map.158 = (f32[8,4096]{1,0:T(8,128)}, f32[8,4096]{1,0:T(8,128)}, f32[8,4096]{1,0:T(8,128)}, bf16[8,4096]{1,0:T(8,128)(2,1)S(1)}, f32[8,10240]{1,0:T(8,128...) custom-call(s32[13]{0:T(128)S(1)} %stack.55.place_ref, ...), custom_call_target="tpu_custom_call" | custom-call | bytes 18350080 | tf_op jit(solution)/shard_map/pallas_call | solution.py:122
  37.7 0.7 collective-permute-start.2
  38.3 0.7 shard_map.159.refs_2_
  39.0 0.7 collective-permute-start.8
  39.7 3.1 %collective-permute-start.4 = (bf16[16,4096]{1,0:T(8,128)(2,1)S(1)}, bf16[16,4096]{1,0:T(8,128)(2,1)S(1)}, u32[]{:S(2)}, u32[]{:S(2)}) collective-permute-start(bf16[16,4096]{1,0:T(8,128)(2,1)S(1)} %constant_dynamic-update-slice_fusion.refs_1_), channel_id=1, source_target_pairs={{0,8},{4,12},{8,0},{12,4},{1,9},{5,13},{9,1},{13,5},{2,10},{6,14},... | collective-permute-start | bytes 393224 | tf_op jit(solution)/shard_map/ppermute | solution.py:470
  42.8 9.2 %shard_map.160 = (f32[256,2048]{1,0:T(8,128)S(1)}, bf16[192,2048]{1,0:T(8,128)(2,1)S(1)}) custom-call(s32[13]{0:T(128)S(1)} %stack.55.place_ref, bf16[256,4096]{1,0:T(8,128)(2,1)S(1)} %copy-done.1, bf16[4096,10240]{1,0:T(8,128)(2,1)} %refs_1_.13, bf16[128,2560]{1,0:T(8,128)(2,1)S(1)} %shard_map.159.refs_2_), custom_call_target="tpu_custom_call" | custom-call | flops 21474836480 | bytes 83886080 | tf_op jit(solution)/shard_map/pallas_call | solution.py:122
  52.0 4.9 %collective-permute-start.9 = (bf16[192,2048]{1,0:T(8,128)(2,1)S(1)}, bf16[192,2048]{1,0:T(8,128)(2,1)S(1)}, u32[]{:S(2)}, u32[]{:S(2)}) collective-permute-start(bf16[192,2048]{1,0:T(8,128)(2,1)S(1)} %get-tuple-element.44.refs_4_), channel_id=1, source_target_pairs={{0,1},{3,2},{4,5},{7,6},{8,9},{11,10},{12,13},{15,14},{16,17},{19,... | collective-permute-start | bytes 2359304 | tf_op jit(solution)/shard_map/ppermute | solution.py:467
  57.0 1.7 %shard_map.161 = (f32[8,1024]{1,0:T(8,128)S(1)}, bf16[8,12288]{1,0:T(8,128)(2,1)S(1)}) custom-call(s32[13]{0:T(128)S(1)} %stack.55.place_ref, bf16[256,4096]{1,0:T(8,128)(2,1)S(1)} %copy-done.1, bf16[16,4096]{1,0:T(8,128)(2,1)S(1)} %constant_dynamic-update-slice_fusion.refs_1_, bf16[16,4096]{1,0:T(8,128)(2,1)S(1)} %collective-permute-done.4.refs_2_, ...), custom_call_target="tpu_custom_call" | custom-call | flops 335544320 | bytes 10485760 | tf_op jit(solution)/shard_map/pallas_call | solution.py:122
  59.6 0.7 collective-permute-start.16
  60.3 9.9 %shard_map.163 = (f32[256,2048]{1,0:T(8,128)S(1)}, bf16[192,2048]{1,0:T(8,128)(2,1)}) custom-call(s32[13]{0:T(128)S(1)} %stack.55.place_ref, bf16[256,4096]{1,0:T(8,128)(2,1)S(1)} %copy-done.1, bf16[4096,10240]{1,0:T(8,128)(2,1)} %refs_1_.13, bf16[128,2048]{1,0:T(8,128)(2,1)S(1)} %shard_map.162.refs_2_), custom_call_target="tpu_custom_call" | custom-call | flops 21474836480 | bytes 83886080 | tf_op jit(solution)/shard_map/pallas_call | solution.py:122
  70.2 8.6 %collective-permute-start.18 = (bf16[192,2048]{1,0:T(8,128)(2,1)}, bf16[192,2048]{1,0:T(8,128)(2,1)S(1)}, u32[]{:S(2)}, u32[]{:S(2)}) collective-permute-start(bf16[192,2048]{1,0:T(8,128)(2,1)} %get-tuple-element.49.refs_3_), channel_id=1, source_target_pairs={{0,1},{3,2},{4,5},{7,6},{8,9},{11,10},{12,13},{15,14},{16,17},{19,... | collective-permute-start | bytes 2359304 | tf_op jit(solution)/shard_map/ppermute | solution.py:467
  78.9 1.4 %shard_map.164.refs_4_ = bf16[128,2048]{1,0:T(8,128)(2,1)} custom-call(s32[13]{0:T(128)S(1)} %stack.55.place_ref, f32[256,2048]{1,0:T(8,128)S(1)} %get-tuple-element.47.refs_0_.refs_2_.refs_8_, bf16[192,2048]{1,0:T(8,128)(2,1)S(1)} %collective-permute-done.9.refs_1_.refs_2_.refs_9_, bf16[192,2048]{1,0:T(8,128)(2,1)S(1)} %collective-permute-done.9.refs_1_.refs_2_.refs_9_, ...), custom_call_target="tpu_custom_call" | custom-call | bytes 10485760 | tf_op jit(solution)/shard_map/pallas_call | solution.py:122
  80.3 0.7 collective-permute-start.17
  81.7 1.3 collective-permute-start.13
  83.6 0.7 collective-permute-start.11
  84.2 5.5 %shard_map.167 = (f32[256,1024]{1,0:T(8,128)S(1)}, bf16[192,1024]{1,0:T(8,128)(2,1)S(1)}) custom-call(s32[13]{0:T(128)S(1)} %stack.55.place_ref, bf16[256,4096]{1,0:T(8,128)(2,1)S(1)} %copy-done.1, bf16[4096,10240]{1,0:T(8,128)(2,1)} %refs_1_.13, bf16[16,11264]{1,0:T(8,128)(2,1)S(1)} %get-tuple-element.51.refs_2_.refs_5_.refs_12_), custom_call_target="tpu_custom_call" | custom-call | flops 10737418240 | bytes 41943040 | tf_op jit(solution)/shard_map/pallas_call | solution.py:122
  89.8 2.0 %collective-permute-done.13.refs_3_.refs_4_.refs_11_ = bf16[64,2560]{1,0:T(8,128)(2,1)S(1)} collective-permute-done((bf16[64,2560]{1,0:T(8,128)(2,1)S(1)}, bf16[64,2560]{1,0:T(8,128)(2,1)S(1)}, u32[]{:S(2)}, u32[]{:S(2)}) %collective-permute-start.13) | collective-permute-done | bytes 327712 | tf_op jit(solution)/shard_map/ppermute | solution.py:467
  91.7 3.9 %collective-permute-start.15 = (bf16[192,1024]{1,0:T(8,128)(2,1)S(1)}, bf16[192,1024]{1,0:T(8,128)(2,1)S(1)}, u32[]{:S(2)}, u32[]{:S(2)}) collective-permute-start(bf16[192,1024]{1,0:T(8,128)(2,1)S(1)} %get-tuple-element.52.refs_2_), channel_id=1, source_target_pairs={{0,1},{3,2},{4,5},{7,6},{8,9},{11,10},{12,13},{15,14},{16,17},{19,... | collective-permute-start | bytes 1179656 | tf_op jit(solution)/shard_map/ppermute | solution.py:467
  95.6 4.0 %shard_map.168 = (f32[256,512]{1,0:T(8,128)S(1)}, bf16[192,512]{1,0:T(8,128)(2,1)S(1)}) custom-call(s32[13]{0:T(128)S(1)} %stack.55.place_ref, bf16[256,4096]{1,0:T(8,128)(2,1)S(1)} %copy-done.1, bf16[4096,10240]{1,0:T(8,128)(2,1)} %refs_1_.13, bf16[192,1024]{1,0:T(8,128)(2,1)S(1)} %get-tuple-element.52.refs_2_, ...), custom_call_target="tpu_custom_call" | custom-call | flops 5368709120 | bytes 20971520 | tf_op jit(solution)/shard_map/pallas_call | solution.py:122
  100.3 0.7 collective-permute-start.21
  101.0 1.3 collective-permute-start.12
  103.0 1.3 collective-permute-start.23
  104.3 4.6 %collective-permute-start.14 = (bf16[192,512]{1,0:T(8,128)(2,1)S(1)}, bf16[192,512]{1,0:T(8,128)(2,1)S(1)}, u32[]{:S(2)}, u32[]{:S(2)}) collective-permute-start(bf16[192,512]{1,0:T(8,128)(2,1)S(1)} %get-tuple-element.54.refs_3_), channel_id=1, source_target_pairs={{0,1},{3,2},{4,5},{7,6},{8,9},{11,10},{12,13},{15,14},{16,17},{19,... | collective-permute-start | bytes 589832 | tf_op jit(solution)/shard_map/ppermute | solution.py:467
  109.5 0.7 collective-permute-start.20
  110.2 1.9 %collective-permute-done.14.refs_1_.refs_2_ = bf16[192,512]{1,0:T(8,128)(2,1)S(1)} collective-permute-done((bf16[192,512]{1,0:T(8,128)(2,1)S(1)}, bf16[192,512]{1,0:T(8,128)(2,1)S(1)}, u32[]{:S(2)}, u32[]{:S(2)}) %collective-permute-start.14) | collective-permute-done | bytes 196640 | tf_op jit(solution)/shard_map/ppermute | solution.py:467
  112.6 1.6 %collective-permute-done.12.refs_2_.refs_7_.refs_14_ = bf16[16,11264]{1,0:T(8,128)(2,1)S(1)} collective-permute-done((bf16[16,11264]{1,0:T(8,128)(2,1)S(1)}, bf16[16,11264]{1,0:T(8,128)(2,1)S(1)}, u32[]{:S(2)}, u32[]{:S(2)}) %collective-permute-start.12) | collective-permute-done | bytes 360480 | tf_op jit(solution)/shard_map/ppermute | solution.py:467
  114.3 1.0 shard_map.173.refs_0_.refs_15_
  115.3 0.8 shard_map.174.refs_2_.refs_8_
  116.7 1.3 collective-permute-start.24
  118.0 0.7 collective-permute-start.19
  119.2 1.3 collective-permute-start.25
  121.1 1.4 %collective-permute-start.22 = (bf16[64,512]{1,0:T(8,128)(2,1)S(1)}, bf16[64,512]{1,0:T(8,128)(2,1)S(1)}, u32[]{:S(2)}, u32[]{:S(2)}) collective-permute-start(bf16[64,512]{1,0:T(8,128)(2,1)S(1)} %shard_map.177.refs_15_), channel_id=1, source_target_pairs={{2,3},{1,0},{6,7},{5,4},{10,11},{9,8},{14,15},{13,12},{18,19},{17,... | collective-permute-start | bytes 196616 | tf_op jit(solution)/shard_map/ppermute | solution.py:467
  122.6 2.9 %collective-permute-done.23.refs_4_.refs_11_ = bf16[64,4096]{1,0:T(8,128)(2,1)S(1)} collective-permute-done((bf16[64,4096]{1,0:T(8,128)(2,1)S(1)}, bf16[64,4096]{1,0:T(8,128)(2,1)S(1)}, u32[]{:S(2)}, u32[]{:S(2)}) %collective-permute-start.23) | collective-permute-done | bytes 524320 | tf_op jit(solution)/shard_map/ppermute | solution.py:467
  125.5 0.9 shard_map.178.refs_8_.refs_9_
  126.4 3.8 %collective-permute-done.24.refs_4_ = bf16[64,2048]{1,0:T(8,128)(2,1)S(1)} collective-permute-done((bf16[64,2048]{1,0:T(8,128)(2,1)S(1)}, bf16[64,2048]{1,0:T(8,128)(2,1)S(1)}, u32[]{:S(2)}, u32[]{:S(2)}) %collective-permute-start.24) | collective-permute-done | bytes 262176 | tf_op jit(solution)/shard_map/ppermute | solution.py:467
  130.2 0.7 shard_map.179.refs_8_.refs_10_
  130.9 0.6 collective-permute-done.25.refs_4_
  131.6 0.7 shard_map.180.refs_11_.refs_12_
  132.3 2.3 %shard_map.181 = f32[64,10240]{1,0:T(8,128)} custom-call(s32[13]{0:T(128)S(1)} %stack.55.place_ref, bf16[64,64]{1,0:T(8,128)(2,1)S(1)} %shard_map.173.refs_0_.refs_15_, f32[256,512]{1,0:T(8,128)S(1)} %get-tuple-element.53.refs_0_.refs_1_, bf16[192,512]{1,0:T(8,128)(2,1)S(1)} %collective-permute-done.14.refs_1_.refs_2_, ...), custom_call_target="tpu_custom_call" | custom-call | bytes 45875200 | tf_op jit(solution)/shard_map/pallas_call | solution.py:122
  (60 shorter events, 7.3 us)
Async XLA Ops:
  0.8 1.6 %copy-start = (bf16[256,4096]{1,0:T(8,128)(2,1)S(1)}, bf16[256,4096]{1,0:T(8,128)(2,1)}, u32[]{:S(2)}) copy-start(bf16[256,4096]{1,0:T(8,128)(2,1)} %refs_0_.15) | copy-start | bytes 6291460
  2.4 10.6 %copy-start.2 = (f32[1,32,10240]{2,1,0:T(8,128)S(1)}, f32[1,32,10240]{2,1,0:T(8,128)}, u32[]{:S(2)}) copy-start(f32[1,32,10240]{2,1,0:T(8,128)} %param.19) | copy-start | bytes 3932164
  2.4 10.6 %copy-start.3 = (f32[1,4096,32]{1,2,0:T(8,128)S(1)}, f32[1,4096,32]{1,2,0:T(8,128)}, u32[]{:S(2)}) copy-start(f32[1,4096,32]{1,2,0:T(8,128)} %param.18) | copy-start | bytes 1572868
  7.8 5.8 %copy-start.1 = (bf16[256,4096]{1,0:T(8,128)(2,1)S(1)}, bf16[256,4096]{1,0:T(8,128)(2,1)}, u32[]{:S(2)}) copy-start(bf16[256,4096]{1,0:T(8,128)(2,1)} %refs_0_.15) | copy-start | bytes 6291460
  7.9 30.5 %collective-permute-start.5 = (bf16[192,1024]{1,0:T(8,128)(2,1)S(1)}, bf16[192,1024]{1,0:T(8,128)(2,1)S(1)}, u32[]{:S(2)}, u32[]{:S(2)}) collective-permute-start(bf16[192,1024]{1,0:T(8,128)(2,1)S(1)} %get-tuple-element.35.refs_2_), channel_id=1, source_target_pairs={{0,1},{3,2},{4,5},{7,6},{8,9},{11,10},{12,13},{15,14},{16,17},{19,... | collective-permute-start | bytes 1179656 | tf_op jit(solution)/shard_map/ppermute | solution.py:467
  13.6 9.1 %collective-permute-start = (bf16[16,14336]{1,0:T(8,128)(2,1)S(1)}, bf16[16,14336]{1,0:T(8,128)(2,1)S(1)}, u32[]{:S(2)}, u32[]{:S(2)}) collective-permute-start(bf16[16,14336]{1,0:T(8,128)(2,1)S(1)} %shard_map.154.refs_2_), channel_id=1, source_target_pairs={{0,4},{4,0},{8,12},{12,8},{1,5},{5,1},{9,13},{13,9},{2,6},{6,2},{1... | collective-permute-start | bytes 1376264 | tf_op jit(solution)/shard_map/ppermute | solution.py:470
  21.3 17.0 %collective-permute-start.6 = (bf16[192,1536]{1,0:T(8,128)(2,1)S(1)}, bf16[192,1536]{1,0:T(8,128)(2,1)S(1)}, u32[]{:S(2)}, u32[]{:S(2)}) collective-permute-start(bf16[192,1536]{1,0:T(8,128)(2,1)S(1)} %get-tuple-element.36.refs_3_), channel_id=1, source_target_pairs={{0,1},{3,2},{4,5},{7,6},{8,9},{11,10},{12,13},{15,14},{16,17},{19,... | collective-permute-start | bytes 1769480 | tf_op jit(solution)/shard_map/ppermute | solution.py:467
  23.3 12.2 %collective-permute-start.1 = (bf16[8,14336]{1,0:T(8,128)(2,1)S(1)}, bf16[8,14336]{1,0:T(8,128)(2,1)S(1)}, u32[]{:S(2)}, u32[]{:S(2)}) collective-permute-start(bf16[8,14336]{1,0:T(8,128)(2,1)S(1)} %get-tuple-element.38), channel_id=1, source_target_pairs={{0,8},{4,12},{8,0},{12,4},{1,9},{5,13},{9,1},{13,5},{2,10},{6,14},... | collective-permute-start | bytes 688136 | tf_op jit(solution)/shard_map/ppermute | solution.py:470
  24.9 10.6 %copy-start.6 = (f32[8,10240]{1,0:T(8,128)S(1)}, f32[8,10240]{1,0:T(8,128)}, u32[]{:S(2)}) copy-start(f32[8,10240]{1,0:T(8,128)} %refs_5_.1) | copy-start | bytes 983044
  24.9 10.6 %copy-start.7 = (f32[8,10240]{1,0:T(8,128)S(1)}, f32[8,10240]{1,0:T(8,128)}, u32[]{:S(2)}) copy-start(f32[8,10240]{1,0:T(8,128)} %refs_6_.1) | copy-start | bytes 983044
  24.9 10.7 %copy-start.8 = (f32[8,10240]{1,0:T(8,128)S(1)}, f32[8,10240]{1,0:T(8,128)}, u32[]{:S(2)}) copy-start(f32[8,10240]{1,0:T(8,128)} %refs_7_.1) | copy-start | bytes 983044
  24.9 10.7 %copy-start.9 = (f32[4096,8]{0,1:T(8,128)S(1)}, f32[4096,8]{0,1:T(8,128)}, u32[]{:S(2)}) copy-start(f32[4096,8]{0,1:T(8,128)} %param.12) | copy-start | bytes 393220
  24.9 10.7 %copy-start.10 = (f32[4096,8]{0,1:T(8,128)S(1)}, f32[4096,8]{0,1:T(8,128)}, u32[]{:S(2)}) copy-start(f32[4096,8]{0,1:T(8,128)} %param.14) | copy-start | bytes 393220
  24.9 10.7 %copy-start.11 = (f32[4096,8]{0,1:T(8,128)S(1)}, f32[4096,8]{0,1:T(8,128)}, u32[]{:S(2)}) copy-start(f32[4096,8]{0,1:T(8,128)} %param.15) | copy-start | bytes 393220
  34.2 24.8 %collective-permute-start.10 = (bf16[192,2048]{1,0:T(8,128)(2,1)S(1)}, bf16[192,2048]{1,0:T(8,128)(2,1)S(1)}, u32[]{:S(2)}, u32[]{:S(2)}) collective-permute-start(bf16[192,2048]{1,0:T(8,128)(2,1)S(1)} %get-tuple-element.39.refs_8_), channel_id=1, source_target_pairs={{0,1},{3,2},{4,5},{7,6},{8,9},{11,10},{12,13},{15,14},{16,17},{19,... | collective-permute-start | bytes 2359304 | tf_op jit(solution)/shard_map/ppermute | solution.py:467
  37.4 2.3 %collective-permute-start.3 = (bf16[8,4096]{1,0:T(8,128)(2,1)S(1)}, bf16[8,4096]{1,0:T(8,128)(2,1)S(1)}, u32[]{:S(2)}, u32[]{:S(2)}) collective-permute-start(bf16[8,4096]{1,0:T(8,128)(2,1)S(1)} %get-tuple-element.41), channel_id=1, source_target_pairs={{0,4},{4,0},{8,12},{12,8},{1,5},{5,1},{9,13},{13,9},{2,6},{6,2},{1... | collective-permute-start | bytes 196616 | tf_op jit(solution)/shard_map/ppermute | solution.py:470
  37.7 19.3 %collective-permute-start.2 = (bf16[8,10240]{1,0:T(8,128)(2,1)S(1)}, bf16[8,10240]{1,0:T(8,128)(2,1)S(1)}, u32[]{:S(2)}, u32[]{:S(2)}) collective-permute-start(bf16[8,10240]{1,0:T(8,128)(2,1)S(1)} %get-tuple-element.40.refs_6_), channel_id=1, source_target_pairs={{0,0},{1,4},{2,8},{3,12},{4,1},{5,5},{6,9},{7,13},{8,2},{9,6},{10,... | collective-permute-start | bytes 491528 | tf_op jit(solution)/shard_map/ppermute | solution.py:511
  39.0 42.0 %collective-permute-start.8 = (bf16[128,2560]{1,0:T(8,128)(2,1)S(1)}, bf16[128,2560]{1,0:T(8,128)(2,1)S(1)}, u32[]{:S(2)}, u32[]{:S(2)}) collective-permute-start(bf16[128,2560]{1,0:T(8,128)(2,1)S(1)} %shard_map.159.refs_2_), channel_id=1, source_target_pairs={{1,2},{2,1},{5,6},{6,5},{9,10},{10,9},{13,14},{14,13},{17,18},{18,... | collective-permute-start | bytes 1966088 | tf_op jit(solution)/shard_map/ppermute | solution.py:467
  39.7 17.2 %collective-permute-start.4 = (bf16[16,4096]{1,0:T(8,128)(2,1)S(1)}, bf16[16,4096]{1,0:T(8,128)(2,1)S(1)}, u32[]{:S(2)}, u32[]{:S(2)}) collective-permute-start(bf16[16,4096]{1,0:T(8,128)(2,1)S(1)} %constant_dynamic-update-slice_fusion.refs_1_), channel_id=1, source_target_pairs={{0,8},{4,12},{8,0},{12,4},{1,9},{5,13},{9,1},{13,5},{2,10},{6,14},... | collective-permute-start | bytes 393224 | tf_op jit(solution)/shard_map/ppermute | solution.py:470
  52.0 26.9 %collective-permute-start.9 = (bf16[192,2048]{1,0:T(8,128)(2,1)S(1)}, bf16[192,2048]{1,0:T(8,128)(2,1)S(1)}, u32[]{:S(2)}, u32[]{:S(2)}) collective-permute-start(bf16[192,2048]{1,0:T(8,128)(2,1)S(1)} %get-tuple-element.44.refs_4_), channel_id=1, source_target_pairs={{0,1},{3,2},{4,5},{7,6},{8,9},{11,10},{12,13},{15,14},{16,17},{19,... | collective-permute-start | bytes 2359304 | tf_op jit(solution)/shard_map/ppermute | solution.py:467
  58.7 24.3 %collective-permute-start.7 = (bf16[8,12288]{1,0:T(8,128)(2,1)S(1)}, bf16[8,12288]{1,0:T(8,128)(2,1)S(1)}, u32[]{:S(2)}, u32[]{:S(2)}) collective-permute-start(bf16[8,12288]{1,0:T(8,128)(2,1)S(1)} %get-tuple-element.45.refs_3_), channel_id=1, source_target_pairs={{0,1},{1,0},{2,3},{3,2},{4,5},{5,4},{6,7},{7,6},{8,9},{9,8},{10,11... | collective-permute-start | bytes 589832 | tf_op jit(solution)/shard_map/ppermute | solution.py:517
  59.6 42.7 %collective-permute-start.16 = (bf16[128,2048]{1,0:T(8,128)(2,1)S(1)}, bf16[128,2048]{1,0:T(8,128)(2,1)S(1)}, u32[]{:S(2)}, u32[]{:S(2)}) collective-permute-start(bf16[128,2048]{1,0:T(8,128)(2,1)S(1)} %shard_map.162.refs_2_), channel_id=1, source_target_pairs={{1,2},{2,1},{5,6},{6,5},{9,10},{10,9},{13,14},{14,13},{17,18},{18,... | collective-permute-start | bytes 1572872 | tf_op jit(solution)/shard_map/ppermute | solution.py:467
  70.2 29.4 %collective-permute-start.18 = (bf16[192,2048]{1,0:T(8,128)(2,1)}, bf16[192,2048]{1,0:T(8,128)(2,1)S(1)}, u32[]{:S(2)}, u32[]{:S(2)}) collective-permute-start(bf16[192,2048]{1,0:T(8,128)(2,1)} %get-tuple-element.49.refs_3_), channel_id=1, source_target_pairs={{0,1},{3,2},{4,5},{7,6},{8,9},{11,10},{12,13},{15,14},{16,17},{19,... | collective-permute-start | bytes 2359304 | tf_op jit(solution)/shard_map/ppermute | solution.py:467
  80.3 22.0 %collective-permute-start.17 = (bf16[128,2048]{1,0:T(8,128)(2,1)}, bf16[128,2048]{1,0:T(8,128)(2,1)S(1)}, u32[]{:S(2)}, u32[]{:S(2)}) collective-permute-start(bf16[128,2048]{1,0:T(8,128)(2,1)} %shard_map.164.refs_4_), channel_id=1, source_target_pairs={{1,2},{2,1},{5,6},{6,5},{9,10},{10,9},{13,14},{14,13},{17,18},{18,... | collective-permute-start | bytes 1572872 | tf_op jit(solution)/shard_map/ppermute | solution.py:467
  81.7 10.1 %collective-permute-start.13 = (bf16[64,2560]{1,0:T(8,128)(2,1)S(1)}, bf16[64,2560]{1,0:T(8,128)(2,1)S(1)}, u32[]{:S(2)}, u32[]{:S(2)}) collective-permute-start(bf16[64,2560]{1,0:T(8,128)(2,1)S(1)} %shard_map.165.refs_3_), channel_id=1, source_target_pairs={{2,3},{1,0},{6,7},{5,4},{10,11},{9,8},{14,15},{13,12},{18,19},{17,... | collective-permute-start | bytes 983048 | tf_op jit(solution)/shard_map/ppermute | solution.py:467
  83.6 17.4 %collective-permute-start.11 = (bf16[16,11264]{1,0:T(8,128)(2,1)S(1)}, bf16[16,11264]{1,0:T(8,128)(2,1)S(1)}, u32[]{:S(2)}, u32[]{:S(2)}) collective-permute-start(bf16[16,11264]{1,0:T(8,128)(2,1)S(1)} %get-tuple-element.51.refs_2_.refs_5_.refs_12_), channel_id=1, source_target_pairs={{1,2},{2,1},{5,6},{6,5},{9,10},{10,9},{13,14},{14,13},{17,18},{18,... | collective-permute-start | bytes 1081352 | tf_op jit(solution)/shard_map/ppermute | solution.py:467
  91.7 17.2 %collective-permute-start.15 = (bf16[192,1024]{1,0:T(8,128)(2,1)S(1)}, bf16[192,1024]{1,0:T(8,128)(2,1)S(1)}, u32[]{:S(2)}, u32[]{:S(2)}) collective-permute-start(bf16[192,1024]{1,0:T(8,128)(2,1)S(1)} %get-tuple-element.52.refs_2_), channel_id=1, source_target_pairs={{0,1},{3,2},{4,5},{7,6},{8,9},{11,10},{12,13},{15,14},{16,17},{19,... | collective-permute-start | bytes 1179656 | tf_op jit(solution)/shard_map/ppermute | solution.py:467
  100.3 15.7 %collective-permute-start.21 = (bf16[128,2048]{1,0:T(8,128)(2,1)S(1)}, bf16[128,2048]{1,0:T(8,128)(2,1)S(1)}, u32[]{:S(2)}, u32[]{:S(2)}) collective-permute-start(bf16[128,2048]{1,0:T(8,128)(2,1)S(1)} %shard_map.169.refs_4_), channel_id=1, source_target_pairs={{1,2},{2,1},{5,6},{6,5},{9,10},{10,9},{13,14},{14,13},{17,18},{18,... | collective-permute-start | bytes 1572872 | tf_op jit(solution)/shard_map/ppermute | solution.py:467
  101.0 13.2 %collective-permute-start.12 = (bf16[16,11264]{1,0:T(8,128)(2,1)S(1)}, bf16[16,11264]{1,0:T(8,128)(2,1)S(1)}, u32[]{:S(2)}, u32[]{:S(2)}) collective-permute-start(bf16[16,11264]{1,0:T(8,128)(2,1)S(1)} %collective-permute-done.11.refs_1_.refs_6_.refs_13_), channel_id=1, source_target_pairs={{2,3},{1,0},{6,7},{5,4},{10,11},{9,8},{14,15},{13,12},{18,19},{17,... | collective-permute-start | bytes 1081352 | tf_op jit(solution)/shard_map/ppermute | solution.py:467
  103.0 22.5 %collective-permute-start.23 = (bf16[64,4096]{1,0:T(8,128)(2,1)S(1)}, bf16[64,4096]{1,0:T(8,128)(2,1)S(1)}, u32[]{:S(2)}, u32[]{:S(2)}) collective-permute-start(bf16[64,4096]{1,0:T(8,128)(2,1)S(1)} %shard_map.170.refs_3_), channel_id=1, source_target_pairs={{2,3},{1,0},{6,7},{5,4},{10,11},{9,8},{14,15},{13,12},{18,19},{17,... | collective-permute-start | bytes 1572872 | tf_op jit(solution)/shard_map/ppermute | solution.py:467
  104.3 7.8 %collective-permute-start.14 = (bf16[192,512]{1,0:T(8,128)(2,1)S(1)}, bf16[192,512]{1,0:T(8,128)(2,1)S(1)}, u32[]{:S(2)}, u32[]{:S(2)}) collective-permute-start(bf16[192,512]{1,0:T(8,128)(2,1)S(1)} %get-tuple-element.54.refs_3_), channel_id=1, source_target_pairs={{0,1},{3,2},{4,5},{7,6},{8,9},{11,10},{12,13},{15,14},{16,17},{19,... | collective-permute-start | bytes 589832 | tf_op jit(solution)/shard_map/ppermute | solution.py:467
  109.5 9.1 %collective-permute-start.20 = (bf16[128,1024]{1,0:T(8,128)(2,1)S(1)}, bf16[128,1024]{1,0:T(8,128)(2,1)S(1)}, u32[]{:S(2)}, u32[]{:S(2)}) collective-permute-start(bf16[128,1024]{1,0:T(8,128)(2,1)S(1)} %shard_map.171.refs_3_), channel_id=1, source_target_pairs={{1,2},{2,1},{5,6},{6,5},{9,10},{10,9},{13,14},{14,13},{17,18},{18,... | collective-permute-start | bytes 786440 | tf_op jit(solution)/shard_map/ppermute | solution.py:467
  116.0 3.2 %copy-start.4 = (bf16[128,2048]{1,0:T(8,128)(2,1)}, bf16[128,2048]{1,0:T(8,128)(2,1)S(1)}, u32[]{:S(2)}) copy-start(bf16[128,2048]{1,0:T(8,128)(2,1)S(1)} %collective-permute-done.21.refs_1_.refs_3_) | copy-start | bytes 1572868
  116.7 13.5 %collective-permute-start.24 = (bf16[64,2048]{1,0:T(8,128)(2,1)S(1)}, bf16[64,2048]{1,0:T(8,128)(2,1)S(1)}, u32[]{:S(2)}, u32[]{:S(2)}) collective-permute-start(bf16[64,2048]{1,0:T(8,128)(2,1)S(1)} %shard_map.175.refs_2_), channel_id=1, source_target_pairs={{2,3},{1,0},{6,7},{5,4},{10,11},{9,8},{14,15},{13,12},{18,19},{17,... | collective-permute-start | bytes 786440 | tf_op jit(solution)/shard_map/ppermute | solution.py:467
  118.0 2.6 %collective-permute-start.19 = (bf16[128,512]{1,0:T(8,128)(2,1)S(1)}, bf16[128,512]{1,0:T(8,128)(2,1)S(1)}, u32[]{:S(2)}, u32[]{:S(2)}) collective-permute-start(bf16[128,512]{1,0:T(8,128)(2,1)S(1)} %shard_map.172.refs_3_), channel_id=1, source_target_pairs={{1,2},{2,1},{5,6},{6,5},{9,10},{10,9},{13,14},{14,13},{17,18},{18,... | collective-permute-start | bytes 393224 | tf_op jit(solution)/shard_map/ppermute | solution.py:467
  119.2 12.3 %collective-permute-start.25 = (bf16[64,1024]{1,0:T(8,128)(2,1)S(1)}, bf16[64,1024]{1,0:T(8,128)(2,1)S(1)}, u32[]{:S(2)}, u32[]{:S(2)}) collective-permute-start(bf16[64,1024]{1,0:T(8,128)(2,1)S(1)} %shard_map.176.refs_2_), channel_id=1, source_target_pairs={{2,3},{1,0},{6,7},{5,4},{10,11},{9,8},{14,15},{13,12},{18,19},{17,... | collective-permute-start | bytes 393224 | tf_op jit(solution)/shard_map/ppermute | solution.py:467
  121.1 9.0 %copy-start.5 = (bf16[128,2048]{1,0:T(8,128)(2,1)S(1)}, bf16[128,2048]{1,0:T(8,128)(2,1)}, u32[]{:S(2)}) copy-start(bf16[128,2048]{1,0:T(8,128)(2,1)} %copy-done.4) | copy-start | bytes 1572868
  121.1 11.2 %collective-permute-start.22 = (bf16[64,512]{1,0:T(8,128)(2,1)S(1)}, bf16[64,512]{1,0:T(8,128)(2,1)S(1)}, u32[]{:S(2)}, u32[]{:S(2)}) collective-permute-start(bf16[64,512]{1,0:T(8,128)(2,1)S(1)} %shard_map.177.refs_15_), channel_id=1, source_target_pairs={{2,3},{1,0},{6,7},{5,4},{10,11},{9,8},{14,15},{13,12},{18,19},{17,... | collective-permute-start | bytes 196616 | tf_op jit(solution)/shard_map/ppermute | solution.py:467

commit v5 on v4

--- a/solution.py
+++ b/solution.py
@@ -518,26 +518,25 @@
     last = second((2,), last)
     last = matmul(4, last)
     last = second((3,), last)
-    last = third((0, 1), last)
+    last = third((0, 1, 2), last)
     pair, inner = join_pair(place, turned, swapped, inner, [last])
     near_out = line(1, pair)
     last = matmul(5, pair)
-    last = matmul(6, last, thirds[0][0])
-    last = second((4,), last)
-    last = third((2, 3), last)
+    last = matmul(6, last)
+    last = second((4,), last, thirds[0][0])
     far_out = line(2, near_out)
     factors = (pair, near_out, far_out)
     last = second((5,), last)
+    last = third((3,), last)
     last = second((6,), last)
     last = spread = spread_inner(place, inner, near_out, far_out, width, share, [last])
-    last = finish((0, 1), last)
+    last = finish((0, 1, 2), last)
     last = third((4,), last)
     last = third((5,), last)
     last = third((6,), last)
-    last = finish((2, 3), last)
+    last = finish((3,), last)
     last = finish((4,), last)
-    last = finish((5,), last)
-    decoded = finish((6,), last, full_width=width, done=list(finished))
+    decoded = finish((5, 6), last, full_width=width, done=list(finished))
     return (decoded, new_in.T, new_out, first_in.T, second_in.T, first_out, second_out)
 
 

time: 135 us -> 132 us (0.978)
  waiting for transfers between devices: 12.9 us -> 8.95 us
  Pallas kernels: 70.3 us -> 68.2 us
  starting transfers between devices: 48.3 us -> 50.1 us
    ppermute x20, waiting for transfers between devices: 12.8 us -> 8.94 us  [line(): return lax.ppermute(values, 'tp', LINE[step])]
    pallas_call x29 -> x28, Pallas kernels: 70.3 us -> 68.2 us  [call(): pl.pallas_call(kernel, grid_spec=pltpu.PrefetchScalarGridSpec(num_scalar_...]
    ppermute x20, starting transfers between devices: 42.4 us -> 44.5 us  [line(): return lax.ppermute(values, 'tp', LINE[step])]
    unnamed x25 -> x37, local copies, waits for them, and re-layouts: 1.65 us -> 2.83 us
  transfers between devices with their start and end apart: 26 -> 26, of which waited for: 6 -> 3; matrix products, arithmetic and copies ran while one was open for 0% -> 0% of each run, Pallas kernels for 47% -> 46%
where the time goes in v5:
time: 132 us
  Pallas kernels  68.2 us (52%)
  starting transfers between devices  50.1 us (38%)
  waiting for transfers between devices  8.95 us (7%)
  local copies, waits for them, and re-layouts  2.92 us (2%)
  between operations  1.42 us (1%)
    pallas_call x28, Pallas kernels, call(): pl.pallas_call(kernel, grid_spec=pltpu.PrefetchScalarGridSpec(num_scalar_...  68.2 us
    ppermute x20, starting transfers between devices, line(): return lax.ppermute(values, 'tp', LINE[step])  44.5 us
    ppermute x20, waiting for transfers between devices, line(): return lax.ppermute(values, 'tp', LINE[step])  8.94 us
    ppermute x4, starting transfers between devices, chip(): return lax.ppermute(values, 'rep', [(i, i ^ bit) for i in range(4)])  4.89 us
    unnamed x37, local copies, waits for them, and re-layouts  2.83 us
  transfers between devices with their start and end apart: 26, of which 3 were waited for; matrix products, arithmetic and copies ran while one was open for 0% of the time, Pallas kernels for 46%

profile of v5, /device:TPU:0, one launch (start us, length us, event | category | flops | bytes accessed | tf_op | source)
XLA Modules:
  0.0 131.6 jit_solution(4358528349296338956)
XLA Ops:
  0.8 1.6 %copy-done = bf16[256,4096]{1,0:T(8,128)(2,1)S(1)} copy-done((bf16[256,4096]{1,0:T(8,128)(2,1)S(1)}, bf16[256,4096]{1,0:T(8,128)(2,1)}, u32[]{:S(2)}) %copy-start) | copy-done | bytes 2097176
  2.4 5.5 %shard_map.153 = (f32[256,1024]{1,0:T(8,128)S(1)}, bf16[192,1024]{1,0:T(8,128)(2,1)S(1)}) custom-call(s32[13]{0:T(128)S(1)} %stack.55.place_ref, bf16[256,4096]{1,0:T(8,128)(2,1)S(1)} %copy-done, bf16[4096,10240]{1,0:T(8,128)(2,1)} %refs_1_.13), custom_call_target="tpu_custom_call" | custom-call | flops 10737418240 | bytes 41943040 | tf_op jit(solution)/shard_map/pallas_call | solution.py:122
  7.9 5.1 %collective-permute-start.5 = (bf16[192,1024]{1,0:T(8,128)(2,1)S(1)}, bf16[192,1024]{1,0:T(8,128)(2,1)S(1)}, u32[]{:S(2)}, u32[]{:S(2)}) collective-permute-start(bf16[192,1024]{1,0:T(8,128)(2,1)S(1)} %get-tuple-element.35.refs_2_), channel_id=1, source_target_pairs={{0,1},{3,2},{4,5},{7,6},{8,9},{11,10},{12,13},{15,14},{16,17},{19,... | collective-permute-start | bytes 1179656 | tf_op jit(solution)/shard_map/ppermute | solution.py:467
  13.7 7.7 %shard_map.155 = (f32[256,1536]{1,0:T(8,128)S(1)}, bf16[192,1536]{1,0:T(8,128)(2,1)S(1)}) custom-call(s32[13]{0:T(128)S(1)} %stack.55.place_ref, bf16[256,4096]{1,0:T(8,128)(2,1)S(1)} %copy-done.1, bf16[4096,10240]{1,0:T(8,128)(2,1)} %refs_1_.13, bf16[16,14336]{1,0:T(8,128)(2,1)S(1)} %shard_map.154.refs_2_), custom_call_target="tpu_custom_call" | custom-call | flops 16106127360 | bytes 62914560 | tf_op jit(solution)/shard_map/pallas_call | solution.py:122
  21.3 1.3 %collective-permute-start.6 = (bf16[192,1536]{1,0:T(8,128)(2,1)S(1)}, bf16[192,1536]{1,0:T(8,128)(2,1)S(1)}, u32[]{:S(2)}, u32[]{:S(2)}) collective-permute-start(bf16[192,1536]{1,0:T(8,128)(2,1)S(1)} %get-tuple-element.36.refs_3_), channel_id=1, source_target_pairs={{0,1},{3,2},{4,5},{7,6},{8,9},{11,10},{12,13},{15,14},{16,17},{19,... | collective-permute-start | bytes 1769480 | tf_op jit(solution)/shard_map/ppermute | solution.py:467
  22.7 0.7 shard_map.156
  23.3 1.6 %collective-permute-start.1 = (bf16[8,14336]{1,0:T(8,128)(2,1)S(1)}, bf16[8,14336]{1,0:T(8,128)(2,1)S(1)}, u32[]{:S(2)}, u32[]{:S(2)}) collective-permute-start(bf16[8,14336]{1,0:T(8,128)(2,1)S(1)} %get-tuple-element.38), channel_id=1, source_target_pairs={{0,8},{4,12},{8,0},{12,4},{1,9},{5,13},{9,1},{13,5},{2,10},{6,14},... | collective-permute-start | bytes 688136 | tf_op jit(solution)/shard_map/ppermute | solution.py:470
  24.9 9.2 %shard_map.157 = (f32[256,2048]{1,0:T(8,128)S(1)}, bf16[192,2048]{1,0:T(8,128)(2,1)S(1)}) custom-call(s32[13]{0:T(128)S(1)} %stack.55.place_ref, bf16[256,4096]{1,0:T(8,128)(2,1)S(1)} %copy-done.1, bf16[4096,10240]{1,0:T(8,128)(2,1)} %refs_1_.13, f32[8,14336]{1,0:T(8,128)S(1)} %get-tuple-element.37.refs_2_.refs_0_), custom_call_target="tpu_custom_call" | custom-call | flops 21474836480 | bytes 83886080 | tf_op jit(solution)/shard_map/pallas_call | solution.py:122
  34.2 1.3 %collective-permute-start.9 = (bf16[192,2048]{1,0:T(8,128)(2,1)S(1)}, bf16[192,2048]{1,0:T(8,128)(2,1)S(1)}, u32[]{:S(2)}, u32[]{:S(2)}) collective-permute-start(bf16[192,2048]{1,0:T(8,128)(2,1)S(1)} %get-tuple-element.39.refs_8_), channel_id=1, source_target_pairs={{0,1},{3,2},{4,5},{7,6},{8,9},{11,10},{12,13},{15,14},{16,17},{19,... | collective-permute-start | bytes 2359304 | tf_op jit(solution)/shard_map/ppermute | solution.py:467
  35.6 1.9 %shard_map.158 = (f32[8,4096]{1,0:T(8,128)}, f32[8,4096]{1,0:T(8,128)}, f32[8,4096]{1,0:T(8,128)}, bf16[8,4096]{1,0:T(8,128)(2,1)S(1)}, f32[8,10240]{1,0:T(8,128...) custom-call(s32[13]{0:T(128)S(1)} %stack.55.place_ref, ...), custom_call_target="tpu_custom_call" | custom-call | bytes 18350080 | tf_op jit(solution)/shard_map/pallas_call | solution.py:122
  37.7 0.7 collective-permute-start.2
  38.4 0.7 shard_map.159.refs_2_
  39.3 0.7 collective-permute-start.8
  40.0 3.1 %collective-permute-start.4 = (bf16[16,4096]{1,0:T(8,128)(2,1)S(1)}, bf16[16,4096]{1,0:T(8,128)(2,1)S(1)}, u32[]{:S(2)}, u32[]{:S(2)}) collective-permute-start(bf16[16,4096]{1,0:T(8,128)(2,1)S(1)} %constant_dynamic-update-slice_fusion.refs_1_), channel_id=1, source_target_pairs={{0,8},{4,12},{8,0},{12,4},{1,9},{5,13},{9,1},{13,5},{2,10},{6,14},... | collective-permute-start | bytes 393224 | tf_op jit(solution)/shard_map/ppermute | solution.py:470
  43.1 9.2 %shard_map.160 = (f32[256,2048]{1,0:T(8,128)S(1)}, bf16[192,2048]{1,0:T(8,128)(2,1)S(1)}) custom-call(s32[13]{0:T(128)S(1)} %stack.55.place_ref, bf16[256,4096]{1,0:T(8,128)(2,1)S(1)} %copy-done.1, bf16[4096,10240]{1,0:T(8,128)(2,1)} %refs_1_.13, bf16[128,2560]{1,0:T(8,128)(2,1)S(1)} %shard_map.159.refs_2_), custom_call_target="tpu_custom_call" | custom-call | flops 21474836480 | bytes 83886080 | tf_op jit(solution)/shard_map/pallas_call | solution.py:122
  52.3 4.9 %collective-permute-start.11 = (bf16[192,2048]{1,0:T(8,128)(2,1)S(1)}, bf16[192,2048]{1,0:T(8,128)(2,1)S(1)}, u32[]{:S(2)}, u32[]{:S(2)}) collective-permute-start(bf16[192,2048]{1,0:T(8,128)(2,1)S(1)} %get-tuple-element.44.refs_4_), channel_id=1, source_target_pairs={{0,1},{3,2},{4,5},{7,6},{8,9},{11,10},{12,13},{15,14},{16,17},{19,... | collective-permute-start | bytes 2359304 | tf_op jit(solution)/shard_map/ppermute | solution.py:467
  57.2 1.7 %shard_map.161 = (f32[8,1024]{1,0:T(8,128)S(1)}, bf16[8,12288]{1,0:T(8,128)(2,1)S(1)}) custom-call(s32[13]{0:T(128)S(1)} %stack.55.place_ref, bf16[256,4096]{1,0:T(8,128)(2,1)S(1)} %copy-done.1, bf16[16,4096]{1,0:T(8,128)(2,1)S(1)} %constant_dynamic-update-slice_fusion.refs_1_, bf16[16,4096]{1,0:T(8,128)(2,1)S(1)} %collective-permute-done.4.refs_2_, ...), custom_call_target="tpu_custom_call" | custom-call | flops 335544320 | bytes 10485760 | tf_op jit(solution)/shard_map/pallas_call | solution.py:122
  59.0 0.6 shard_map.162.refs_2_
  59.6 0.7 collective-permute-start.10
  60.3 9.2 %shard_map.163 = (f32[256,2048]{1,0:T(8,128)S(1)}, bf16[192,2048]{1,0:T(8,128)(2,1)S(1)}) custom-call(s32[13]{0:T(128)S(1)} %stack.55.place_ref, bf16[256,4096]{1,0:T(8,128)(2,1)S(1)} %copy-done.1, bf16[4096,10240]{1,0:T(8,128)(2,1)} %refs_1_.13, bf16[128,2048]{1,0:T(8,128)(2,1)S(1)} %shard_map.162.refs_2_), custom_call_target="tpu_custom_call" | custom-call | flops 21474836480 | bytes 83886080 | tf_op jit(solution)/shard_map/pallas_call | solution.py:122
  69.5 8.7 %collective-permute-start.17 = (bf16[192,2048]{1,0:T(8,128)(2,1)S(1)}, bf16[192,2048]{1,0:T(8,128)(2,1)S(1)}, u32[]{:S(2)}, u32[]{:S(2)}) collective-permute-start(bf16[192,2048]{1,0:T(8,128)(2,1)S(1)} %get-tuple-element.49.refs_3_), channel_id=1, source_target_pairs={{0,1},{3,2},{4,5},{7,6},{8,9},{11,10},{12,13},{15,14},{16,17},{19,... | collective-permute-start | bytes 2359304 | tf_op jit(solution)/shard_map/ppermute | solution.py:467
  78.2 0.6 shard_map.164.refs_6_
  78.9 0.7 collective-permute-start.15
  79.6 0.6 shard_map.165.refs_3_
  80.4 1.3 collective-permute-start.18
  82.3 0.7 collective-permute-start.12
  83.0 5.5 %shard_map.167 = (f32[256,1024]{1,0:T(8,128)S(1)}, bf16[192,1024]{1,0:T(8,128)(2,1)S(1)}) custom-call(s32[13]{0:T(128)S(1)} %stack.55.place_ref, bf16[256,4096]{1,0:T(8,128)(2,1)S(1)} %copy-done.1, bf16[4096,10240]{1,0:T(8,128)(2,1)} %refs_1_.13, bf16[16,11264]{1,0:T(8,128)(2,1)S(1)} %get-tuple-element.51.refs_2_.refs_5_.refs_12_.refs_19_), custom_call_target="tpu_custom_call" | custom-call | flops 10737418240 | bytes 41943040 | tf_op jit(solution)/shard_map/pallas_call | solution.py:122
  88.5 5.8 %collective-permute-start.16 = (bf16[192,1024]{1,0:T(8,128)(2,1)S(1)}, bf16[192,1024]{1,0:T(8,128)(2,1)S(1)}, u32[]{:S(2)}, u32[]{:S(2)}) collective-permute-start(bf16[192,1024]{1,0:T(8,128)(2,1)S(1)} %get-tuple-element.52.refs_2_), channel_id=1, source_target_pairs={{0,1},{3,2},{4,5},{7,6},{8,9},{11,10},{12,13},{15,14},{16,17},{19,... | collective-permute-start | bytes 1179656 | tf_op jit(solution)/shard_map/ppermute | solution.py:467
  94.3 4.0 %shard_map.168 = (f32[256,512]{1,0:T(8,128)S(1)}, bf16[192,512]{1,0:T(8,128)(2,1)S(1)}) custom-call(s32[13]{0:T(128)S(1)} %stack.55.place_ref, bf16[256,4096]{1,0:T(8,128)(2,1)S(1)} %copy-done.1, bf16[4096,10240]{1,0:T(8,128)(2,1)} %refs_1_.13, bf16[192,1024]{1,0:T(8,128)(2,1)S(1)} %get-tuple-element.52.refs_2_), custom_call_target="tpu_custom_call" | custom-call | flops 5368709120 | bytes 20971520 | tf_op jit(solution)/shard_map/pallas_call | solution.py:122
  98.4 0.6 shard_map.169.refs_3_
  99.0 0.7 collective-permute-start.20
  99.7 1.3 collective-permute-start.13
  101.0 4.6 %collective-permute-start.14 = (bf16[192,512]{1,0:T(8,128)(2,1)S(1)}, bf16[192,512]{1,0:T(8,128)(2,1)S(1)}, u32[]{:S(2)}, u32[]{:S(2)}) collective-permute-start(bf16[192,512]{1,0:T(8,128)(2,1)S(1)} %get-tuple-element.54.refs_3_), channel_id=1, source_target_pairs={{0,1},{3,2},{4,5},{7,6},{8,9},{11,10},{12,13},{15,14},{16,17},{19,... | collective-permute-start | bytes 589832 | tf_op jit(solution)/shard_map/ppermute | solution.py:467
  106.3 0.8 collective-permute-start.19
  107.7 0.8 copy-done.8
  108.5 1.3 collective-permute-start.24
  110.4 1.3 collective-permute-done.13.refs_2_.refs_7_.refs_14_.refs_21_
  111.6 1.0 shard_map.173.refs_0_.refs_22_
  112.7 0.9 shard_map.174.refs_2_.refs_15_
  114.2 1.4 %collective-permute-start.25 = (bf16[64,2048]{1,0:T(8,128)(2,1)S(1)}, bf16[64,2048]{1,0:T(8,128)(2,1)S(1)}, u32[]{:S(2)}, u32[]{:S(2)}) collective-permute-start(bf16[64,2048]{1,0:T(8,128)(2,1)S(1)} %shard_map.175.refs_2_), channel_id=1, source_target_pairs={{2,3},{1,0},{6,7},{5,4},{10,11},{9,8},{14,15},{13,12},{18,19},{17,... | collective-permute-start | bytes 786440 | tf_op jit(solution)/shard_map/ppermute | solution.py:467
  115.6 0.7 collective-permute-start.22
  116.9 1.3 collective-permute-start.21
  118.8 1.3 collective-permute-start.23
  120.1 0.7 shard_map.178.refs_8_.refs_16_
  120.9 4.6 %collective-permute-done.25.refs_4_ = bf16[64,2048]{1,0:T(8,128)(2,1)S(1)} collective-permute-done((bf16[64,2048]{1,0:T(8,128)(2,1)S(1)}, bf16[64,2048]{1,0:T(8,128)(2,1)S(1)}, u32[]{:S(2)}, u32[]{:S(2)}) %collective-permute-start.25) | collective-permute-done | bytes 262176 | tf_op jit(solution)/shard_map/ppermute | solution.py:467
  125.4 0.8 shard_map.179.refs_17_.refs_18_
  126.2 3.0 %collective-permute-done.23.refs_11_ = bf16[64,512]{1,0:T(8,128)(2,1)S(1)} collective-permute-done((bf16[64,512]{1,0:T(8,128)(2,1)S(1)}, bf16[64,512]{1,0:T(8,128)(2,1)S(1)}, u32[]{:S(2)}, u32[]{:S(2)}) %collective-permute-start.23) | collective-permute-done | bytes 65568 | tf_op jit(solution)/shard_map/ppermute | solution.py:467
  129.2 2.3 %shard_map.180 = f32[64,10240]{1,0:T(8,128)} custom-call(s32[13]{0:T(128)S(1)} %stack.55.place_ref, bf16[64,64]{1,0:T(8,128)(2,1)S(1)} %shard_map.173.refs_0_.refs_22_, f32[256,1024]{1,0:T(8,128)S(1)} %get-tuple-element.55.refs_0_.refs_1_, bf16[192,1024]{1,0:T(8,128)(2,1)S(1)} %collective-permute-done.16.refs_1_.refs_2_, ...), custom_call_target="tpu_custom_call" | custom-call | bytes 45875200 | tf_op jit(solution)/shard_map/pallas_call | solution.py:122
  (71 shorter events, 5.6 us)
Async XLA Ops:
  0.8 1.6 %copy-start = (bf16[256,4096]{1,0:T(8,128)(2,1)S(1)}, bf16[256,4096]{1,0:T(8,128)(2,1)}, u32[]{:S(2)}) copy-start(bf16[256,4096]{1,0:T(8,128)(2,1)} %refs_0_.15) | copy-start | bytes 6291460
  2.4 10.6 %copy-start.4 = (f32[1,32,10240]{2,1,0:T(8,128)S(1)}, f32[1,32,10240]{2,1,0:T(8,128)}, u32[]{:S(2)}) copy-start(f32[1,32,10240]{2,1,0:T(8,128)} %param.19) | copy-start | bytes 3932164
  2.4 10.6 %copy-start.7 = (f32[1,4096,32]{1,2,0:T(8,128)S(1)}, f32[1,4096,32]{1,2,0:T(8,128)}, u32[]{:S(2)}) copy-start(f32[1,4096,32]{1,2,0:T(8,128)} %param.18) | copy-start | bytes 1572868
  7.8 5.8 %copy-start.1 = (bf16[256,4096]{1,0:T(8,128)(2,1)S(1)}, bf16[256,4096]{1,0:T(8,128)(2,1)}, u32[]{:S(2)}) copy-start(bf16[256,4096]{1,0:T(8,128)(2,1)} %refs_0_.15) | copy-start | bytes 6291460
  7.9 30.5 %collective-permute-start.5 = (bf16[192,1024]{1,0:T(8,128)(2,1)S(1)}, bf16[192,1024]{1,0:T(8,128)(2,1)S(1)}, u32[]{:S(2)}, u32[]{:S(2)}) collective-permute-start(bf16[192,1024]{1,0:T(8,128)(2,1)S(1)} %get-tuple-element.35.refs_2_), channel_id=1, source_target_pairs={{0,1},{3,2},{4,5},{7,6},{8,9},{11,10},{12,13},{15,14},{16,17},{19,... | collective-permute-start | bytes 1179656 | tf_op jit(solution)/shard_map/ppermute | solution.py:467
  13.6 9.1 %collective-permute-start = (bf16[16,14336]{1,0:T(8,128)(2,1)S(1)}, bf16[16,14336]{1,0:T(8,128)(2,1)S(1)}, u32[]{:S(2)}, u32[]{:S(2)}) collective-permute-start(bf16[16,14336]{1,0:T(8,128)(2,1)S(1)} %shard_map.154.refs_2_), channel_id=1, source_target_pairs={{0,4},{4,0},{8,12},{12,8},{1,5},{5,1},{9,13},{13,9},{2,6},{6,2},{1... | collective-permute-start | bytes 1376264 | tf_op jit(solution)/shard_map/ppermute | solution.py:470
  21.3 17.0 %collective-permute-start.6 = (bf16[192,1536]{1,0:T(8,128)(2,1)S(1)}, bf16[192,1536]{1,0:T(8,128)(2,1)S(1)}, u32[]{:S(2)}, u32[]{:S(2)}) collective-permute-start(bf16[192,1536]{1,0:T(8,128)(2,1)S(1)} %get-tuple-element.36.refs_3_), channel_id=1, source_target_pairs={{0,1},{3,2},{4,5},{7,6},{8,9},{11,10},{12,13},{15,14},{16,17},{19,... | collective-permute-start | bytes 1769480 | tf_op jit(solution)/shard_map/ppermute | solution.py:467
  23.3 12.2 %collective-permute-start.1 = (bf16[8,14336]{1,0:T(8,128)(2,1)S(1)}, bf16[8,14336]{1,0:T(8,128)(2,1)S(1)}, u32[]{:S(2)}, u32[]{:S(2)}) collective-permute-start(bf16[8,14336]{1,0:T(8,128)(2,1)S(1)} %get-tuple-element.38), channel_id=1, source_target_pairs={{0,8},{4,12},{8,0},{12,4},{1,9},{5,13},{9,1},{13,5},{2,10},{6,14},... | collective-permute-start | bytes 688136 | tf_op jit(solution)/shard_map/ppermute | solution.py:470
  24.9 10.6 %copy-start.12 = (f32[8,10240]{1,0:T(8,128)S(1)}, f32[8,10240]{1,0:T(8,128)}, u32[]{:S(2)}) copy-start(f32[8,10240]{1,0:T(8,128)} %refs_5_.1) | copy-start | bytes 983044
  24.9 10.6 %copy-start.13 = (f32[8,10240]{1,0:T(8,128)S(1)}, f32[8,10240]{1,0:T(8,128)}, u32[]{:S(2)}) copy-start(f32[8,10240]{1,0:T(8,128)} %refs_6_.1) | copy-start | bytes 983044
  24.9 10.7 %copy-start.14 = (f32[8,10240]{1,0:T(8,128)S(1)}, f32[8,10240]{1,0:T(8,128)}, u32[]{:S(2)}) copy-start(f32[8,10240]{1,0:T(8,128)} %refs_7_.1) | copy-start | bytes 983044
  24.9 10.7 %copy-start.15 = (f32[4096,8]{0,1:T(8,128)S(1)}, f32[4096,8]{0,1:T(8,128)}, u32[]{:S(2)}) copy-start(f32[4096,8]{0,1:T(8,128)} %param.12) | copy-start | bytes 393220
  24.9 10.7 %copy-start.16 = (f32[4096,8]{0,1:T(8,128)S(1)}, f32[4096,8]{0,1:T(8,128)}, u32[]{:S(2)}) copy-start(f32[4096,8]{0,1:T(8,128)} %param.14) | copy-start | bytes 393220
  24.9 10.7 %copy-start.17 = (f32[4096,8]{0,1:T(8,128)S(1)}, f32[4096,8]{0,1:T(8,128)}, u32[]{:S(2)}) copy-start(f32[4096,8]{0,1:T(8,128)} %param.15) | copy-start | bytes 393220
  34.2 24.8 %collective-permute-start.9 = (bf16[192,2048]{1,0:T(8,128)(2,1)S(1)}, bf16[192,2048]{1,0:T(8,128)(2,1)S(1)}, u32[]{:S(2)}, u32[]{:S(2)}) collective-permute-start(bf16[192,2048]{1,0:T(8,128)(2,1)S(1)} %get-tuple-element.39.refs_8_), channel_id=1, source_target_pairs={{0,1},{3,2},{4,5},{7,6},{8,9},{11,10},{12,13},{15,14},{16,17},{19,... | collective-permute-start | bytes 2359304 | tf_op jit(solution)/shard_map/ppermute | solution.py:467
  37.4 2.5 %collective-permute-start.3 = (bf16[8,4096]{1,0:T(8,128)(2,1)S(1)}, bf16[8,4096]{1,0:T(8,128)(2,1)S(1)}, u32[]{:S(2)}, u32[]{:S(2)}) collective-permute-start(bf16[8,4096]{1,0:T(8,128)(2,1)S(1)} %get-tuple-element.41), channel_id=1, source_target_pairs={{0,4},{4,0},{8,12},{12,8},{1,5},{5,1},{9,13},{13,9},{2,6},{6,2},{1... | collective-permute-start | bytes 196616 | tf_op jit(solution)/shard_map/ppermute | solution.py:470
  37.7 19.5 %collective-permute-start.2 = (bf16[8,10240]{1,0:T(8,128)(2,1)S(1)}, bf16[8,10240]{1,0:T(8,128)(2,1)S(1)}, u32[]{:S(2)}, u32[]{:S(2)}) collective-permute-start(bf16[8,10240]{1,0:T(8,128)(2,1)S(1)} %get-tuple-element.40.refs_6_), channel_id=1, source_target_pairs={{0,0},{1,4},{2,8},{3,12},{4,1},{5,5},{6,9},{7,13},{8,2},{9,6},{10,... | collective-permute-start | bytes 491528 | tf_op jit(solution)/shard_map/ppermute | solution.py:511
  38.3 0.8 copy-start.5
  38.3 0.9 copy-start.2
  39.3 40.3 %collective-permute-start.8 = (bf16[128,2560]{1,0:T(8,128)(2,1)S(1)}, bf16[128,2560]{1,0:T(8,128)(2,1)S(1)}, u32[]{:S(2)}, u32[]{:S(2)}) collective-permute-start(bf16[128,2560]{1,0:T(8,128)(2,1)S(1)} %shard_map.159.refs_2_), channel_id=1, source_target_pairs={{1,2},{2,1},{5,6},{6,5},{9,10},{10,9},{13,14},{14,13},{17,18},{18,... | collective-permute-start | bytes 1966088 | tf_op jit(solution)/shard_map/ppermute | solution.py:467
  40.0 17.2 %collective-permute-start.4 = (bf16[16,4096]{1,0:T(8,128)(2,1)S(1)}, bf16[16,4096]{1,0:T(8,128)(2,1)S(1)}, u32[]{:S(2)}, u32[]{:S(2)}) collective-permute-start(bf16[16,4096]{1,0:T(8,128)(2,1)S(1)} %constant_dynamic-update-slice_fusion.refs_1_), channel_id=1, source_target_pairs={{0,8},{4,12},{8,0},{12,4},{1,9},{5,13},{9,1},{13,5},{2,10},{6,14},... | collective-permute-start | bytes 393224 | tf_op jit(solution)/shard_map/ppermute | solution.py:470
  52.3 25.9 %collective-permute-start.11 = (bf16[192,2048]{1,0:T(8,128)(2,1)S(1)}, bf16[192,2048]{1,0:T(8,128)(2,1)S(1)}, u32[]{:S(2)}, u32[]{:S(2)}) collective-permute-start(bf16[192,2048]{1,0:T(8,128)(2,1)S(1)} %get-tuple-element.44.refs_4_), channel_id=1, source_target_pairs={{0,1},{3,2},{4,5},{7,6},{8,9},{11,10},{12,13},{15,14},{16,17},{19,... | collective-permute-start | bytes 2359304 | tf_op jit(solution)/shard_map/ppermute | solution.py:467
  58.9 22.8 %collective-permute-start.7 = (bf16[8,12288]{1,0:T(8,128)(2,1)S(1)}, bf16[8,12288]{1,0:T(8,128)(2,1)S(1)}, u32[]{:S(2)}, u32[]{:S(2)}) collective-permute-start(bf16[8,12288]{1,0:T(8,128)(2,1)S(1)} %get-tuple-element.45.refs_3_), channel_id=1, source_target_pairs={{0,1},{1,0},{2,3},{3,2},{4,5},{5,4},{6,7},{7,6},{8,9},{9,8},{10,11... | collective-permute-start | bytes 589832 | tf_op jit(solution)/shard_map/ppermute | solution.py:517
  59.6 20.0 %collective-permute-start.10 = (bf16[128,2048]{1,0:T(8,128)(2,1)S(1)}, bf16[128,2048]{1,0:T(8,128)(2,1)S(1)}, u32[]{:S(2)}, u32[]{:S(2)}) collective-permute-start(bf16[128,2048]{1,0:T(8,128)(2,1)S(1)} %shard_map.162.refs_2_), channel_id=1, source_target_pairs={{1,2},{2,1},{5,6},{6,5},{9,10},{10,9},{13,14},{14,13},{17,18},{18,... | collective-permute-start | bytes 1572872 | tf_op jit(solution)/shard_map/ppermute | solution.py:467
  69.5 28.8 %collective-permute-start.17 = (bf16[192,2048]{1,0:T(8,128)(2,1)S(1)}, bf16[192,2048]{1,0:T(8,128)(2,1)S(1)}, u32[]{:S(2)}, u32[]{:S(2)}) collective-permute-start(bf16[192,2048]{1,0:T(8,128)(2,1)S(1)} %get-tuple-element.49.refs_3_), channel_id=1, source_target_pairs={{0,1},{3,2},{4,5},{7,6},{8,9},{11,10},{12,13},{15,14},{16,17},{19,... | collective-permute-start | bytes 2359304 | tf_op jit(solution)/shard_map/ppermute | solution.py:467
  78.9 28.2 %collective-permute-start.15 = (bf16[128,2048]{1,0:T(8,128)(2,1)S(1)}, bf16[128,2048]{1,0:T(8,128)(2,1)S(1)}, u32[]{:S(2)}, u32[]{:S(2)}) collective-permute-start(bf16[128,2048]{1,0:T(8,128)(2,1)S(1)} %shard_map.164.refs_6_), channel_id=1, source_target_pairs={{1,2},{2,1},{5,6},{6,5},{9,10},{10,9},{13,14},{14,13},{17,18},{18,... | collective-permute-start | bytes 1572872 | tf_op jit(solution)/shard_map/ppermute | solution.py:467
  79.6 0.8 copy-start.10
  80.4 18.0 %collective-permute-start.18 = (bf16[64,4608]{1,0:T(8,128)(2,1)S(1)}, bf16[64,4608]{1,0:T(8,128)(2,1)S(1)}, u32[]{:S(2)}, u32[]{:S(2)}) collective-permute-start(bf16[64,4608]{1,0:T(8,128)(2,1)S(1)} %shard_map.165.refs_3_), channel_id=1, source_target_pairs={{2,3},{1,0},{6,7},{5,4},{10,11},{9,8},{14,15},{13,12},{18,19},{17,... | collective-permute-start | bytes 1769480 | tf_op jit(solution)/shard_map/ppermute | solution.py:467
  82.3 17.5 %collective-permute-start.12 = (bf16[16,11264]{1,0:T(8,128)(2,1)S(1)}, bf16[16,11264]{1,0:T(8,128)(2,1)S(1)}, u32[]{:S(2)}, u32[]{:S(2)}) collective-permute-start(bf16[16,11264]{1,0:T(8,128)(2,1)S(1)} %get-tuple-element.51.refs_2_.refs_5_.refs_12_.refs_19_), channel_id=1, source_target_pairs={{1,2},{2,1},{5,6},{6,5},{9,10},{10,9},{13,14},{14,13},{17,18},{18,... | collective-permute-start | bytes 1081352 | tf_op jit(solution)/shard_map/ppermute | solution.py:467
  88.5 17.1 %collective-permute-start.16 = (bf16[192,1024]{1,0:T(8,128)(2,1)S(1)}, bf16[192,1024]{1,0:T(8,128)(2,1)S(1)}, u32[]{:S(2)}, u32[]{:S(2)}) collective-permute-start(bf16[192,1024]{1,0:T(8,128)(2,1)S(1)} %get-tuple-element.52.refs_2_), channel_id=1, source_target_pairs={{0,1},{3,2},{4,5},{7,6},{8,9},{11,10},{12,13},{15,14},{16,17},{19,... | collective-permute-start | bytes 1179656 | tf_op jit(solution)/shard_map/ppermute | solution.py:467
  99.0 14.6 %collective-permute-start.20 = (bf16[128,2048]{1,0:T(8,128)(2,1)S(1)}, bf16[128,2048]{1,0:T(8,128)(2,1)S(1)}, u32[]{:S(2)}, u32[]{:S(2)}) collective-permute-start(bf16[128,2048]{1,0:T(8,128)(2,1)S(1)} %shard_map.169.refs_3_), channel_id=1, source_target_pairs={{1,2},{2,1},{5,6},{6,5},{9,10},{10,9},{13,14},{14,13},{17,18},{18,... | collective-permute-start | bytes 1572872 | tf_op jit(solution)/shard_map/ppermute | solution.py:467
  99.7 11.9 %collective-permute-start.13 = (bf16[16,11264]{1,0:T(8,128)(2,1)S(1)}, bf16[16,11264]{1,0:T(8,128)(2,1)S(1)}, u32[]{:S(2)}, u32[]{:S(2)}) collective-permute-start(bf16[16,11264]{1,0:T(8,128)(2,1)S(1)} %collective-permute-done.12.refs_1_.refs_6_.refs_13_.refs_20_), channel_id=1, source_target_pairs={{2,3},{1,0},{6,7},{5,4},{10,11},{9,8},{14,15},{13,12},{18,19},{17,... | collective-permute-start | bytes 1081352 | tf_op jit(solution)/shard_map/ppermute | solution.py:467
  101.0 8.7 %collective-permute-start.14 = (bf16[192,512]{1,0:T(8,128)(2,1)S(1)}, bf16[192,512]{1,0:T(8,128)(2,1)S(1)}, u32[]{:S(2)}, u32[]{:S(2)}) collective-permute-start(bf16[192,512]{1,0:T(8,128)(2,1)S(1)} %get-tuple-element.54.refs_3_), channel_id=1, source_target_pairs={{0,1},{3,2},{4,5},{7,6},{8,9},{11,10},{12,13},{15,14},{16,17},{19,... | collective-permute-start | bytes 589832 | tf_op jit(solution)/shard_map/ppermute | solution.py:467
  106.2 6.4 %copy-start.3 = (bf16[192,1536]{1,0:T(8,128)(2,1)S(1)}, bf16[192,1536]{1,0:T(8,128)(2,1)}, u32[]{:S(2)}) copy-start(bf16[192,1536]{1,0:T(8,128)(2,1)} %copy-done.2) | copy-start | bytes 1769476
  106.2 6.4 %copy-start.6 = (bf16[192,1024]{1,0:T(8,128)(2,1)S(1)}, bf16[192,1024]{1,0:T(8,128)(2,1)}, u32[]{:S(2)}) copy-start(bf16[192,1024]{1,0:T(8,128)(2,1)} %copy-done.5) | copy-start | bytes 1179652
  106.2 6.4 %copy-start.11 = (bf16[128,2048]{1,0:T(8,128)(2,1)S(1)}, bf16[128,2048]{1,0:T(8,128)(2,1)}, u32[]{:S(2)}) copy-start(bf16[128,2048]{1,0:T(8,128)(2,1)} %copy-done.10) | copy-start | bytes 1572868
  106.3 10.1 %collective-permute-start.19 = (bf16[128,1024]{1,0:T(8,128)(2,1)S(1)}, bf16[128,1024]{1,0:T(8,128)(2,1)S(1)}, u32[]{:S(2)}, u32[]{:S(2)}) collective-permute-start(bf16[128,1024]{1,0:T(8,128)(2,1)S(1)} %shard_map.170.refs_2_), channel_id=1, source_target_pairs={{1,2},{2,1},{5,6},{6,5},{9,10},{10,9},{13,14},{14,13},{17,18},{18,... | collective-permute-start | bytes 786440 | tf_op jit(solution)/shard_map/ppermute | solution.py:467
  107.7 0.8 copy-start.8
  108.5 11.6 %collective-permute-start.24 = (bf16[64,2048]{1,0:T(8,128)(2,1)S(1)}, bf16[64,2048]{1,0:T(8,128)(2,1)S(1)}, u32[]{:S(2)}, u32[]{:S(2)}) collective-permute-start(bf16[64,2048]{1,0:T(8,128)(2,1)S(1)} %shard_map.171.refs_3_), channel_id=1, source_target_pairs={{2,3},{1,0},{6,7},{5,4},{10,11},{9,8},{14,15},{13,12},{18,19},{17,... | collective-permute-start | bytes 786440 | tf_op jit(solution)/shard_map/ppermute | solution.py:467
  114.2 5.9 %copy-start.9 = (bf16[128,2048]{1,0:T(8,128)(2,1)S(1)}, bf16[128,2048]{1,0:T(8,128)(2,1)}, u32[]{:S(2)}) copy-start(bf16[128,2048]{1,0:T(8,128)(2,1)} %copy-done.8) | copy-start | bytes 1572868
  114.2 11.2 %collective-permute-start.25 = (bf16[64,2048]{1,0:T(8,128)(2,1)S(1)}, bf16[64,2048]{1,0:T(8,128)(2,1)S(1)}, u32[]{:S(2)}, u32[]{:S(2)}) collective-permute-start(bf16[64,2048]{1,0:T(8,128)(2,1)S(1)} %shard_map.175.refs_2_), channel_id=1, source_target_pairs={{2,3},{1,0},{6,7},{5,4},{10,11},{9,8},{14,15},{13,12},{18,19},{17,... | collective-permute-start | bytes 786440 | tf_op jit(solution)/shard_map/ppermute | solution.py:467
  115.6 2.6 %collective-permute-start.22 = (bf16[128,512]{1,0:T(8,128)(2,1)S(1)}, bf16[128,512]{1,0:T(8,128)(2,1)S(1)}, u32[]{:S(2)}, u32[]{:S(2)}) collective-permute-start(bf16[128,512]{1,0:T(8,128)(2,1)S(1)} %shard_map.172.refs_3_), channel_id=1, source_target_pairs={{1,2},{2,1},{5,6},{6,5},{9,10},{10,9},{13,14},{14,13},{17,18},{18,... | collective-permute-start | bytes 393224 | tf_op jit(solution)/shard_map/ppermute | solution.py:467
  116.9 12.3 %collective-permute-start.21 = (bf16[64,1024]{1,0:T(8,128)(2,1)S(1)}, bf16[64,1024]{1,0:T(8,128)(2,1)S(1)}, u32[]{:S(2)}, u32[]{:S(2)}) collective-permute-start(bf16[64,1024]{1,0:T(8,128)(2,1)S(1)} %shard_map.176.refs_2_), channel_id=1, source_target_pairs={{2,3},{1,0},{6,7},{5,4},{10,11},{9,8},{14,15},{13,12},{18,19},{17,... | collective-permute-start | bytes 393224 | tf_op jit(solution)/shard_map/ppermute | solution.py:467
  118.8 10.5 %collective-permute-start.23 = (bf16[64,512]{1,0:T(8,128)(2,1)S(1)}, bf16[64,512]{1,0:T(8,128)(2,1)S(1)}, u32[]{:S(2)}, u32[]{:S(2)}) collective-permute-start(bf16[64,512]{1,0:T(8,128)(2,1)S(1)} %shard_map.177.refs_8_), channel_id=1, source_target_pairs={{2,3},{1,0},{6,7},{5,4},{10,11},{9,8},{14,15},{13,12},{18,19},{17,... | collective-permute-start | bytes 196616 | tf_op jit(solution)/shard_map/ppermute | solution.py:467

commit v6 on v5

--- a/solution.py
+++ b/solution.py
@@ -522,18 +522,17 @@
     pair, inner = join_pair(place, turned, swapped, inner, [last])
     near_out = line(1, pair)
     last = matmul(5, pair)
+    last = third((3,), last)
+    last = second((4,), last, thirds[0][0])
     last = matmul(6, last)
-    last = second((4,), last, thirds[0][0])
     far_out = line(2, near_out)
     factors = (pair, near_out, far_out)
-    last = second((5,), last)
-    last = third((3,), last)
+    last = second((5,), last, thirds[3][0])
     last = second((6,), last)
+    last = third((4,), last)
+    last = third((5, 6), last)
     last = spread = spread_inner(place, inner, near_out, far_out, width, share, [last])
     last = finish((0, 1, 2), last)
-    last = third((4,), last)
-    last = third((5,), last)
-    last = third((6,), last)
     last = finish((3,), last)
     last = finish((4,), last)
     decoded = finish((5, 6), last, full_width=width, done=list(finished))

time: 132 us -> 134 us (1.015)
  waiting for transfers between devices: 8.95 us -> 10.5 us
    ppermute x20 -> x19, waiting for transfers between devices: 8.94 us -> 10.5 us  [line(): return lax.ppermute(values, 'tp', LINE[step])]
    ppermute x20 -> x19, starting transfers between devices: 44.5 us -> 45.6 us  [line(): return lax.ppermute(values, 'tp', LINE[step])]
    pallas_call x28 -> x27, Pallas kernels: 68.2 us -> 67.6 us  [call(): pl.pallas_call(kernel, grid_spec=pltpu.PrefetchScalarGridSpec(num_scalar_...]
    unnamed x37 -> x41, local copies, waits for them, and re-layouts: 2.83 us -> 2.8 us
  transfers between devices with their start and end apart: 26 -> 25, of which waited for: 3 -> 5; matrix products, arithmetic and copies ran while one was open for 0% -> 0% of each run, Pallas kernels for 46% -> 45%
where the time goes in v6:
time: 134 us
  Pallas kernels  67.6 us (50%)
  starting transfers between devices  51.2 us (38%)
  waiting for transfers between devices  10.5 us (8%)
  local copies, waits for them, and re-layouts  2.89 us (2%)
  between operations  1.39 us (1%)
    pallas_call x27, Pallas kernels, call(): pl.pallas_call(kernel, grid_spec=pltpu.PrefetchScalarGridSpec(num_scalar_...  67.6 us
    ppermute x19, starting transfers between devices, line(): return lax.ppermute(values, 'tp', LINE[step])  45.6 us
    ppermute x19, waiting for transfers between devices, line(): return lax.ppermute(values, 'tp', LINE[step])  10.5 us
    ppermute x4, starting transfers between devices, chip(): return lax.ppermute(values, 'rep', [(i, i ^ bit) for i in range(4)])  4.89 us
    unnamed x41, local copies, waits for them, and re-layouts  2.8 us
  transfers between devices with their start and end apart: 25, of which 5 were waited for; matrix products, arithmetic and copies ran while one was open for 0% of the time, Pallas kernels for 45%

profile of v6, /device:TPU:0, one launch (start us, length us, event | category | flops | bytes accessed | tf_op | source)
XLA Modules:
  0.0 133.6 jit_solution(17907227743116672705)
XLA Ops:
  0.8 1.6 %copy-done = bf16[256,4096]{1,0:T(8,128)(2,1)S(1)} copy-done((bf16[256,4096]{1,0:T(8,128)(2,1)S(1)}, bf16[256,4096]{1,0:T(8,128)(2,1)}, u32[]{:S(2)}) %copy-start) | copy-done | bytes 2097176
  2.4 5.5 %shard_map.153 = (f32[256,1024]{1,0:T(8,128)S(1)}, bf16[192,1024]{1,0:T(8,128)(2,1)S(1)}) custom-call(s32[13]{0:T(128)S(1)} %stack.55.place_ref, bf16[256,4096]{1,0:T(8,128)(2,1)S(1)} %copy-done, bf16[4096,10240]{1,0:T(8,128)(2,1)} %refs_1_.13), custom_call_target="tpu_custom_call" | custom-call | flops 10737418240 | bytes 41943040 | tf_op jit(solution)/shard_map/pallas_call | solution.py:122
  7.9 5.1 %collective-permute-start.5 = (bf16[192,1024]{1,0:T(8,128)(2,1)S(1)}, bf16[192,1024]{1,0:T(8,128)(2,1)S(1)}, u32[]{:S(2)}, u32[]{:S(2)}) collective-permute-start(bf16[192,1024]{1,0:T(8,128)(2,1)S(1)} %get-tuple-element.35.refs_2_), channel_id=1, source_target_pairs={{0,1},{3,2},{4,5},{7,6},{8,9},{11,10},{12,13},{15,14},{16,17},{19,... | collective-permute-start | bytes 1179656 | tf_op jit(solution)/shard_map/ppermute | solution.py:467
  13.7 7.7 %shard_map.155 = (f32[256,1536]{1,0:T(8,128)S(1)}, bf16[192,1536]{1,0:T(8,128)(2,1)S(1)}) custom-call(s32[13]{0:T(128)S(1)} %stack.55.place_ref, bf16[256,4096]{1,0:T(8,128)(2,1)S(1)} %copy-done.1, bf16[4096,10240]{1,0:T(8,128)(2,1)} %refs_1_.13, bf16[16,14336]{1,0:T(8,128)(2,1)S(1)} %shard_map.154.refs_2_), custom_call_target="tpu_custom_call" | custom-call | flops 16106127360 | bytes 62914560 | tf_op jit(solution)/shard_map/pallas_call | solution.py:122
  21.3 1.3 collective-permute-start.6
  22.7 0.7 shard_map.156
  23.3 1.6 %collective-permute-start.1 = (bf16[8,14336]{1,0:T(8,128)(2,1)S(1)}, bf16[8,14336]{1,0:T(8,128)(2,1)S(1)}, u32[]{:S(2)}, u32[]{:S(2)}) collective-permute-start(bf16[8,14336]{1,0:T(8,128)(2,1)S(1)} %get-tuple-element.38), channel_id=1, source_target_pairs={{0,8},{4,12},{8,0},{12,4},{1,9},{5,13},{9,1},{13,5},{2,10},{6,14},... | collective-permute-start | bytes 688136 | tf_op jit(solution)/shard_map/ppermute | solution.py:470
  24.9 9.2 %shard_map.157 = (f32[256,2048]{1,0:T(8,128)S(1)}, bf16[192,2048]{1,0:T(8,128)(2,1)S(1)}) custom-call(s32[13]{0:T(128)S(1)} %stack.55.place_ref, bf16[256,4096]{1,0:T(8,128)(2,1)S(1)} %copy-done.1, bf16[4096,10240]{1,0:T(8,128)(2,1)} %refs_1_.13, f32[8,14336]{1,0:T(8,128)S(1)} %get-tuple-element.37.refs_2_.refs_0_), custom_call_target="tpu_custom_call" | custom-call | flops 21474836480 | bytes 83886080 | tf_op jit(solution)/shard_map/pallas_call | solution.py:122
  34.2 1.3 %collective-permute-start.9 = (bf16[192,2048]{1,0:T(8,128)(2,1)S(1)}, bf16[192,2048]{1,0:T(8,128)(2,1)S(1)}, u32[]{:S(2)}, u32[]{:S(2)}) collective-permute-start(bf16[192,2048]{1,0:T(8,128)(2,1)S(1)} %get-tuple-element.39.refs_8_), channel_id=1, source_target_pairs={{0,1},{3,2},{4,5},{7,6},{8,9},{11,10},{12,13},{15,14},{16,17},{19,... | collective-permute-start | bytes 2359304 | tf_op jit(solution)/shard_map/ppermute | solution.py:467
  35.6 1.9 %shard_map.158 = (f32[8,4096]{1,0:T(8,128)}, f32[8,4096]{1,0:T(8,128)}, f32[8,4096]{1,0:T(8,128)}, bf16[8,4096]{1,0:T(8,128)(2,1)S(1)}, f32[8,10240]{1,0:T(8,128...) custom-call(s32[13]{0:T(128)S(1)} %stack.55.place_ref, ...), custom_call_target="tpu_custom_call" | custom-call | bytes 18350080 | tf_op jit(solution)/shard_map/pallas_call | solution.py:122
  37.7 0.7 collective-permute-start.2
  38.4 0.7 shard_map.159.refs_2_
  39.3 0.7 collective-permute-start.8
  40.0 3.1 %collective-permute-start.4 = (bf16[16,4096]{1,0:T(8,128)(2,1)S(1)}, bf16[16,4096]{1,0:T(8,128)(2,1)S(1)}, u32[]{:S(2)}, u32[]{:S(2)}) collective-permute-start(bf16[16,4096]{1,0:T(8,128)(2,1)S(1)} %constant_dynamic-update-slice_fusion.refs_1_), channel_id=1, source_target_pairs={{0,8},{4,12},{8,0},{12,4},{1,9},{5,13},{9,1},{13,5},{2,10},{6,14},... | collective-permute-start | bytes 393224 | tf_op jit(solution)/shard_map/ppermute | solution.py:470
  43.1 9.2 %shard_map.160 = (f32[256,2048]{1,0:T(8,128)S(1)}, bf16[192,2048]{1,0:T(8,128)(2,1)S(1)}) custom-call(s32[13]{0:T(128)S(1)} %stack.55.place_ref, bf16[256,4096]{1,0:T(8,128)(2,1)S(1)} %copy-done.1, bf16[4096,10240]{1,0:T(8,128)(2,1)} %refs_1_.13, bf16[128,2560]{1,0:T(8,128)(2,1)S(1)} %shard_map.159.refs_2_), custom_call_target="tpu_custom_call" | custom-call | flops 21474836480 | bytes 83886080 | tf_op jit(solution)/shard_map/pallas_call | solution.py:122
  52.3 4.9 %collective-permute-start.11 = (bf16[192,2048]{1,0:T(8,128)(2,1)S(1)}, bf16[192,2048]{1,0:T(8,128)(2,1)S(1)}, u32[]{:S(2)}, u32[]{:S(2)}) collective-permute-start(bf16[192,2048]{1,0:T(8,128)(2,1)S(1)} %get-tuple-element.44.refs_4_), channel_id=1, source_target_pairs={{0,1},{3,2},{4,5},{7,6},{8,9},{11,10},{12,13},{15,14},{16,17},{19,... | collective-permute-start | bytes 2359304 | tf_op jit(solution)/shard_map/ppermute | solution.py:467
  57.2 1.7 %shard_map.161 = (f32[8,1024]{1,0:T(8,128)S(1)}, bf16[8,12288]{1,0:T(8,128)(2,1)S(1)}) custom-call(s32[13]{0:T(128)S(1)} %stack.55.place_ref, bf16[256,4096]{1,0:T(8,128)(2,1)S(1)} %copy-done.1, bf16[16,4096]{1,0:T(8,128)(2,1)S(1)} %constant_dynamic-update-slice_fusion.refs_1_, bf16[16,4096]{1,0:T(8,128)(2,1)S(1)} %collective-permute-done.4.refs_2_, ...), custom_call_target="tpu_custom_call" | custom-call | flops 335544320 | bytes 10485760 | tf_op jit(solution)/shard_map/pallas_call | solution.py:122
  59.0 0.6 shard_map.162.refs_2_
  59.6 0.7 collective-permute-start.10
  60.3 9.2 %shard_map.163 = (f32[256,2048]{1,0:T(8,128)S(1)}, bf16[192,2048]{1,0:T(8,128)(2,1)S(1)}) custom-call(s32[13]{0:T(128)S(1)} %stack.55.place_ref, bf16[256,4096]{1,0:T(8,128)(2,1)S(1)} %copy-done.1, bf16[4096,10240]{1,0:T(8,128)(2,1)} %refs_1_.13, bf16[128,2048]{1,0:T(8,128)(2,1)S(1)} %shard_map.162.refs_2_), custom_call_target="tpu_custom_call" | custom-call | flops 21474836480 | bytes 83886080 | tf_op jit(solution)/shard_map/pallas_call | solution.py:122
  69.5 8.7 %collective-permute-start.15 = (bf16[192,2048]{1,0:T(8,128)(2,1)S(1)}, bf16[192,2048]{1,0:T(8,128)(2,1)S(1)}, u32[]{:S(2)}, u32[]{:S(2)}) collective-permute-start(bf16[192,2048]{1,0:T(8,128)(2,1)S(1)} %get-tuple-element.49.refs_3_), channel_id=1, source_target_pairs={{0,1},{3,2},{4,5},{7,6},{8,9},{11,10},{12,13},{15,14},{16,17},{19,... | collective-permute-start | bytes 2359304 | tf_op jit(solution)/shard_map/ppermute | solution.py:467
  78.2 0.6 shard_map.164.refs_6_
  78.9 0.7 collective-permute-start.16
  79.6 0.6 shard_map.165.refs_3_
  80.2 0.8 copy-done.12
  81.0 1.3 collective-permute-start.17
  82.9 0.7 collective-permute-start.12
  83.6 5.5 %shard_map.167 = (f32[256,1024]{1,0:T(8,128)S(1)}, bf16[192,1024]{1,0:T(8,128)(2,1)S(1)}) custom-call(s32[13]{0:T(128)S(1)} %stack.55.place_ref, bf16[256,4096]{1,0:T(8,128)(2,1)S(1)} %copy-done.1, bf16[4096,10240]{1,0:T(8,128)(2,1)} %refs_1_.13, bf16[16,11264]{1,0:T(8,128)(2,1)S(1)} %get-tuple-element.51.refs_2_.refs_5_.refs_12_.refs_19_), custom_call_target="tpu_custom_call" | custom-call | flops 10737418240 | bytes 41943040 | tf_op jit(solution)/shard_map/pallas_call | solution.py:122
  89.1 5.9 %collective-permute-start.14 = (bf16[192,1024]{1,0:T(8,128)(2,1)S(1)}, bf16[192,1024]{1,0:T(8,128)(2,1)S(1)}, u32[]{:S(2)}, u32[]{:S(2)}) collective-permute-start(bf16[192,1024]{1,0:T(8,128)(2,1)S(1)} %get-tuple-element.53.refs_2_), channel_id=1, source_target_pairs={{0,1},{3,2},{4,5},{7,6},{8,9},{11,10},{12,13},{15,14},{16,17},{19,... | collective-permute-start | bytes 1179656 | tf_op jit(solution)/shard_map/ppermute | solution.py:467
  95.6 1.3 collective-permute-start.18
  96.9 0.7 collective-permute-done.17.refs_4_.refs_11_.refs_18_
  97.6 0.6 shard_map.169.refs_2_
  98.3 0.7 collective-permute-start.22
  99.0 4.0 %shard_map.170 = (f32[256,512]{1,0:T(8,128)S(1)}, bf16[192,512]{1,0:T(8,128)(2,1)S(1)}) custom-call(s32[13]{0:T(128)S(1)} %stack.55.place_ref, bf16[256,4096]{1,0:T(8,128)(2,1)S(1)} %copy-done.1, bf16[4096,10240]{1,0:T(8,128)(2,1)} %refs_1_.13, bf16[128,2048]{1,0:T(8,128)(2,1)S(1)} %shard_map.169.refs_2_), custom_call_target="tpu_custom_call" | custom-call | flops 5368709120 | bytes 20971520 | tf_op jit(solution)/shard_map/pallas_call | solution.py:122
  103.0 7.1 %collective-permute-start.20 = (bf16[192,512]{1,0:T(8,128)(2,1)S(1)}, bf16[192,512]{1,0:T(8,128)(2,1)S(1)}, u32[]{:S(2)}, u32[]{:S(2)}) collective-permute-start(bf16[192,512]{1,0:T(8,128)(2,1)S(1)} %get-tuple-element.55.refs_3_), channel_id=1, source_target_pairs={{0,1},{3,2},{4,5},{7,6},{8,9},{11,10},{12,13},{15,14},{16,17},{19,... | collective-permute-start | bytes 589832 | tf_op jit(solution)/shard_map/ppermute | solution.py:467
  110.7 0.7 collective-permute-start.19
  111.4 1.3 collective-permute-start.13
  113.8 0.7 collective-permute-start.21
  115.2 1.4 %collective-permute-start.24 = (bf16[64,2048]{1,0:T(8,128)(2,1)S(1)}, bf16[64,2048]{1,0:T(8,128)(2,1)S(1)}, u32[]{:S(2)}, u32[]{:S(2)}) collective-permute-start(bf16[64,2048]{1,0:T(8,128)(2,1)S(1)} %shard_map.173.refs_4_), channel_id=1, source_target_pairs={{2,3},{1,0},{6,7},{5,4},{10,11},{9,8},{14,15},{13,12},{18,19},{17,... | collective-permute-start | bytes 786440 | tf_op jit(solution)/shard_map/ppermute | solution.py:467
  117.2 1.3 collective-permute-start.23
  118.5 5.8 %collective-permute-done.13.refs_2_.refs_7_.refs_14_.refs_21_ = bf16[16,11264]{1,0:T(8,128)(2,1)S(1)} collective-permute-done((bf16[16,11264]{1,0:T(8,128)(2,1)S(1)}, bf16[16,11264]{1,0:T(8,128)(2,1)S(1)}, u32[]{:S(2)}, u32[]{:S(2)}) %collective-permute-start.13) | collective-permute-done | bytes 360480 | tf_op jit(solution)/shard_map/ppermute | solution.py:467
  124.3 1.0 shard_map.175.refs_0_.refs_22_
  125.4 0.9 shard_map.176.refs_8_.refs_15_
  126.4 0.8 shard_map.177.refs_8_.refs_16_
  127.2 2.0 %collective-permute-done.24.refs_4_ = bf16[64,2048]{1,0:T(8,128)(2,1)S(1)} collective-permute-done((bf16[64,2048]{1,0:T(8,128)(2,1)S(1)}, bf16[64,2048]{1,0:T(8,128)(2,1)S(1)}, u32[]{:S(2)}, u32[]{:S(2)}) %collective-permute-start.24) | collective-permute-done | bytes 262176 | tf_op jit(solution)/shard_map/ppermute | solution.py:467
  129.2 0.8 shard_map.178.refs_17_.refs_18_
  129.9 1.3 %collective-permute-done.23.refs_4_.refs_11_ = bf16[64,1536]{1,0:T(8,128)(2,1)S(1)} collective-permute-done((bf16[64,1536]{1,0:T(8,128)(2,1)S(1)}, bf16[64,1536]{1,0:T(8,128)(2,1)S(1)}, u32[]{:S(2)}, u32[]{:S(2)}) %collective-permute-start.23) | collective-permute-done | bytes 196640 | tf_op jit(solution)/shard_map/ppermute | solution.py:467
  131.3 2.3 %shard_map.179 = f32[64,10240]{1,0:T(8,128)} custom-call(s32[13]{0:T(128)S(1)} %stack.55.place_ref, bf16[64,64]{1,0:T(8,128)(2,1)S(1)} %shard_map.175.refs_0_.refs_22_, f32[256,1024]{1,0:T(8,128)S(1)} %get-tuple-element.52.refs_0_.refs_1_, bf16[192,1024]{1,0:T(8,128)(2,1)S(1)} %collective-permute-done.14.refs_1_.refs_2_, ...), custom_call_target="tpu_custom_call" | custom-call | bytes 45875200 | tf_op jit(solution)/shard_map/pallas_call | solution.py:122
  (72 shorter events, 5.5 us)
Async XLA Ops:
  0.8 1.6 %copy-start = (bf16[256,4096]{1,0:T(8,128)(2,1)S(1)}, bf16[256,4096]{1,0:T(8,128)(2,1)}, u32[]{:S(2)}) copy-start(bf16[256,4096]{1,0:T(8,128)(2,1)} %refs_0_.15) | copy-start | bytes 6291460
  2.4 10.6 %copy-start.4 = (f32[1,32,10240]{2,1,0:T(8,128)S(1)}, f32[1,32,10240]{2,1,0:T(8,128)}, u32[]{:S(2)}) copy-start(f32[1,32,10240]{2,1,0:T(8,128)} %param.19) | copy-start | bytes 3932164
  2.4 10.6 %copy-start.11 = (f32[1,4096,32]{1,2,0:T(8,128)S(1)}, f32[1,4096,32]{1,2,0:T(8,128)}, u32[]{:S(2)}) copy-start(f32[1,4096,32]{1,2,0:T(8,128)} %param.18) | copy-start | bytes 1572868
  7.8 5.8 %copy-start.1 = (bf16[256,4096]{1,0:T(8,128)(2,1)S(1)}, bf16[256,4096]{1,0:T(8,128)(2,1)}, u32[]{:S(2)}) copy-start(bf16[256,4096]{1,0:T(8,128)(2,1)} %refs_0_.15) | copy-start | bytes 6291460
  7.9 30.5 %collective-permute-start.5 = (bf16[192,1024]{1,0:T(8,128)(2,1)S(1)}, bf16[192,1024]{1,0:T(8,128)(2,1)S(1)}, u32[]{:S(2)}, u32[]{:S(2)}) collective-permute-start(bf16[192,1024]{1,0:T(8,128)(2,1)S(1)} %get-tuple-element.35.refs_2_), channel_id=1, source_target_pairs={{0,1},{3,2},{4,5},{7,6},{8,9},{11,10},{12,13},{15,14},{16,17},{19,... | collective-permute-start | bytes 1179656 | tf_op jit(solution)/shard_map/ppermute | solution.py:467
  13.6 9.1 %collective-permute-start = (bf16[16,14336]{1,0:T(8,128)(2,1)S(1)}, bf16[16,14336]{1,0:T(8,128)(2,1)S(1)}, u32[]{:S(2)}, u32[]{:S(2)}) collective-permute-start(bf16[16,14336]{1,0:T(8,128)(2,1)S(1)} %shard_map.154.refs_2_), channel_id=1, source_target_pairs={{0,4},{4,0},{8,12},{12,8},{1,5},{5,1},{9,13},{13,9},{2,6},{6,2},{1... | collective-permute-start | bytes 1376264 | tf_op jit(solution)/shard_map/ppermute | solution.py:470
  21.3 17.0 %collective-permute-start.6 = (bf16[192,1536]{1,0:T(8,128)(2,1)S(1)}, bf16[192,1536]{1,0:T(8,128)(2,1)S(1)}, u32[]{:S(2)}, u32[]{:S(2)}) collective-permute-start(bf16[192,1536]{1,0:T(8,128)(2,1)S(1)} %get-tuple-element.36.refs_3_), channel_id=1, source_target_pairs={{0,1},{3,2},{4,5},{7,6},{8,9},{11,10},{12,13},{15,14},{16,17},{19,... | collective-permute-start | bytes 1769480 | tf_op jit(solution)/shard_map/ppermute | solution.py:467
  23.3 12.2 %collective-permute-start.1 = (bf16[8,14336]{1,0:T(8,128)(2,1)S(1)}, bf16[8,14336]{1,0:T(8,128)(2,1)S(1)}, u32[]{:S(2)}, u32[]{:S(2)}) collective-permute-start(bf16[8,14336]{1,0:T(8,128)(2,1)S(1)} %get-tuple-element.38), channel_id=1, source_target_pairs={{0,8},{4,12},{8,0},{12,4},{1,9},{5,13},{9,1},{13,5},{2,10},{6,14},... | collective-permute-start | bytes 688136 | tf_op jit(solution)/shard_map/ppermute | solution.py:470
  24.9 10.6 %copy-start.14 = (f32[8,10240]{1,0:T(8,128)S(1)}, f32[8,10240]{1,0:T(8,128)}, u32[]{:S(2)}) copy-start(f32[8,10240]{1,0:T(8,128)} %refs_5_.1) | copy-start | bytes 983044
  24.9 10.6 %copy-start.15 = (f32[8,10240]{1,0:T(8,128)S(1)}, f32[8,10240]{1,0:T(8,128)}, u32[]{:S(2)}) copy-start(f32[8,10240]{1,0:T(8,128)} %refs_6_.1) | copy-start | bytes 983044
  24.9 10.7 %copy-start.16 = (f32[8,10240]{1,0:T(8,128)S(1)}, f32[8,10240]{1,0:T(8,128)}, u32[]{:S(2)}) copy-start(f32[8,10240]{1,0:T(8,128)} %refs_7_.1) | copy-start | bytes 983044
  24.9 10.7 %copy-start.17 = (f32[4096,8]{0,1:T(8,128)S(1)}, f32[4096,8]{0,1:T(8,128)}, u32[]{:S(2)}) copy-start(f32[4096,8]{0,1:T(8,128)} %param.12) | copy-start | bytes 393220
  24.9 10.7 %copy-start.18 = (f32[4096,8]{0,1:T(8,128)S(1)}, f32[4096,8]{0,1:T(8,128)}, u32[]{:S(2)}) copy-start(f32[4096,8]{0,1:T(8,128)} %param.14) | copy-start | bytes 393220
  24.9 10.7 %copy-start.19 = (f32[4096,8]{0,1:T(8,128)S(1)}, f32[4096,8]{0,1:T(8,128)}, u32[]{:S(2)}) copy-start(f32[4096,8]{0,1:T(8,128)} %param.15) | copy-start | bytes 393220
  34.2 24.8 %collective-permute-start.9 = (bf16[192,2048]{1,0:T(8,128)(2,1)S(1)}, bf16[192,2048]{1,0:T(8,128)(2,1)S(1)}, u32[]{:S(2)}, u32[]{:S(2)}) collective-permute-start(bf16[192,2048]{1,0:T(8,128)(2,1)S(1)} %get-tuple-element.39.refs_8_), channel_id=1, source_target_pairs={{0,1},{3,2},{4,5},{7,6},{8,9},{11,10},{12,13},{15,14},{16,17},{19,... | collective-permute-start | bytes 2359304 | tf_op jit(solution)/shard_map/ppermute | solution.py:467
  37.4 2.5 %collective-permute-start.3 = (bf16[8,4096]{1,0:T(8,128)(2,1)S(1)}, bf16[8,4096]{1,0:T(8,128)(2,1)S(1)}, u32[]{:S(2)}, u32[]{:S(2)}) collective-permute-start(bf16[8,4096]{1,0:T(8,128)(2,1)S(1)} %get-tuple-element.41), channel_id=1, source_target_pairs={{0,4},{4,0},{8,12},{12,8},{1,5},{5,1},{9,13},{13,9},{2,6},{6,2},{1... | collective-permute-start | bytes 196616 | tf_op jit(solution)/shard_map/ppermute | solution.py:470
  37.7 19.5 %collective-permute-start.2 = (bf16[8,10240]{1,0:T(8,128)(2,1)S(1)}, bf16[8,10240]{1,0:T(8,128)(2,1)S(1)}, u32[]{:S(2)}, u32[]{:S(2)}) collective-permute-start(bf16[8,10240]{1,0:T(8,128)(2,1)S(1)} %get-tuple-element.40.refs_6_), channel_id=1, source_target_pairs={{0,0},{1,4},{2,8},{3,12},{4,1},{5,5},{6,9},{7,13},{8,2},{9,6},{10,... | collective-permute-start | bytes 491528 | tf_op jit(solution)/shard_map/ppermute | solution.py:511
  38.3 0.7 copy-start.5
  38.3 0.9 copy-start.2
  39.3 40.3 %collective-permute-start.8 = (bf16[128,2560]{1,0:T(8,128)(2,1)S(1)}, bf16[128,2560]{1,0:T(8,128)(2,1)S(1)}, u32[]{:S(2)}, u32[]{:S(2)}) collective-permute-start(bf16[128,2560]{1,0:T(8,128)(2,1)S(1)} %shard_map.159.refs_2_), channel_id=1, source_target_pairs={{1,2},{2,1},{5,6},{6,5},{9,10},{10,9},{13,14},{14,13},{17,18},{18,... | collective-permute-start | bytes 1966088 | tf_op jit(solution)/shard_map/ppermute | solution.py:467
  40.0 17.2 %collective-permute-start.4 = (bf16[16,4096]{1,0:T(8,128)(2,1)S(1)}, bf16[16,4096]{1,0:T(8,128)(2,1)S(1)}, u32[]{:S(2)}, u32[]{:S(2)}) collective-permute-start(bf16[16,4096]{1,0:T(8,128)(2,1)S(1)} %constant_dynamic-update-slice_fusion.refs_1_), channel_id=1, source_target_pairs={{0,8},{4,12},{8,0},{12,4},{1,9},{5,13},{9,1},{13,5},{2,10},{6,14},... | collective-permute-start | bytes 393224 | tf_op jit(solution)/shard_map/ppermute | solution.py:470
  52.3 25.9 %collective-permute-start.11 = (bf16[192,2048]{1,0:T(8,128)(2,1)S(1)}, bf16[192,2048]{1,0:T(8,128)(2,1)S(1)}, u32[]{:S(2)}, u32[]{:S(2)}) collective-permute-start(bf16[192,2048]{1,0:T(8,128)(2,1)S(1)} %get-tuple-element.44.refs_4_), channel_id=1, source_target_pairs={{0,1},{3,2},{4,5},{7,6},{8,9},{11,10},{12,13},{15,14},{16,17},{19,... | collective-permute-start | bytes 2359304 | tf_op jit(solution)/shard_map/ppermute | solution.py:467
  58.9 23.4 %collective-permute-start.7 = (bf16[8,12288]{1,0:T(8,128)(2,1)S(1)}, bf16[8,12288]{1,0:T(8,128)(2,1)S(1)}, u32[]{:S(2)}, u32[]{:S(2)}) collective-permute-start(bf16[8,12288]{1,0:T(8,128)(2,1)S(1)} %get-tuple-element.45.refs_3_), channel_id=1, source_target_pairs={{0,1},{1,0},{2,3},{3,2},{4,5},{5,4},{6,7},{7,6},{8,9},{9,8},{10,11... | collective-permute-start | bytes 589832 | tf_op jit(solution)/shard_map/ppermute | solution.py:517
  59.6 20.0 %collective-permute-start.10 = (bf16[128,2048]{1,0:T(8,128)(2,1)S(1)}, bf16[128,2048]{1,0:T(8,128)(2,1)S(1)}, u32[]{:S(2)}, u32[]{:S(2)}) collective-permute-start(bf16[128,2048]{1,0:T(8,128)(2,1)S(1)} %shard_map.162.refs_2_), channel_id=1, source_target_pairs={{1,2},{2,1},{5,6},{6,5},{9,10},{10,9},{13,14},{14,13},{17,18},{18,... | collective-permute-start | bytes 1572872 | tf_op jit(solution)/shard_map/ppermute | solution.py:467
  69.5 27.4 %collective-permute-start.15 = (bf16[192,2048]{1,0:T(8,128)(2,1)S(1)}, bf16[192,2048]{1,0:T(8,128)(2,1)S(1)}, u32[]{:S(2)}, u32[]{:S(2)}) collective-permute-start(bf16[192,2048]{1,0:T(8,128)(2,1)S(1)} %get-tuple-element.49.refs_3_), channel_id=1, source_target_pairs={{0,1},{3,2},{4,5},{7,6},{8,9},{11,10},{12,13},{15,14},{16,17},{19,... | collective-permute-start | bytes 2359304 | tf_op jit(solution)/shard_map/ppermute | solution.py:467
  78.9 16.1 %collective-permute-start.16 = (bf16[128,2048]{1,0:T(8,128)(2,1)S(1)}, bf16[128,2048]{1,0:T(8,128)(2,1)S(1)}, u32[]{:S(2)}, u32[]{:S(2)}) collective-permute-start(bf16[128,2048]{1,0:T(8,128)(2,1)S(1)} %shard_map.164.refs_6_), channel_id=1, source_target_pairs={{1,2},{2,1},{5,6},{6,5},{9,10},{10,9},{13,14},{14,13},{17,18},{18,... | collective-permute-start | bytes 1572872 | tf_op jit(solution)/shard_map/ppermute | solution.py:467
  80.2 0.8 copy-start.12
  81.0 16.6 %collective-permute-start.17 = (bf16[64,4608]{1,0:T(8,128)(2,1)S(1)}, bf16[64,4608]{1,0:T(8,128)(2,1)S(1)}, u32[]{:S(2)}, u32[]{:S(2)}) collective-permute-start(bf16[64,4608]{1,0:T(8,128)(2,1)S(1)} %shard_map.165.refs_3_), channel_id=1, source_target_pairs={{2,3},{1,0},{6,7},{5,4},{10,11},{9,8},{14,15},{13,12},{18,19},{17,... | collective-permute-start | bytes 1769480 | tf_op jit(solution)/shard_map/ppermute | solution.py:467
  82.9 28.5 %collective-permute-start.12 = (bf16[16,11264]{1,0:T(8,128)(2,1)S(1)}, bf16[16,11264]{1,0:T(8,128)(2,1)S(1)}, u32[]{:S(2)}, u32[]{:S(2)}) collective-permute-start(bf16[16,11264]{1,0:T(8,128)(2,1)S(1)} %get-tuple-element.51.refs_2_.refs_5_.refs_12_.refs_19_), channel_id=1, source_target_pairs={{1,2},{2,1},{5,6},{6,5},{9,10},{10,9},{13,14},{14,13},{17,18},{18,... | collective-permute-start | bytes 1081352 | tf_op jit(solution)/shard_map/ppermute | solution.py:467
  89.1 21.0 %collective-permute-start.14 = (bf16[192,1024]{1,0:T(8,128)(2,1)S(1)}, bf16[192,1024]{1,0:T(8,128)(2,1)S(1)}, u32[]{:S(2)}, u32[]{:S(2)}) collective-permute-start(bf16[192,1024]{1,0:T(8,128)(2,1)S(1)} %get-tuple-element.53.refs_2_), channel_id=1, source_target_pairs={{0,1},{3,2},{4,5},{7,6},{8,9},{11,10},{12,13},{15,14},{16,17},{19,... | collective-permute-start | bytes 1179656 | tf_op jit(solution)/shard_map/ppermute | solution.py:467
  95.0 2.6 %copy-start.9 = (bf16[128,2048]{1,0:T(8,128)(2,1)}, bf16[128,2048]{1,0:T(8,128)(2,1)S(1)}, u32[]{:S(2)}) copy-start(bf16[128,2048]{1,0:T(8,128)(2,1)S(1)} %collective-permute-done.16.refs_1_.refs_3_) | copy-start | bytes 1572868
  95.6 14.5 %collective-permute-start.18 = (bf16[64,2048]{1,0:T(8,128)(2,1)S(1)}, bf16[64,2048]{1,0:T(8,128)(2,1)S(1)}, u32[]{:S(2)}, u32[]{:S(2)}) collective-permute-start(bf16[64,2048]{1,0:T(8,128)(2,1)S(1)} %shard_map.168.refs_3_), channel_id=1, source_target_pairs={{2,3},{1,0},{6,7},{5,4},{10,11},{9,8},{14,15},{13,12},{18,19},{17,... | collective-permute-start | bytes 786440 | tf_op jit(solution)/shard_map/ppermute | solution.py:467
  98.3 16.2 %collective-permute-start.22 = (bf16[128,2048]{1,0:T(8,128)(2,1)S(1)}, bf16[128,2048]{1,0:T(8,128)(2,1)S(1)}, u32[]{:S(2)}, u32[]{:S(2)}) collective-permute-start(bf16[128,2048]{1,0:T(8,128)(2,1)S(1)} %shard_map.169.refs_2_), channel_id=1, source_target_pairs={{1,2},{2,1},{5,6},{6,5},{9,10},{10,9},{13,14},{14,13},{17,18},{18,... | collective-permute-start | bytes 1572872 | tf_op jit(solution)/shard_map/ppermute | solution.py:467
  103.0 10.2 %collective-permute-start.20 = (bf16[192,512]{1,0:T(8,128)(2,1)S(1)}, bf16[192,512]{1,0:T(8,128)(2,1)S(1)}, u32[]{:S(2)}, u32[]{:S(2)}) collective-permute-start(bf16[192,512]{1,0:T(8,128)(2,1)S(1)} %get-tuple-element.55.refs_3_), channel_id=1, source_target_pairs={{0,1},{3,2},{4,5},{7,6},{8,9},{11,10},{12,13},{15,14},{16,17},{19,... | collective-permute-start | bytes 589832 | tf_op jit(solution)/shard_map/ppermute | solution.py:467
  110.7 5.9 %collective-permute-start.19 = (bf16[128,1024]{1,0:T(8,128)(2,1)S(1)}, bf16[128,1024]{1,0:T(8,128)(2,1)S(1)}, u32[]{:S(2)}, u32[]{:S(2)}) collective-permute-start(bf16[128,1024]{1,0:T(8,128)(2,1)S(1)} %shard_map.171.refs_3_), channel_id=1, source_target_pairs={{1,2},{2,1},{5,6},{6,5},{9,10},{10,9},{13,14},{14,13},{17,18},{18,... | collective-permute-start | bytes 786440 | tf_op jit(solution)/shard_map/ppermute | solution.py:467
  111.4 12.9 %collective-permute-start.13 = (bf16[16,11264]{1,0:T(8,128)(2,1)S(1)}, bf16[16,11264]{1,0:T(8,128)(2,1)S(1)}, u32[]{:S(2)}, u32[]{:S(2)}) collective-permute-start(bf16[16,11264]{1,0:T(8,128)(2,1)S(1)} %collective-permute-done.12.refs_1_.refs_6_.refs_13_.refs_20_), channel_id=1, source_target_pairs={{2,3},{1,0},{6,7},{5,4},{10,11},{9,8},{14,15},{13,12},{18,19},{17,... | collective-permute-start | bytes 1081352 | tf_op jit(solution)/shard_map/ppermute | solution.py:467
  113.8 2.8 %collective-permute-start.21 = (bf16[128,512]{1,0:T(8,128)(2,1)S(1)}, bf16[128,512]{1,0:T(8,128)(2,1)S(1)}, u32[]{:S(2)}, u32[]{:S(2)}) collective-permute-start(bf16[128,512]{1,0:T(8,128)(2,1)S(1)} %shard_map.172.refs_2_), channel_id=1, source_target_pairs={{1,2},{2,1},{5,6},{6,5},{9,10},{10,9},{13,14},{14,13},{17,18},{18,... | collective-permute-start | bytes 393224 | tf_op jit(solution)/shard_map/ppermute | solution.py:467
  114.5 2.7 %copy-start.7 = (bf16[128,2048]{1,0:T(8,128)(2,1)}, bf16[128,2048]{1,0:T(8,128)(2,1)S(1)}, u32[]{:S(2)}) copy-start(bf16[128,2048]{1,0:T(8,128)(2,1)S(1)} %collective-permute-done.22.refs_1_.refs_3_) | copy-start | bytes 1572868
  115.1 10.2 %copy-start.3 = (bf16[192,1536]{1,0:T(8,128)(2,1)S(1)}, bf16[192,1536]{1,0:T(8,128)(2,1)}, u32[]{:S(2)}) copy-start(bf16[192,1536]{1,0:T(8,128)(2,1)} %copy-done.2) | copy-start | bytes 1769476
  115.2 10.2 %copy-start.6 = (bf16[192,1024]{1,0:T(8,128)(2,1)S(1)}, bf16[192,1024]{1,0:T(8,128)(2,1)}, u32[]{:S(2)}) copy-start(bf16[192,1024]{1,0:T(8,128)(2,1)} %copy-done.5) | copy-start | bytes 1179652
  115.2 10.2 %copy-start.13 = (bf16[128,2048]{1,0:T(8,128)(2,1)S(1)}, bf16[128,2048]{1,0:T(8,128)(2,1)}, u32[]{:S(2)}) copy-start(bf16[128,2048]{1,0:T(8,128)(2,1)} %copy-done.12) | copy-start | bytes 1572868
  115.2 14.0 %collective-permute-start.24 = (bf16[64,2048]{1,0:T(8,128)(2,1)S(1)}, bf16[64,2048]{1,0:T(8,128)(2,1)S(1)}, u32[]{:S(2)}, u32[]{:S(2)}) collective-permute-start(bf16[64,2048]{1,0:T(8,128)(2,1)S(1)} %shard_map.173.refs_4_), channel_id=1, source_target_pairs={{2,3},{1,0},{6,7},{5,4},{10,11},{9,8},{14,15},{13,12},{18,19},{17,... | collective-permute-start | bytes 786440 | tf_op jit(solution)/shard_map/ppermute | solution.py:467
  117.2 14.1 %collective-permute-start.23 = (bf16[64,1536]{1,0:T(8,128)(2,1)S(1)}, bf16[64,1536]{1,0:T(8,128)(2,1)S(1)}, u32[]{:S(2)}, u32[]{:S(2)}) collective-permute-start(bf16[64,1536]{1,0:T(8,128)(2,1)S(1)} %shard_map.174.refs_3_), channel_id=1, source_target_pairs={{2,3},{1,0},{6,7},{5,4},{10,11},{9,8},{14,15},{13,12},{18,19},{17,... | collective-permute-start | bytes 589832 | tf_op jit(solution)/shard_map/ppermute | solution.py:467
  125.4 1.0 copy-start.10
  126.4 2.8 %copy-start.8 = (bf16[128,2048]{1,0:T(8,128)(2,1)S(1)}, bf16[128,2048]{1,0:T(8,128)(2,1)}, u32[]{:S(2)}) copy-start(bf16[128,2048]{1,0:T(8,128)(2,1)} %copy-done.7) | copy-start | bytes 1572868

commit v7 on v5

--- a/solution.py
+++ b/solution.py
@@ -529,11 +529,10 @@
     last = second((5,), last)
     last = third((3,), last)
     last = second((6,), last)
+    last = third((4,), last)
+    last = third((5, 6), last)
     last = spread = spread_inner(place, inner, near_out, far_out, width, share, [last])
     last = finish((0, 1, 2), last)
-    last = third((4,), last)
-    last = third((5,), last)
-    last = third((6,), last)
     last = finish((3,), last)
     last = finish((4,), last)
     decoded = finish((5, 6), last, full_width=width, done=list(finished))

time: 132 us -> 150 us (1.14)
  waiting for transfers between devices: 8.95 us -> 26.2 us
    ppermute x20 -> x19, waiting for transfers between devices: 8.94 us -> 26.2 us  [line(): return lax.ppermute(values, 'tp', LINE[step])]
    ppermute x20 -> x19, starting transfers between devices: 44.5 us -> 45.5 us  [line(): return lax.ppermute(values, 'tp', LINE[step])]
    pallas_call x28 -> x27, Pallas kernels: 68.2 us -> 67.6 us  [call(): pl.pallas_call(kernel, grid_spec=pltpu.PrefetchScalarGridSpec(num_scalar_...]
  transfers between devices with their start and end apart: 26 -> 25, of which waited for: 3 -> 5; matrix products, arithmetic and copies ran while one was open for 0% -> 0% of each run, Pallas kernels for 46% -> 40%
where the time goes in v7:
time: 150 us; the launch traced here: 149 us
  Pallas kernels  67.6 us (45%)
  starting transfers between devices  51.2 us (34%)
  waiting for transfers between devices  26.2 us (17%)
  local copies, waits for them, and re-layouts  2.75 us (2%)
    pallas_call x27, Pallas kernels, call(): pl.pallas_call(kernel, grid_spec=pltpu.PrefetchScalarGridSpec(num_scalar_...  67.6 us
    ppermute x19, starting transfers between devices, line(): return lax.ppermute(values, 'tp', LINE[step])  45.5 us
    ppermute x19, waiting for transfers between devices, line(): return lax.ppermute(values, 'tp', LINE[step])  26.2 us
    ppermute x4, starting transfers between devices, chip(): return lax.ppermute(values, 'rep', [(i, i ^ bit) for i in range(4)])  4.89 us
  transfers between devices with their start and end apart: 25, of which 5 were waited for; matrix products, arithmetic and copies ran while one was open for 0% of the time, Pallas kernels for 40%

profile of v7, /device:TPU:0, one launch (start us, length us, event | category | flops | bytes accessed | tf_op | source)
XLA Modules:
  0.0 149.2 jit_solution(11394352388060220467)
XLA Ops:
  0.8 1.6 %copy-done = bf16[256,4096]{1,0:T(8,128)(2,1)S(1)} copy-done((bf16[256,4096]{1,0:T(8,128)(2,1)S(1)}, bf16[256,4096]{1,0:T(8,128)(2,1)}, u32[]{:S(2)}) %copy-start) | copy-done | bytes 2097176
  2.4 5.5 %shard_map.153 = (f32[256,1024]{1,0:T(8,128)S(1)}, bf16[192,1024]{1,0:T(8,128)(2,1)S(1)}) custom-call(s32[13]{0:T(128)S(1)} %stack.55.place_ref, bf16[256,4096]{1,0:T(8,128)(2,1)S(1)} %copy-done, bf16[4096,10240]{1,0:T(8,128)(2,1)} %refs_1_.13), custom_call_target="tpu_custom_call" | custom-call | flops 10737418240 | bytes 41943040 | tf_op jit(solution)/shard_map/pallas_call | solution.py:122
  7.9 5.1 %collective-permute-start.5 = (bf16[192,1024]{1,0:T(8,128)(2,1)S(1)}, bf16[192,1024]{1,0:T(8,128)(2,1)S(1)}, u32[]{:S(2)}, u32[]{:S(2)}) collective-permute-start(bf16[192,1024]{1,0:T(8,128)(2,1)S(1)} %get-tuple-element.35.refs_2_), channel_id=1, source_target_pairs={{0,1},{3,2},{4,5},{7,6},{8,9},{11,10},{12,13},{15,14},{16,17},{19,... | collective-permute-start | bytes 1179656 | tf_op jit(solution)/shard_map/ppermute | solution.py:467
  13.7 7.7 %shard_map.155 = (f32[256,1536]{1,0:T(8,128)S(1)}, bf16[192,1536]{1,0:T(8,128)(2,1)S(1)}) custom-call(s32[13]{0:T(128)S(1)} %stack.55.place_ref, bf16[256,4096]{1,0:T(8,128)(2,1)S(1)} %copy-done.1, bf16[4096,10240]{1,0:T(8,128)(2,1)} %refs_1_.13, bf16[16,14336]{1,0:T(8,128)(2,1)S(1)} %shard_map.154.refs_2_), custom_call_target="tpu_custom_call" | custom-call | flops 16106127360 | bytes 62914560 | tf_op jit(solution)/shard_map/pallas_call | solution.py:122
  21.3 1.3 collective-permute-start.6
  22.7 0.7 shard_map.156
  23.3 1.6 %collective-permute-start.1 = (bf16[8,14336]{1,0:T(8,128)(2,1)S(1)}, bf16[8,14336]{1,0:T(8,128)(2,1)S(1)}, u32[]{:S(2)}, u32[]{:S(2)}) collective-permute-start(bf16[8,14336]{1,0:T(8,128)(2,1)S(1)} %get-tuple-element.38), channel_id=1, source_target_pairs={{0,8},{4,12},{8,0},{12,4},{1,9},{5,13},{9,1},{13,5},{2,10},{6,14},... | collective-permute-start | bytes 688136 | tf_op jit(solution)/shard_map/ppermute | solution.py:470
  24.9 9.2 %shard_map.157 = (f32[256,2048]{1,0:T(8,128)S(1)}, bf16[192,2048]{1,0:T(8,128)(2,1)S(1)}) custom-call(s32[13]{0:T(128)S(1)} %stack.55.place_ref, bf16[256,4096]{1,0:T(8,128)(2,1)S(1)} %copy-done.1, bf16[4096,10240]{1,0:T(8,128)(2,1)} %refs_1_.13, f32[8,14336]{1,0:T(8,128)S(1)} %get-tuple-element.37.refs_2_.refs_0_), custom_call_target="tpu_custom_call" | custom-call | flops 21474836480 | bytes 83886080 | tf_op jit(solution)/shard_map/pallas_call | solution.py:122
  34.2 1.3 collective-permute-start.9
  35.6 1.9 %shard_map.158 = (f32[8,4096]{1,0:T(8,128)}, f32[8,4096]{1,0:T(8,128)}, f32[8,4096]{1,0:T(8,128)}, bf16[8,4096]{1,0:T(8,128)(2,1)S(1)}, f32[8,10240]{1,0:T(8,128...) custom-call(s32[13]{0:T(128)S(1)} %stack.55.place_ref, ...), custom_call_target="tpu_custom_call" | custom-call | bytes 18350080 | tf_op jit(solution)/shard_map/pallas_call | solution.py:122
  37.7 0.7 collective-permute-start.2
  38.3 0.7 shard_map.159.refs_2_
  39.1 0.7 collective-permute-start.8
  39.8 3.1 %collective-permute-start.4 = (bf16[16,4096]{1,0:T(8,128)(2,1)S(1)}, bf16[16,4096]{1,0:T(8,128)(2,1)S(1)}, u32[]{:S(2)}, u32[]{:S(2)}) collective-permute-start(bf16[16,4096]{1,0:T(8,128)(2,1)S(1)} %constant_dynamic-update-slice_fusion.refs_1_), channel_id=1, source_target_pairs={{0,8},{4,12},{8,0},{12,4},{1,9},{5,13},{9,1},{13,5},{2,10},{6,14},... | collective-permute-start | bytes 393224 | tf_op jit(solution)/shard_map/ppermute | solution.py:470
  42.9 9.2 %shard_map.160 = (f32[256,2048]{1,0:T(8,128)S(1)}, bf16[192,2048]{1,0:T(8,128)(2,1)S(1)}) custom-call(s32[13]{0:T(128)S(1)} %stack.55.place_ref, bf16[256,4096]{1,0:T(8,128)(2,1)S(1)} %copy-done.1, bf16[4096,10240]{1,0:T(8,128)(2,1)} %refs_1_.13, bf16[128,2560]{1,0:T(8,128)(2,1)S(1)} %shard_map.159.refs_2_), custom_call_target="tpu_custom_call" | custom-call | flops 21474836480 | bytes 83886080 | tf_op jit(solution)/shard_map/pallas_call | solution.py:122
  52.1 4.9 %collective-permute-start.11 = (bf16[192,2048]{1,0:T(8,128)(2,1)S(1)}, bf16[192,2048]{1,0:T(8,128)(2,1)S(1)}, u32[]{:S(2)}, u32[]{:S(2)}) collective-permute-start(bf16[192,2048]{1,0:T(8,128)(2,1)S(1)} %get-tuple-element.44.refs_4_), channel_id=1, source_target_pairs={{0,1},{3,2},{4,5},{7,6},{8,9},{11,10},{12,13},{15,14},{16,17},{19,... | collective-permute-start | bytes 2359304 | tf_op jit(solution)/shard_map/ppermute | solution.py:467
  57.0 1.7 %shard_map.161 = (f32[8,1024]{1,0:T(8,128)S(1)}, bf16[8,12288]{1,0:T(8,128)(2,1)S(1)}) custom-call(s32[13]{0:T(128)S(1)} %stack.55.place_ref, bf16[256,4096]{1,0:T(8,128)(2,1)S(1)} %copy-done.1, bf16[16,4096]{1,0:T(8,128)(2,1)S(1)} %constant_dynamic-update-slice_fusion.refs_1_, bf16[16,4096]{1,0:T(8,128)(2,1)S(1)} %collective-permute-done.4.refs_2_, ...), custom_call_target="tpu_custom_call" | custom-call | flops 335544320 | bytes 10485760 | tf_op jit(solution)/shard_map/pallas_call | solution.py:122
  59.0 0.6 shard_map.162.refs_2_
  59.6 0.7 collective-permute-start.10
  60.3 9.2 %shard_map.163 = (f32[256,2048]{1,0:T(8,128)S(1)}, bf16[192,2048]{1,0:T(8,128)(2,1)S(1)}) custom-call(s32[13]{0:T(128)S(1)} %stack.55.place_ref, bf16[256,4096]{1,0:T(8,128)(2,1)S(1)} %copy-done.1, bf16[4096,10240]{1,0:T(8,128)(2,1)} %refs_1_.13, bf16[128,2048]{1,0:T(8,128)(2,1)S(1)} %shard_map.162.refs_2_), custom_call_target="tpu_custom_call" | custom-call | flops 21474836480 | bytes 83886080 | tf_op jit(solution)/shard_map/pallas_call | solution.py:122
  69.5 8.7 %collective-permute-start.15 = (bf16[192,2048]{1,0:T(8,128)(2,1)S(1)}, bf16[192,2048]{1,0:T(8,128)(2,1)S(1)}, u32[]{:S(2)}, u32[]{:S(2)}) collective-permute-start(bf16[192,2048]{1,0:T(8,128)(2,1)S(1)} %get-tuple-element.49.refs_3_), channel_id=1, source_target_pairs={{0,1},{3,2},{4,5},{7,6},{8,9},{11,10},{12,13},{15,14},{16,17},{19,... | collective-permute-start | bytes 2359304 | tf_op jit(solution)/shard_map/ppermute | solution.py:467
  78.2 0.6 shard_map.164.refs_6_
  78.9 0.7 collective-permute-start.19
  79.6 0.6 shard_map.165.refs_3_
  80.4 1.3 collective-permute-start.16
  82.3 5.5 %shard_map.167 = (f32[256,1024]{1,0:T(8,128)S(1)}, bf16[192,1024]{1,0:T(8,128)(2,1)S(1)}) custom-call(s32[13]{0:T(128)S(1)} %stack.55.place_ref, bf16[256,4096]{1,0:T(8,128)(2,1)S(1)} %copy-done.1, bf16[4096,10240]{1,0:T(8,128)(2,1)} %refs_1_.13, bf16[16,11264]{1,0:T(8,128)(2,1)S(1)} %get-tuple-element.51.refs_2_.refs_5_.refs_12_.refs_19_), custom_call_target="tpu_custom_call" | custom-call | flops 10737418240 | bytes 41943040 | tf_op jit(solution)/shard_map/pallas_call | solution.py:122
  87.8 4.6 %collective-permute-start.14 = (bf16[192,1024]{1,0:T(8,128)(2,1)S(1)}, bf16[192,1024]{1,0:T(8,128)(2,1)S(1)}, u32[]{:S(2)}, u32[]{:S(2)}) collective-permute-start(bf16[192,1024]{1,0:T(8,128)(2,1)S(1)} %get-tuple-element.53.refs_2_), channel_id=1, source_target_pairs={{0,1},{3,2},{4,5},{7,6},{8,9},{11,10},{12,13},{15,14},{16,17},{19,... | collective-permute-start | bytes 1179656 | tf_op jit(solution)/shard_map/ppermute | solution.py:467
  92.4 4.0 %shard_map.168 = (f32[256,512]{1,0:T(8,128)S(1)}, bf16[192,512]{1,0:T(8,128)(2,1)S(1)}) custom-call(s32[13]{0:T(128)S(1)} %stack.55.place_ref, bf16[256,4096]{1,0:T(8,128)(2,1)S(1)} %copy-done.1, bf16[4096,10240]{1,0:T(8,128)(2,1)} %refs_1_.13, bf16[192,1024]{1,0:T(8,128)(2,1)S(1)} %get-tuple-element.53.refs_2_), custom_call_target="tpu_custom_call" | custom-call | flops 5368709120 | bytes 20971520 | tf_op jit(solution)/shard_map/pallas_call | solution.py:122
  96.8 0.6 shard_map.169.refs_3_
  97.4 0.7 collective-permute-start.21
  98.2 0.7 collective-permute-start.12
  98.8 8.2 %collective-permute-start.18 = (bf16[192,512]{1,0:T(8,128)(2,1)S(1)}, bf16[192,512]{1,0:T(8,128)(2,1)S(1)}, u32[]{:S(2)}, u32[]{:S(2)}) collective-permute-start(bf16[192,512]{1,0:T(8,128)(2,1)S(1)} %get-tuple-element.55.refs_3_), channel_id=1, source_target_pairs={{0,1},{3,2},{4,5},{7,6},{8,9},{11,10},{12,13},{15,14},{16,17},{19,... | collective-permute-start | bytes 589832 | tf_op jit(solution)/shard_map/ppermute | solution.py:467
  107.7 0.7 collective-permute-start.17
  108.4 1.3 collective-permute-start.13
  110.3 0.8 copy-done.5
  111.6 0.7 collective-permute-start.20
  112.3 1.3 collective-permute-start.23
  114.3 1.4 collective-permute-start.24
  116.3 1.3 collective-permute-start.22
  117.6 14.1 %collective-permute-done.13.refs_2_.refs_7_.refs_14_.refs_21_ = bf16[16,11264]{1,0:T(8,128)(2,1)S(1)} collective-permute-done((bf16[16,11264]{1,0:T(8,128)(2,1)S(1)}, bf16[16,11264]{1,0:T(8,128)(2,1)S(1)}, u32[]{:S(2)}, u32[]{:S(2)}) %collective-permute-start.13) | collective-permute-done | bytes 360480 | tf_op jit(solution)/shard_map/ppermute | solution.py:467
  131.7 1.0 shard_map.175.refs_0_.refs_22_
  132.7 0.9 shard_map.176.refs_8_.refs_15_
  133.6 3.8 %collective-permute-done.23.refs_4_ = bf16[64,2048]{1,0:T(8,128)(2,1)S(1)} collective-permute-done((bf16[64,2048]{1,0:T(8,128)(2,1)S(1)}, bf16[64,2048]{1,0:T(8,128)(2,1)S(1)}, u32[]{:S(2)}, u32[]{:S(2)}) %collective-permute-start.23) | collective-permute-done | bytes 262176 | tf_op jit(solution)/shard_map/ppermute | solution.py:467
  137.4 0.7 shard_map.177.refs_8_.refs_16_
  138.2 4.9 %collective-permute-done.24.refs_4_ = bf16[64,2048]{1,0:T(8,128)(2,1)S(1)} collective-permute-done((bf16[64,2048]{1,0:T(8,128)(2,1)S(1)}, bf16[64,2048]{1,0:T(8,128)(2,1)S(1)}, u32[]{:S(2)}, u32[]{:S(2)}) %collective-permute-start.24) | collective-permute-done | bytes 262176 | tf_op jit(solution)/shard_map/ppermute | solution.py:467
  143.0 0.8 shard_map.178.refs_17_.refs_18_
  143.8 3.1 %collective-permute-done.22.refs_4_.refs_11_ = bf16[64,1536]{1,0:T(8,128)(2,1)S(1)} collective-permute-done((bf16[64,1536]{1,0:T(8,128)(2,1)S(1)}, bf16[64,1536]{1,0:T(8,128)(2,1)S(1)}, u32[]{:S(2)}, u32[]{:S(2)}) %collective-permute-start.22) | collective-permute-done | bytes 196640 | tf_op jit(solution)/shard_map/ppermute | solution.py:467
  146.9 2.3 %shard_map.179 = f32[64,10240]{1,0:T(8,128)} custom-call(s32[13]{0:T(128)S(1)} %stack.55.place_ref, bf16[64,64]{1,0:T(8,128)(2,1)S(1)} %shard_map.175.refs_0_.refs_22_, f32[256,1024]{1,0:T(8,128)S(1)} %get-tuple-element.52.refs_0_.refs_1_, bf16[192,1024]{1,0:T(8,128)(2,1)S(1)} %collective-permute-done.14.refs_1_.refs_2_, ...), custom_call_target="tpu_custom_call" | custom-call | bytes 45875200 | tf_op jit(solution)/shard_map/pallas_call | solution.py:122
  (64 shorter events, 5.4 us)
Async XLA Ops:
  0.8 1.6 %copy-start = (bf16[256,4096]{1,0:T(8,128)(2,1)S(1)}, bf16[256,4096]{1,0:T(8,128)(2,1)}, u32[]{:S(2)}) copy-start(bf16[256,4096]{1,0:T(8,128)(2,1)} %refs_0_.15) | copy-start | bytes 6291460
  2.4 10.6 %copy-start.2 = (f32[1,32,10240]{2,1,0:T(8,128)S(1)}, f32[1,32,10240]{2,1,0:T(8,128)}, u32[]{:S(2)}) copy-start(f32[1,32,10240]{2,1,0:T(8,128)} %param.19) | copy-start | bytes 3932164
  2.4 10.6 %copy-start.7 = (f32[1,4096,32]{1,2,0:T(8,128)S(1)}, f32[1,4096,32]{1,2,0:T(8,128)}, u32[]{:S(2)}) copy-start(f32[1,4096,32]{1,2,0:T(8,128)} %param.18) | copy-start | bytes 1572868
  7.8 5.8 %copy-start.1 = (bf16[256,4096]{1,0:T(8,128)(2,1)S(1)}, bf16[256,4096]{1,0:T(8,128)(2,1)}, u32[]{:S(2)}) copy-start(bf16[256,4096]{1,0:T(8,128)(2,1)} %refs_0_.15) | copy-start | bytes 6291460
  7.9 30.5 %collective-permute-start.5 = (bf16[192,1024]{1,0:T(8,128)(2,1)S(1)}, bf16[192,1024]{1,0:T(8,128)(2,1)S(1)}, u32[]{:S(2)}, u32[]{:S(2)}) collective-permute-start(bf16[192,1024]{1,0:T(8,128)(2,1)S(1)} %get-tuple-element.35.refs_2_), channel_id=1, source_target_pairs={{0,1},{3,2},{4,5},{7,6},{8,9},{11,10},{12,13},{15,14},{16,17},{19,... | collective-permute-start | bytes 1179656 | tf_op jit(solution)/shard_map/ppermute | solution.py:467
  13.6 9.1 %collective-permute-start = (bf16[16,14336]{1,0:T(8,128)(2,1)S(1)}, bf16[16,14336]{1,0:T(8,128)(2,1)S(1)}, u32[]{:S(2)}, u32[]{:S(2)}) collective-permute-start(bf16[16,14336]{1,0:T(8,128)(2,1)S(1)} %shard_map.154.refs_2_), channel_id=1, source_target_pairs={{0,4},{4,0},{8,12},{12,8},{1,5},{5,1},{9,13},{13,9},{2,6},{6,2},{1... | collective-permute-start | bytes 1376264 | tf_op jit(solution)/shard_map/ppermute | solution.py:470
  21.3 17.0 %collective-permute-start.6 = (bf16[192,1536]{1,0:T(8,128)(2,1)S(1)}, bf16[192,1536]{1,0:T(8,128)(2,1)S(1)}, u32[]{:S(2)}, u32[]{:S(2)}) collective-permute-start(bf16[192,1536]{1,0:T(8,128)(2,1)S(1)} %get-tuple-element.36.refs_3_), channel_id=1, source_target_pairs={{0,1},{3,2},{4,5},{7,6},{8,9},{11,10},{12,13},{15,14},{16,17},{19,... | collective-permute-start | bytes 1769480 | tf_op jit(solution)/shard_map/ppermute | solution.py:467
  23.3 12.2 %collective-permute-start.1 = (bf16[8,14336]{1,0:T(8,128)(2,1)S(1)}, bf16[8,14336]{1,0:T(8,128)(2,1)S(1)}, u32[]{:S(2)}, u32[]{:S(2)}) collective-permute-start(bf16[8,14336]{1,0:T(8,128)(2,1)S(1)} %get-tuple-element.38), channel_id=1, source_target_pairs={{0,8},{4,12},{8,0},{12,4},{1,9},{5,13},{9,1},{13,5},{2,10},{6,14},... | collective-permute-start | bytes 688136 | tf_op jit(solution)/shard_map/ppermute | solution.py:470
  24.9 10.6 %copy-start.10 = (f32[8,10240]{1,0:T(8,128)S(1)}, f32[8,10240]{1,0:T(8,128)}, u32[]{:S(2)}) copy-start(f32[8,10240]{1,0:T(8,128)} %refs_5_.1) | copy-start | bytes 983044
  24.9 10.6 %copy-start.11 = (f32[8,10240]{1,0:T(8,128)S(1)}, f32[8,10240]{1,0:T(8,128)}, u32[]{:S(2)}) copy-start(f32[8,10240]{1,0:T(8,128)} %refs_6_.1) | copy-start | bytes 983044
  24.9 10.7 %copy-start.12 = (f32[8,10240]{1,0:T(8,128)S(1)}, f32[8,10240]{1,0:T(8,128)}, u32[]{:S(2)}) copy-start(f32[8,10240]{1,0:T(8,128)} %refs_7_.1) | copy-start | bytes 983044
  24.9 10.7 %copy-start.13 = (f32[4096,8]{0,1:T(8,128)S(1)}, f32[4096,8]{0,1:T(8,128)}, u32[]{:S(2)}) copy-start(f32[4096,8]{0,1:T(8,128)} %param.12) | copy-start | bytes 393220
  24.9 10.7 %copy-start.14 = (f32[4096,8]{0,1:T(8,128)S(1)}, f32[4096,8]{0,1:T(8,128)}, u32[]{:S(2)}) copy-start(f32[4096,8]{0,1:T(8,128)} %param.14) | copy-start | bytes 393220
  24.9 10.7 %copy-start.15 = (f32[4096,8]{0,1:T(8,128)S(1)}, f32[4096,8]{0,1:T(8,128)}, u32[]{:S(2)}) copy-start(f32[4096,8]{0,1:T(8,128)} %param.15) | copy-start | bytes 393220
  34.2 24.8 %collective-permute-start.9 = (bf16[192,2048]{1,0:T(8,128)(2,1)S(1)}, bf16[192,2048]{1,0:T(8,128)(2,1)S(1)}, u32[]{:S(2)}, u32[]{:S(2)}) collective-permute-start(bf16[192,2048]{1,0:T(8,128)(2,1)S(1)} %get-tuple-element.39.refs_8_), channel_id=1, source_target_pairs={{0,1},{3,2},{4,5},{7,6},{8,9},{11,10},{12,13},{15,14},{16,17},{19,... | collective-permute-start | bytes 2359304 | tf_op jit(solution)/shard_map/ppermute | solution.py:467
  37.4 2.4 %collective-permute-start.3 = (bf16[8,4096]{1,0:T(8,128)(2,1)S(1)}, bf16[8,4096]{1,0:T(8,128)(2,1)S(1)}, u32[]{:S(2)}, u32[]{:S(2)}) collective-permute-start(bf16[8,4096]{1,0:T(8,128)(2,1)S(1)} %get-tuple-element.41), channel_id=1, source_target_pairs={{0,4},{4,0},{8,12},{12,8},{1,5},{5,1},{9,13},{13,9},{2,6},{6,2},{1... | collective-permute-start | bytes 196616 | tf_op jit(solution)/shard_map/ppermute | solution.py:470
  37.7 19.4 %collective-permute-start.2 = (bf16[8,10240]{1,0:T(8,128)(2,1)S(1)}, bf16[8,10240]{1,0:T(8,128)(2,1)S(1)}, u32[]{:S(2)}, u32[]{:S(2)}) collective-permute-start(bf16[8,10240]{1,0:T(8,128)(2,1)S(1)} %get-tuple-element.40.refs_6_), channel_id=1, source_target_pairs={{0,0},{1,4},{2,8},{3,12},{4,1},{5,5},{6,9},{7,13},{8,2},{9,6},{10,... | collective-permute-start | bytes 491528 | tf_op jit(solution)/shard_map/ppermute | solution.py:511
  38.3 0.8 copy-start.3
  39.1 40.5 %collective-permute-start.8 = (bf16[128,2560]{1,0:T(8,128)(2,1)S(1)}, bf16[128,2560]{1,0:T(8,128)(2,1)S(1)}, u32[]{:S(2)}, u32[]{:S(2)}) collective-permute-start(bf16[128,2560]{1,0:T(8,128)(2,1)S(1)} %shard_map.159.refs_2_), channel_id=1, source_target_pairs={{1,2},{2,1},{5,6},{6,5},{9,10},{10,9},{13,14},{14,13},{17,18},{18,... | collective-permute-start | bytes 1966088 | tf_op jit(solution)/shard_map/ppermute | solution.py:467
  39.8 17.2 %collective-permute-start.4 = (bf16[16,4096]{1,0:T(8,128)(2,1)S(1)}, bf16[16,4096]{1,0:T(8,128)(2,1)S(1)}, u32[]{:S(2)}, u32[]{:S(2)}) collective-permute-start(bf16[16,4096]{1,0:T(8,128)(2,1)S(1)} %constant_dynamic-update-slice_fusion.refs_1_), channel_id=1, source_target_pairs={{0,8},{4,12},{8,0},{12,4},{1,9},{5,13},{9,1},{13,5},{2,10},{6,14},... | collective-permute-start | bytes 393224 | tf_op jit(solution)/shard_map/ppermute | solution.py:470
  52.1 26.1 %collective-permute-start.11 = (bf16[192,2048]{1,0:T(8,128)(2,1)S(1)}, bf16[192,2048]{1,0:T(8,128)(2,1)S(1)}, u32[]{:S(2)}, u32[]{:S(2)}) collective-permute-start(bf16[192,2048]{1,0:T(8,128)(2,1)S(1)} %get-tuple-element.44.refs_4_), channel_id=1, source_target_pairs={{0,1},{3,2},{4,5},{7,6},{8,9},{11,10},{12,13},{15,14},{16,17},{19,... | collective-permute-start | bytes 2359304 | tf_op jit(solution)/shard_map/ppermute | solution.py:467
  58.7 22.9 %collective-permute-start.7 = (bf16[8,12288]{1,0:T(8,128)(2,1)S(1)}, bf16[8,12288]{1,0:T(8,128)(2,1)S(1)}, u32[]{:S(2)}, u32[]{:S(2)}) collective-permute-start(bf16[8,12288]{1,0:T(8,128)(2,1)S(1)} %get-tuple-element.45.refs_3_), channel_id=1, source_target_pairs={{0,1},{1,0},{2,3},{3,2},{4,5},{5,4},{6,7},{7,6},{8,9},{9,8},{10,11... | collective-permute-start | bytes 589832 | tf_op jit(solution)/shard_map/ppermute | solution.py:517
  59.6 20.0 %collective-permute-start.10 = (bf16[128,2048]{1,0:T(8,128)(2,1)S(1)}, bf16[128,2048]{1,0:T(8,128)(2,1)S(1)}, u32[]{:S(2)}, u32[]{:S(2)}) collective-permute-start(bf16[128,2048]{1,0:T(8,128)(2,1)S(1)} %shard_map.162.refs_2_), channel_id=1, source_target_pairs={{1,2},{2,1},{5,6},{6,5},{9,10},{10,9},{13,14},{14,13},{17,18},{18,... | collective-permute-start | bytes 1572872 | tf_op jit(solution)/shard_map/ppermute | solution.py:467
  69.5 26.9 %collective-permute-start.15 = (bf16[192,2048]{1,0:T(8,128)(2,1)S(1)}, bf16[192,2048]{1,0:T(8,128)(2,1)S(1)}, u32[]{:S(2)}, u32[]{:S(2)}) collective-permute-start(bf16[192,2048]{1,0:T(8,128)(2,1)S(1)} %get-tuple-element.49.refs_3_), channel_id=1, source_target_pairs={{0,1},{3,2},{4,5},{7,6},{8,9},{11,10},{12,13},{15,14},{16,17},{19,... | collective-permute-start | bytes 2359304 | tf_op jit(solution)/shard_map/ppermute | solution.py:467
  78.9 30.8 %collective-permute-start.19 = (bf16[128,2048]{1,0:T(8,128)(2,1)S(1)}, bf16[128,2048]{1,0:T(8,128)(2,1)S(1)}, u32[]{:S(2)}, u32[]{:S(2)}) collective-permute-start(bf16[128,2048]{1,0:T(8,128)(2,1)S(1)} %shard_map.164.refs_6_), channel_id=1, source_target_pairs={{1,2},{2,1},{5,6},{6,5},{9,10},{10,9},{13,14},{14,13},{17,18},{18,... | collective-permute-start | bytes 1572872 | tf_op jit(solution)/shard_map/ppermute | solution.py:467
  79.6 0.8 copy-start.8
  80.4 16.4 %collective-permute-start.16 = (bf16[64,4608]{1,0:T(8,128)(2,1)S(1)}, bf16[64,4608]{1,0:T(8,128)(2,1)S(1)}, u32[]{:S(2)}, u32[]{:S(2)}) collective-permute-start(bf16[64,4608]{1,0:T(8,128)(2,1)S(1)} %shard_map.165.refs_3_), channel_id=1, source_target_pairs={{2,3},{1,0},{6,7},{5,4},{10,11},{9,8},{14,15},{13,12},{18,19},{17,... | collective-permute-start | bytes 1769480 | tf_op jit(solution)/shard_map/ppermute | solution.py:467
  87.8 19.3 %collective-permute-start.14 = (bf16[192,1024]{1,0:T(8,128)(2,1)S(1)}, bf16[192,1024]{1,0:T(8,128)(2,1)S(1)}, u32[]{:S(2)}, u32[]{:S(2)}) collective-permute-start(bf16[192,1024]{1,0:T(8,128)(2,1)S(1)} %get-tuple-element.53.refs_2_), channel_id=1, source_target_pairs={{0,1},{3,2},{4,5},{7,6},{8,9},{11,10},{12,13},{15,14},{16,17},{19,... | collective-permute-start | bytes 1179656 | tf_op jit(solution)/shard_map/ppermute | solution.py:467
  97.4 16.2 %collective-permute-start.21 = (bf16[128,2048]{1,0:T(8,128)(2,1)S(1)}, bf16[128,2048]{1,0:T(8,128)(2,1)S(1)}, u32[]{:S(2)}, u32[]{:S(2)}) collective-permute-start(bf16[128,2048]{1,0:T(8,128)(2,1)S(1)} %shard_map.169.refs_3_), channel_id=1, source_target_pairs={{1,2},{2,1},{5,6},{6,5},{9,10},{10,9},{13,14},{14,13},{17,18},{18,... | collective-permute-start | bytes 1572872 | tf_op jit(solution)/shard_map/ppermute | solution.py:467
  98.2 10.2 %collective-permute-start.12 = (bf16[16,11264]{1,0:T(8,128)(2,1)S(1)}, bf16[16,11264]{1,0:T(8,128)(2,1)S(1)}, u32[]{:S(2)}, u32[]{:S(2)}) collective-permute-start(bf16[16,11264]{1,0:T(8,128)(2,1)S(1)} %get-tuple-element.51.refs_2_.refs_5_.refs_12_.refs_19_), channel_id=1, source_target_pairs={{1,2},{2,1},{5,6},{6,5},{9,10},{10,9},{13,14},{14,13},{17,18},{18,... | collective-permute-start | bytes 1081352 | tf_op jit(solution)/shard_map/ppermute | solution.py:467
  98.8 12.2 %collective-permute-start.18 = (bf16[192,512]{1,0:T(8,128)(2,1)S(1)}, bf16[192,512]{1,0:T(8,128)(2,1)S(1)}, u32[]{:S(2)}, u32[]{:S(2)}) collective-permute-start(bf16[192,512]{1,0:T(8,128)(2,1)S(1)} %get-tuple-element.55.refs_3_), channel_id=1, source_target_pairs={{0,1},{3,2},{4,5},{7,6},{8,9},{11,10},{12,13},{15,14},{16,17},{19,... | collective-permute-start | bytes 589832 | tf_op jit(solution)/shard_map/ppermute | solution.py:467
  107.7 8.0 %collective-permute-start.17 = (bf16[128,1024]{1,0:T(8,128)(2,1)S(1)}, bf16[128,1024]{1,0:T(8,128)(2,1)S(1)}, u32[]{:S(2)}, u32[]{:S(2)}) collective-permute-start(bf16[128,1024]{1,0:T(8,128)(2,1)S(1)} %shard_map.170.refs_2_), channel_id=1, source_target_pairs={{1,2},{2,1},{5,6},{6,5},{9,10},{10,9},{13,14},{14,13},{17,18},{18,... | collective-permute-start | bytes 786440 | tf_op jit(solution)/shard_map/ppermute | solution.py:467
  108.4 23.3 %collective-permute-start.13 = (bf16[16,11264]{1,0:T(8,128)(2,1)S(1)}, bf16[16,11264]{1,0:T(8,128)(2,1)S(1)}, u32[]{:S(2)}, u32[]{:S(2)}) collective-permute-start(bf16[16,11264]{1,0:T(8,128)(2,1)S(1)} %collective-permute-done.12.refs_1_.refs_6_.refs_13_.refs_20_), channel_id=1, source_target_pairs={{2,3},{1,0},{6,7},{5,4},{10,11},{9,8},{14,15},{13,12},{18,19},{17,... | collective-permute-start | bytes 1081352 | tf_op jit(solution)/shard_map/ppermute | solution.py:467
  110.3 0.8 copy-start.5
  111.6 4.0 %collective-permute-start.20 = (bf16[128,512]{1,0:T(8,128)(2,1)S(1)}, bf16[128,512]{1,0:T(8,128)(2,1)S(1)}, u32[]{:S(2)}, u32[]{:S(2)}) collective-permute-start(bf16[128,512]{1,0:T(8,128)(2,1)S(1)} %shard_map.172.refs_2_), channel_id=1, source_target_pairs={{1,2},{2,1},{5,6},{6,5},{9,10},{10,9},{13,14},{14,13},{17,18},{18,... | collective-permute-start | bytes 393224 | tf_op jit(solution)/shard_map/ppermute | solution.py:467
  112.3 25.1 %collective-permute-start.23 = (bf16[64,2048]{1,0:T(8,128)(2,1)S(1)}, bf16[64,2048]{1,0:T(8,128)(2,1)S(1)}, u32[]{:S(2)}, u32[]{:S(2)}) collective-permute-start(bf16[64,2048]{1,0:T(8,128)(2,1)S(1)} %shard_map.171.refs_3_), channel_id=1, source_target_pairs={{2,3},{1,0},{6,7},{5,4},{10,11},{9,8},{14,15},{13,12},{18,19},{17,... | collective-permute-start | bytes 786440 | tf_op jit(solution)/shard_map/ppermute | solution.py:467
  114.2 18.4 %copy-start.4 = (bf16[192,1024]{1,0:T(8,128)(2,1)S(1)}, bf16[192,1024]{1,0:T(8,128)(2,1)}, u32[]{:S(2)}) copy-start(bf16[192,1024]{1,0:T(8,128)(2,1)} %copy-done.3) | copy-start | bytes 1179652
  114.2 18.4 %copy-start.9 = (bf16[128,2048]{1,0:T(8,128)(2,1)S(1)}, bf16[128,2048]{1,0:T(8,128)(2,1)}, u32[]{:S(2)}) copy-start(bf16[128,2048]{1,0:T(8,128)(2,1)} %copy-done.8) | copy-start | bytes 1572868
  114.3 28.8 %collective-permute-start.24 = (bf16[64,2048]{1,0:T(8,128)(2,1)S(1)}, bf16[64,2048]{1,0:T(8,128)(2,1)S(1)}, u32[]{:S(2)}, u32[]{:S(2)}) collective-permute-start(bf16[64,2048]{1,0:T(8,128)(2,1)S(1)} %shard_map.173.refs_4_), channel_id=1, source_target_pairs={{2,3},{1,0},{6,7},{5,4},{10,11},{9,8},{14,15},{13,12},{18,19},{17,... | collective-permute-start | bytes 786440 | tf_op jit(solution)/shard_map/ppermute | solution.py:467
  116.3 30.6 %collective-permute-start.22 = (bf16[64,1536]{1,0:T(8,128)(2,1)S(1)}, bf16[64,1536]{1,0:T(8,128)(2,1)S(1)}, u32[]{:S(2)}, u32[]{:S(2)}) collective-permute-start(bf16[64,1536]{1,0:T(8,128)(2,1)S(1)} %shard_map.174.refs_3_), channel_id=1, source_target_pairs={{2,3},{1,0},{6,7},{5,4},{10,11},{9,8},{14,15},{13,12},{18,19},{17,... | collective-permute-start | bytes 589832 | tf_op jit(solution)/shard_map/ppermute | solution.py:467
  132.7 4.7 %copy-start.6 = (bf16[128,2048]{1,0:T(8,128)(2,1)S(1)}, bf16[128,2048]{1,0:T(8,128)(2,1)}, u32[]{:S(2)}) copy-start(bf16[128,2048]{1,0:T(8,128)(2,1)} %copy-done.5) | copy-start | bytes 1572868

commit v8 on v5

--- a/solution.py
+++ b/solution.py
@@ -532,8 +532,7 @@
     last = spread = spread_inner(place, inner, near_out, far_out, width, share, [last])
     last = finish((0, 1, 2), last)
     last = third((4,), last)
-    last = third((5,), last)
-    last = third((6,), last)
+    last = third((5, 6), last)
     last = finish((3,), last)
     last = finish((4,), last)
     decoded = finish((5, 6), last, full_width=width, done=list(finished))

time: 132 us -> 135 us (1.023)
  waiting for transfers between devices: 8.95 us -> 13.9 us
    ppermute x20 -> x19, waiting for transfers between devices: 8.94 us -> 13.9 us  [line(): return lax.ppermute(values, 'tp', LINE[step])]
    ppermute x20 -> x19, starting transfers between devices: 44.5 us -> 43.2 us  [line(): return lax.ppermute(values, 'tp', LINE[step])]
    pallas_call x28 -> x27, Pallas kernels: 68.2 us -> 67.6 us  [call(): pl.pallas_call(kernel, grid_spec=pltpu.PrefetchScalarGridSpec(num_scalar_...]
  transfers between devices with their start and end apart: 26 -> 25, of which waited for: 3 -> 4; matrix products, arithmetic and copies ran while one was open for 0% -> 0% of each run, Pallas kernels for 46% -> 44%
where the time goes in v8:
time: 135 us
  Pallas kernels  67.6 us (50%)
  starting transfers between devices  48.8 us (36%)
  waiting for transfers between devices  13.9 us (10%)
  local copies, waits for them, and re-layouts  2.92 us (2%)
  between operations  1.38 us (1%)
    pallas_call x27, Pallas kernels, call(): pl.pallas_call(kernel, grid_spec=pltpu.PrefetchScalarGridSpec(num_scalar_...  67.6 us
    ppermute x19, starting transfers between devices, line(): return lax.ppermute(values, 'tp', LINE[step])  43.2 us
    ppermute x19, waiting for transfers between devices, line(): return lax.ppermute(values, 'tp', LINE[step])  13.9 us
    ppermute x4, starting transfers between devices, chip(): return lax.ppermute(values, 'rep', [(i, i ^ bit) for i in range(4)])  4.89 us
    unnamed x37, local copies, waits for them, and re-layouts  2.82 us
  transfers between devices with their start and end apart: 25, of which 4 were waited for; matrix products, arithmetic and copies ran while one was open for 0% of the time, Pallas kernels for 44%

profile of v8, /device:TPU:0, one launch (start us, length us, event | category | flops | bytes accessed | tf_op | source)
XLA Modules:
  0.0 134.7 jit_solution(11944670705494660742)
XLA Ops:
  0.8 1.6 %copy-done = bf16[256,4096]{1,0:T(8,128)(2,1)S(1)} copy-done((bf16[256,4096]{1,0:T(8,128)(2,1)S(1)}, bf16[256,4096]{1,0:T(8,128)(2,1)}, u32[]{:S(2)}) %copy-start) | copy-done | bytes 2097176
  2.4 5.5 %shard_map.153 = (f32[256,1024]{1,0:T(8,128)S(1)}, bf16[192,1024]{1,0:T(8,128)(2,1)S(1)}) custom-call(s32[13]{0:T(128)S(1)} %stack.55.place_ref, bf16[256,4096]{1,0:T(8,128)(2,1)S(1)} %copy-done, bf16[4096,10240]{1,0:T(8,128)(2,1)} %refs_1_.13), custom_call_target="tpu_custom_call" | custom-call | flops 10737418240 | bytes 41943040 | tf_op jit(solution)/shard_map/pallas_call | solution.py:122
  7.9 5.1 %collective-permute-start.5 = (bf16[192,1024]{1,0:T(8,128)(2,1)S(1)}, bf16[192,1024]{1,0:T(8,128)(2,1)S(1)}, u32[]{:S(2)}, u32[]{:S(2)}) collective-permute-start(bf16[192,1024]{1,0:T(8,128)(2,1)S(1)} %get-tuple-element.35.refs_2_), channel_id=1, source_target_pairs={{0,1},{3,2},{4,5},{7,6},{8,9},{11,10},{12,13},{15,14},{16,17},{19,... | collective-permute-start | bytes 1179656 | tf_op jit(solution)/shard_map/ppermute | solution.py:467
  13.7 7.7 %shard_map.155 = (f32[256,1536]{1,0:T(8,128)S(1)}, bf16[192,1536]{1,0:T(8,128)(2,1)S(1)}) custom-call(s32[13]{0:T(128)S(1)} %stack.55.place_ref, bf16[256,4096]{1,0:T(8,128)(2,1)S(1)} %copy-done.1, bf16[4096,10240]{1,0:T(8,128)(2,1)} %refs_1_.13, bf16[16,14336]{1,0:T(8,128)(2,1)S(1)} %shard_map.154.refs_2_), custom_call_target="tpu_custom_call" | custom-call | flops 16106127360 | bytes 62914560 | tf_op jit(solution)/shard_map/pallas_call | solution.py:122
  21.3 1.3 collective-permute-start.6
  22.7 0.7 shard_map.156
  23.3 1.6 %collective-permute-start.1 = (bf16[8,14336]{1,0:T(8,128)(2,1)S(1)}, bf16[8,14336]{1,0:T(8,128)(2,1)S(1)}, u32[]{:S(2)}, u32[]{:S(2)}) collective-permute-start(bf16[8,14336]{1,0:T(8,128)(2,1)S(1)} %get-tuple-element.38), channel_id=1, source_target_pairs={{0,8},{4,12},{8,0},{12,4},{1,9},{5,13},{9,1},{13,5},{2,10},{6,14},... | collective-permute-start | bytes 688136 | tf_op jit(solution)/shard_map/ppermute | solution.py:470
  24.9 9.2 %shard_map.157 = (f32[256,2048]{1,0:T(8,128)S(1)}, bf16[192,2048]{1,0:T(8,128)(2,1)S(1)}) custom-call(s32[13]{0:T(128)S(1)} %stack.55.place_ref, bf16[256,4096]{1,0:T(8,128)(2,1)S(1)} %copy-done.1, bf16[4096,10240]{1,0:T(8,128)(2,1)} %refs_1_.13, f32[8,14336]{1,0:T(8,128)S(1)} %get-tuple-element.37.refs_2_.refs_0_), custom_call_target="tpu_custom_call" | custom-call | flops 21474836480 | bytes 83886080 | tf_op jit(solution)/shard_map/pallas_call | solution.py:122
  34.2 1.3 collective-permute-start.9
  35.6 1.9 %shard_map.158 = (f32[8,4096]{1,0:T(8,128)}, f32[8,4096]{1,0:T(8,128)}, f32[8,4096]{1,0:T(8,128)}, bf16[8,4096]{1,0:T(8,128)(2,1)S(1)}, f32[8,10240]{1,0:T(8,128...) custom-call(s32[13]{0:T(128)S(1)} %stack.55.place_ref, ...), custom_call_target="tpu_custom_call" | custom-call | bytes 18350080 | tf_op jit(solution)/shard_map/pallas_call | solution.py:122
  37.7 0.7 collective-permute-start.2
  38.4 0.7 shard_map.159.refs_2_
  39.3 0.7 collective-permute-start.8
  40.0 3.1 %collective-permute-start.4 = (bf16[16,4096]{1,0:T(8,128)(2,1)S(1)}, bf16[16,4096]{1,0:T(8,128)(2,1)S(1)}, u32[]{:S(2)}, u32[]{:S(2)}) collective-permute-start(bf16[16,4096]{1,0:T(8,128)(2,1)S(1)} %constant_dynamic-update-slice_fusion.refs_1_), channel_id=1, source_target_pairs={{0,8},{4,12},{8,0},{12,4},{1,9},{5,13},{9,1},{13,5},{2,10},{6,14},... | collective-permute-start | bytes 393224 | tf_op jit(solution)/shard_map/ppermute | solution.py:470
  43.1 9.2 %shard_map.160 = (f32[256,2048]{1,0:T(8,128)S(1)}, bf16[192,2048]{1,0:T(8,128)(2,1)S(1)}) custom-call(s32[13]{0:T(128)S(1)} %stack.55.place_ref, bf16[256,4096]{1,0:T(8,128)(2,1)S(1)} %copy-done.1, bf16[4096,10240]{1,0:T(8,128)(2,1)} %refs_1_.13, bf16[128,2560]{1,0:T(8,128)(2,1)S(1)} %shard_map.159.refs_2_), custom_call_target="tpu_custom_call" | custom-call | flops 21474836480 | bytes 83886080 | tf_op jit(solution)/shard_map/pallas_call | solution.py:122
  52.3 4.9 %collective-permute-start.11 = (bf16[192,2048]{1,0:T(8,128)(2,1)S(1)}, bf16[192,2048]{1,0:T(8,128)(2,1)S(1)}, u32[]{:S(2)}, u32[]{:S(2)}) collective-permute-start(bf16[192,2048]{1,0:T(8,128)(2,1)S(1)} %get-tuple-element.44.refs_4_), channel_id=1, source_target_pairs={{0,1},{3,2},{4,5},{7,6},{8,9},{11,10},{12,13},{15,14},{16,17},{19,... | collective-permute-start | bytes 2359304 | tf_op jit(solution)/shard_map/ppermute | solution.py:467
  57.2 1.7 %shard_map.161 = (f32[8,1024]{1,0:T(8,128)S(1)}, bf16[8,12288]{1,0:T(8,128)(2,1)S(1)}) custom-call(s32[13]{0:T(128)S(1)} %stack.55.place_ref, bf16[256,4096]{1,0:T(8,128)(2,1)S(1)} %copy-done.1, bf16[16,4096]{1,0:T(8,128)(2,1)S(1)} %constant_dynamic-update-slice_fusion.refs_1_, bf16[16,4096]{1,0:T(8,128)(2,1)S(1)} %collective-permute-done.4.refs_2_, ...), custom_call_target="tpu_custom_call" | custom-call | flops 335544320 | bytes 10485760 | tf_op jit(solution)/shard_map/pallas_call | solution.py:122
  59.0 0.6 shard_map.162.refs_2_
  59.6 0.7 collective-permute-start.10
  60.3 9.2 %shard_map.163 = (f32[256,2048]{1,0:T(8,128)S(1)}, bf16[192,2048]{1,0:T(8,128)(2,1)S(1)}) custom-call(s32[13]{0:T(128)S(1)} %stack.55.place_ref, bf16[256,4096]{1,0:T(8,128)(2,1)S(1)} %copy-done.1, bf16[4096,10240]{1,0:T(8,128)(2,1)} %refs_1_.13, bf16[128,2048]{1,0:T(8,128)(2,1)S(1)} %shard_map.162.refs_2_), custom_call_target="tpu_custom_call" | custom-call | flops 21474836480 | bytes 83886080 | tf_op jit(solution)/shard_map/pallas_call | solution.py:122
  69.5 8.7 %collective-permute-start.17 = (bf16[192,2048]{1,0:T(8,128)(2,1)S(1)}, bf16[192,2048]{1,0:T(8,128)(2,1)S(1)}, u32[]{:S(2)}, u32[]{:S(2)}) collective-permute-start(bf16[192,2048]{1,0:T(8,128)(2,1)S(1)} %get-tuple-element.49.refs_3_), channel_id=1, source_target_pairs={{0,1},{3,2},{4,5},{7,6},{8,9},{11,10},{12,13},{15,14},{16,17},{19,... | collective-permute-start | bytes 2359304 | tf_op jit(solution)/shard_map/ppermute | solution.py:467
  78.2 0.6 shard_map.164.refs_6_
  78.9 0.7 collective-permute-start.15
  79.6 0.6 shard_map.165.refs_3_
  80.4 1.3 collective-permute-start.18
  82.2 0.7 collective-permute-start.12
  82.9 5.5 %shard_map.167 = (f32[256,1024]{1,0:T(8,128)S(1)}, bf16[192,1024]{1,0:T(8,128)(2,1)S(1)}) custom-call(s32[13]{0:T(128)S(1)} %stack.55.place_ref, bf16[256,4096]{1,0:T(8,128)(2,1)S(1)} %copy-done.1, bf16[4096,10240]{1,0:T(8,128)(2,1)} %refs_1_.13, bf16[16,11264]{1,0:T(8,128)(2,1)S(1)} %get-tuple-element.51.refs_2_.refs_5_.refs_12_.refs_19_), custom_call_target="tpu_custom_call" | custom-call | flops 10737418240 | bytes 41943040 | tf_op jit(solution)/shard_map/pallas_call | solution.py:122
  88.5 5.8 %collective-permute-start.16 = (bf16[192,1024]{1,0:T(8,128)(2,1)S(1)}, bf16[192,1024]{1,0:T(8,128)(2,1)S(1)}, u32[]{:S(2)}, u32[]{:S(2)}) collective-permute-start(bf16[192,1024]{1,0:T(8,128)(2,1)S(1)} %get-tuple-element.52.refs_2_), channel_id=1, source_target_pairs={{0,1},{3,2},{4,5},{7,6},{8,9},{11,10},{12,13},{15,14},{16,17},{19,... | collective-permute-start | bytes 1179656 | tf_op jit(solution)/shard_map/ppermute | solution.py:467
  94.3 4.0 %shard_map.168 = (f32[256,512]{1,0:T(8,128)S(1)}, bf16[192,512]{1,0:T(8,128)(2,1)S(1)}) custom-call(s32[13]{0:T(128)S(1)} %stack.55.place_ref, bf16[256,4096]{1,0:T(8,128)(2,1)S(1)} %copy-done.1, bf16[4096,10240]{1,0:T(8,128)(2,1)} %refs_1_.13, bf16[192,1024]{1,0:T(8,128)(2,1)S(1)} %get-tuple-element.52.refs_2_), custom_call_target="tpu_custom_call" | custom-call | flops 5368709120 | bytes 20971520 | tf_op jit(solution)/shard_map/pallas_call | solution.py:122
  98.4 0.6 shard_map.169.refs_3_
  99.0 0.7 collective-permute-start.21
  99.7 1.3 collective-permute-start.13
  101.0 4.6 %collective-permute-start.14 = (bf16[192,512]{1,0:T(8,128)(2,1)S(1)}, bf16[192,512]{1,0:T(8,128)(2,1)S(1)}, u32[]{:S(2)}, u32[]{:S(2)}) collective-permute-start(bf16[192,512]{1,0:T(8,128)(2,1)S(1)} %get-tuple-element.54.refs_3_), channel_id=1, source_target_pairs={{0,1},{3,2},{4,5},{7,6},{8,9},{11,10},{12,13},{15,14},{16,17},{19,... | collective-permute-start | bytes 589832 | tf_op jit(solution)/shard_map/ppermute | solution.py:467
  106.3 0.8 collective-permute-start.19
  107.7 0.8 copy-done.8
  108.5 0.8 collective-permute-done.14.refs_1_.refs_2_.refs_9_
  109.9 0.7 collective-permute-start.20
  110.6 1.3 collective-permute-start.23
  111.9 1.0 shard_map.173.refs_0_.refs_22_
  112.9 0.9 shard_map.174.refs_2_.refs_15_
  114.5 1.4 %collective-permute-start.24 = (bf16[64,2048]{1,0:T(8,128)(2,1)S(1)}, bf16[64,2048]{1,0:T(8,128)(2,1)S(1)}, u32[]{:S(2)}, u32[]{:S(2)}) collective-permute-start(bf16[64,2048]{1,0:T(8,128)(2,1)S(1)} %shard_map.175.refs_4_), channel_id=1, source_target_pairs={{2,3},{1,0},{6,7},{5,4},{10,11},{9,8},{14,15},{13,12},{18,19},{17,... | collective-permute-start | bytes 786440 | tf_op jit(solution)/shard_map/ppermute | solution.py:467
  116.5 1.3 collective-permute-start.22
  117.8 6.2 %collective-permute-done.23.refs_4_ = bf16[64,2048]{1,0:T(8,128)(2,1)S(1)} collective-permute-done((bf16[64,2048]{1,0:T(8,128)(2,1)S(1)}, bf16[64,2048]{1,0:T(8,128)(2,1)S(1)}, u32[]{:S(2)}, u32[]{:S(2)}) %collective-permute-start.23) | collective-permute-done | bytes 262176 | tf_op jit(solution)/shard_map/ppermute | solution.py:467
  124.1 0.8 shard_map.177.refs_8_.refs_16_
  124.8 4.9 %collective-permute-done.24.refs_4_ = bf16[64,2048]{1,0:T(8,128)(2,1)S(1)} collective-permute-done((bf16[64,2048]{1,0:T(8,128)(2,1)S(1)}, bf16[64,2048]{1,0:T(8,128)(2,1)S(1)}, u32[]{:S(2)}, u32[]{:S(2)}) %collective-permute-start.24) | collective-permute-done | bytes 262176 | tf_op jit(solution)/shard_map/ppermute | solution.py:467
  129.7 0.8 shard_map.178.refs_17_.refs_18_
  130.4 1.9 %collective-permute-done.22.refs_4_.refs_11_ = bf16[64,1536]{1,0:T(8,128)(2,1)S(1)} collective-permute-done((bf16[64,1536]{1,0:T(8,128)(2,1)S(1)}, bf16[64,1536]{1,0:T(8,128)(2,1)S(1)}, u32[]{:S(2)}, u32[]{:S(2)}) %collective-permute-start.22) | collective-permute-done | bytes 196640 | tf_op jit(solution)/shard_map/ppermute | solution.py:467
  132.4 2.3 %shard_map.179 = f32[64,10240]{1,0:T(8,128)} custom-call(s32[13]{0:T(128)S(1)} %stack.55.place_ref, bf16[64,64]{1,0:T(8,128)(2,1)S(1)} %shard_map.173.refs_0_.refs_22_, f32[256,1024]{1,0:T(8,128)S(1)} %get-tuple-element.55.refs_0_.refs_1_, bf16[192,1024]{1,0:T(8,128)(2,1)S(1)} %collective-permute-done.16.refs_1_.refs_2_, ...), custom_call_target="tpu_custom_call" | custom-call | bytes 45875200 | tf_op jit(solution)/shard_map/pallas_call | solution.py:122
  (68 shorter events, 5.0 us)
Async XLA Ops:
  0.8 1.6 %copy-start = (bf16[256,4096]{1,0:T(8,128)(2,1)S(1)}, bf16[256,4096]{1,0:T(8,128)(2,1)}, u32[]{:S(2)}) copy-start(bf16[256,4096]{1,0:T(8,128)(2,1)} %refs_0_.15) | copy-start | bytes 6291460
  2.4 10.6 %copy-start.4 = (f32[1,32,10240]{2,1,0:T(8,128)S(1)}, f32[1,32,10240]{2,1,0:T(8,128)}, u32[]{:S(2)}) copy-start(f32[1,32,10240]{2,1,0:T(8,128)} %param.19) | copy-start | bytes 3932164
  2.4 10.6 %copy-start.7 = (f32[1,4096,32]{1,2,0:T(8,128)S(1)}, f32[1,4096,32]{1,2,0:T(8,128)}, u32[]{:S(2)}) copy-start(f32[1,4096,32]{1,2,0:T(8,128)} %param.18) | copy-start | bytes 1572868
  7.8 5.8 %copy-start.1 = (bf16[256,4096]{1,0:T(8,128)(2,1)S(1)}, bf16[256,4096]{1,0:T(8,128)(2,1)}, u32[]{:S(2)}) copy-start(bf16[256,4096]{1,0:T(8,128)(2,1)} %refs_0_.15) | copy-start | bytes 6291460
  7.9 30.5 %collective-permute-start.5 = (bf16[192,1024]{1,0:T(8,128)(2,1)S(1)}, bf16[192,1024]{1,0:T(8,128)(2,1)S(1)}, u32[]{:S(2)}, u32[]{:S(2)}) collective-permute-start(bf16[192,1024]{1,0:T(8,128)(2,1)S(1)} %get-tuple-element.35.refs_2_), channel_id=1, source_target_pairs={{0,1},{3,2},{4,5},{7,6},{8,9},{11,10},{12,13},{15,14},{16,17},{19,... | collective-permute-start | bytes 1179656 | tf_op jit(solution)/shard_map/ppermute | solution.py:467
  13.6 9.1 %collective-permute-start = (bf16[16,14336]{1,0:T(8,128)(2,1)S(1)}, bf16[16,14336]{1,0:T(8,128)(2,1)S(1)}, u32[]{:S(2)}, u32[]{:S(2)}) collective-permute-start(bf16[16,14336]{1,0:T(8,128)(2,1)S(1)} %shard_map.154.refs_2_), channel_id=1, source_target_pairs={{0,4},{4,0},{8,12},{12,8},{1,5},{5,1},{9,13},{13,9},{2,6},{6,2},{1... | collective-permute-start | bytes 1376264 | tf_op jit(solution)/shard_map/ppermute | solution.py:470
  21.3 17.0 %collective-permute-start.6 = (bf16[192,1536]{1,0:T(8,128)(2,1)S(1)}, bf16[192,1536]{1,0:T(8,128)(2,1)S(1)}, u32[]{:S(2)}, u32[]{:S(2)}) collective-permute-start(bf16[192,1536]{1,0:T(8,128)(2,1)S(1)} %get-tuple-element.36.refs_3_), channel_id=1, source_target_pairs={{0,1},{3,2},{4,5},{7,6},{8,9},{11,10},{12,13},{15,14},{16,17},{19,... | collective-permute-start | bytes 1769480 | tf_op jit(solution)/shard_map/ppermute | solution.py:467
  23.3 12.2 %collective-permute-start.1 = (bf16[8,14336]{1,0:T(8,128)(2,1)S(1)}, bf16[8,14336]{1,0:T(8,128)(2,1)S(1)}, u32[]{:S(2)}, u32[]{:S(2)}) collective-permute-start(bf16[8,14336]{1,0:T(8,128)(2,1)S(1)} %get-tuple-element.38), channel_id=1, source_target_pairs={{0,8},{4,12},{8,0},{12,4},{1,9},{5,13},{9,1},{13,5},{2,10},{6,14},... | collective-permute-start | bytes 688136 | tf_op jit(solution)/shard_map/ppermute | solution.py:470
  24.9 10.6 %copy-start.12 = (f32[8,10240]{1,0:T(8,128)S(1)}, f32[8,10240]{1,0:T(8,128)}, u32[]{:S(2)}) copy-start(f32[8,10240]{1,0:T(8,128)} %refs_5_.1) | copy-start | bytes 983044
  24.9 10.6 %copy-start.13 = (f32[8,10240]{1,0:T(8,128)S(1)}, f32[8,10240]{1,0:T(8,128)}, u32[]{:S(2)}) copy-start(f32[8,10240]{1,0:T(8,128)} %refs_6_.1) | copy-start | bytes 983044
  24.9 10.7 %copy-start.14 = (f32[8,10240]{1,0:T(8,128)S(1)}, f32[8,10240]{1,0:T(8,128)}, u32[]{:S(2)}) copy-start(f32[8,10240]{1,0:T(8,128)} %refs_7_.1) | copy-start | bytes 983044
  24.9 10.7 %copy-start.15 = (f32[4096,8]{0,1:T(8,128)S(1)}, f32[4096,8]{0,1:T(8,128)}, u32[]{:S(2)}) copy-start(f32[4096,8]{0,1:T(8,128)} %param.12) | copy-start | bytes 393220
  24.9 10.7 %copy-start.16 = (f32[4096,8]{0,1:T(8,128)S(1)}, f32[4096,8]{0,1:T(8,128)}, u32[]{:S(2)}) copy-start(f32[4096,8]{0,1:T(8,128)} %param.14) | copy-start | bytes 393220
  24.9 10.7 %copy-start.17 = (f32[4096,8]{0,1:T(8,128)S(1)}, f32[4096,8]{0,1:T(8,128)}, u32[]{:S(2)}) copy-start(f32[4096,8]{0,1:T(8,128)} %param.15) | copy-start | bytes 393220
  34.2 24.8 %collective-permute-start.9 = (bf16[192,2048]{1,0:T(8,128)(2,1)S(1)}, bf16[192,2048]{1,0:T(8,128)(2,1)S(1)}, u32[]{:S(2)}, u32[]{:S(2)}) collective-permute-start(bf16[192,2048]{1,0:T(8,128)(2,1)S(1)} %get-tuple-element.39.refs_8_), channel_id=1, source_target_pairs={{0,1},{3,2},{4,5},{7,6},{8,9},{11,10},{12,13},{15,14},{16,17},{19,... | collective-permute-start | bytes 2359304 | tf_op jit(solution)/shard_map/ppermute | solution.py:467
  37.4 2.5 %collective-permute-start.3 = (bf16[8,4096]{1,0:T(8,128)(2,1)S(1)}, bf16[8,4096]{1,0:T(8,128)(2,1)S(1)}, u32[]{:S(2)}, u32[]{:S(2)}) collective-permute-start(bf16[8,4096]{1,0:T(8,128)(2,1)S(1)} %get-tuple-element.41), channel_id=1, source_target_pairs={{0,4},{4,0},{8,12},{12,8},{1,5},{5,1},{9,13},{13,9},{2,6},{6,2},{1... | collective-permute-start | bytes 196616 | tf_op jit(solution)/shard_map/ppermute | solution.py:470
  37.7 19.5 %collective-permute-start.2 = (bf16[8,10240]{1,0:T(8,128)(2,1)S(1)}, bf16[8,10240]{1,0:T(8,128)(2,1)S(1)}, u32[]{:S(2)}, u32[]{:S(2)}) collective-permute-start(bf16[8,10240]{1,0:T(8,128)(2,1)S(1)} %get-tuple-element.40.refs_6_), channel_id=1, source_target_pairs={{0,0},{1,4},{2,8},{3,12},{4,1},{5,5},{6,9},{7,13},{8,2},{9,6},{10,... | collective-permute-start | bytes 491528 | tf_op jit(solution)/shard_map/ppermute | solution.py:511
  38.3 0.8 copy-start.5
  38.3 0.9 copy-start.2
  39.3 40.3 %collective-permute-start.8 = (bf16[128,2560]{1,0:T(8,128)(2,1)S(1)}, bf16[128,2560]{1,0:T(8,128)(2,1)S(1)}, u32[]{:S(2)}, u32[]{:S(2)}) collective-permute-start(bf16[128,2560]{1,0:T(8,128)(2,1)S(1)} %shard_map.159.refs_2_), channel_id=1, source_target_pairs={{1,2},{2,1},{5,6},{6,5},{9,10},{10,9},{13,14},{14,13},{17,18},{18,... | collective-permute-start | bytes 1966088 | tf_op jit(solution)/shard_map/ppermute | solution.py:467
  40.0 17.2 %collective-permute-start.4 = (bf16[16,4096]{1,0:T(8,128)(2,1)S(1)}, bf16[16,4096]{1,0:T(8,128)(2,1)S(1)}, u32[]{:S(2)}, u32[]{:S(2)}) collective-permute-start(bf16[16,4096]{1,0:T(8,128)(2,1)S(1)} %constant_dynamic-update-slice_fusion.refs_1_), channel_id=1, source_target_pairs={{0,8},{4,12},{8,0},{12,4},{1,9},{5,13},{9,1},{13,5},{2,10},{6,14},... | collective-permute-start | bytes 393224 | tf_op jit(solution)/shard_map/ppermute | solution.py:470
  52.3 25.9 %collective-permute-start.11 = (bf16[192,2048]{1,0:T(8,128)(2,1)S(1)}, bf16[192,2048]{1,0:T(8,128)(2,1)S(1)}, u32[]{:S(2)}, u32[]{:S(2)}) collective-permute-start(bf16[192,2048]{1,0:T(8,128)(2,1)S(1)} %get-tuple-element.44.refs_4_), channel_id=1, source_target_pairs={{0,1},{3,2},{4,5},{7,6},{8,9},{11,10},{12,13},{15,14},{16,17},{19,... | collective-permute-start | bytes 2359304 | tf_op jit(solution)/shard_map/ppermute | solution.py:467
  58.9 22.7 %collective-permute-start.7 = (bf16[8,12288]{1,0:T(8,128)(2,1)S(1)}, bf16[8,12288]{1,0:T(8,128)(2,1)S(1)}, u32[]{:S(2)}, u32[]{:S(2)}) collective-permute-start(bf16[8,12288]{1,0:T(8,128)(2,1)S(1)} %get-tuple-element.45.refs_3_), channel_id=1, source_target_pairs={{0,1},{1,0},{2,3},{3,2},{4,5},{5,4},{6,7},{7,6},{8,9},{9,8},{10,11... | collective-permute-start | bytes 589832 | tf_op jit(solution)/shard_map/ppermute | solution.py:517
  59.6 20.0 %collective-permute-start.10 = (bf16[128,2048]{1,0:T(8,128)(2,1)S(1)}, bf16[128,2048]{1,0:T(8,128)(2,1)S(1)}, u32[]{:S(2)}, u32[]{:S(2)}) collective-permute-start(bf16[128,2048]{1,0:T(8,128)(2,1)S(1)} %shard_map.162.refs_2_), channel_id=1, source_target_pairs={{1,2},{2,1},{5,6},{6,5},{9,10},{10,9},{13,14},{14,13},{17,18},{18,... | collective-permute-start | bytes 1572872 | tf_op jit(solution)/shard_map/ppermute | solution.py:467
  69.5 28.8 %collective-permute-start.17 = (bf16[192,2048]{1,0:T(8,128)(2,1)S(1)}, bf16[192,2048]{1,0:T(8,128)(2,1)S(1)}, u32[]{:S(2)}, u32[]{:S(2)}) collective-permute-start(bf16[192,2048]{1,0:T(8,128)(2,1)S(1)} %get-tuple-element.49.refs_3_), channel_id=1, source_target_pairs={{0,1},{3,2},{4,5},{7,6},{8,9},{11,10},{12,13},{15,14},{16,17},{19,... | collective-permute-start | bytes 2359304 | tf_op jit(solution)/shard_map/ppermute | solution.py:467
  78.9 28.2 %collective-permute-start.15 = (bf16[128,2048]{1,0:T(8,128)(2,1)S(1)}, bf16[128,2048]{1,0:T(8,128)(2,1)S(1)}, u32[]{:S(2)}, u32[]{:S(2)}) collective-permute-start(bf16[128,2048]{1,0:T(8,128)(2,1)S(1)} %shard_map.164.refs_6_), channel_id=1, source_target_pairs={{1,2},{2,1},{5,6},{6,5},{9,10},{10,9},{13,14},{14,13},{17,18},{18,... | collective-permute-start | bytes 1572872 | tf_op jit(solution)/shard_map/ppermute | solution.py:467
  79.6 0.8 copy-start.10
  80.4 18.0 %collective-permute-start.18 = (bf16[64,4608]{1,0:T(8,128)(2,1)S(1)}, bf16[64,4608]{1,0:T(8,128)(2,1)S(1)}, u32[]{:S(2)}, u32[]{:S(2)}) collective-permute-start(bf16[64,4608]{1,0:T(8,128)(2,1)S(1)} %shard_map.165.refs_3_), channel_id=1, source_target_pairs={{2,3},{1,0},{6,7},{5,4},{10,11},{9,8},{14,15},{13,12},{18,19},{17,... | collective-permute-start | bytes 1769480 | tf_op jit(solution)/shard_map/ppermute | solution.py:467
  82.2 17.5 %collective-permute-start.12 = (bf16[16,11264]{1,0:T(8,128)(2,1)S(1)}, bf16[16,11264]{1,0:T(8,128)(2,1)S(1)}, u32[]{:S(2)}, u32[]{:S(2)}) collective-permute-start(bf16[16,11264]{1,0:T(8,128)(2,1)S(1)} %get-tuple-element.51.refs_2_.refs_5_.refs_12_.refs_19_), channel_id=1, source_target_pairs={{1,2},{2,1},{5,6},{6,5},{9,10},{10,9},{13,14},{14,13},{17,18},{18,... | collective-permute-start | bytes 1081352 | tf_op jit(solution)/shard_map/ppermute | solution.py:467
  88.5 17.2 %collective-permute-start.16 = (bf16[192,1024]{1,0:T(8,128)(2,1)S(1)}, bf16[192,1024]{1,0:T(8,128)(2,1)S(1)}, u32[]{:S(2)}, u32[]{:S(2)}) collective-permute-start(bf16[192,1024]{1,0:T(8,128)(2,1)S(1)} %get-tuple-element.52.refs_2_), channel_id=1, source_target_pairs={{0,1},{3,2},{4,5},{7,6},{8,9},{11,10},{12,13},{15,14},{16,17},{19,... | collective-permute-start | bytes 1179656 | tf_op jit(solution)/shard_map/ppermute | solution.py:467
  99.0 14.8 %collective-permute-start.21 = (bf16[128,2048]{1,0:T(8,128)(2,1)S(1)}, bf16[128,2048]{1,0:T(8,128)(2,1)S(1)}, u32[]{:S(2)}, u32[]{:S(2)}) collective-permute-start(bf16[128,2048]{1,0:T(8,128)(2,1)S(1)} %shard_map.169.refs_3_), channel_id=1, source_target_pairs={{1,2},{2,1},{5,6},{6,5},{9,10},{10,9},{13,14},{14,13},{17,18},{18,... | collective-permute-start | bytes 1572872 | tf_op jit(solution)/shard_map/ppermute | solution.py:467
  99.7 12.2 %collective-permute-start.13 = (bf16[16,11264]{1,0:T(8,128)(2,1)S(1)}, bf16[16,11264]{1,0:T(8,128)(2,1)S(1)}, u32[]{:S(2)}, u32[]{:S(2)}) collective-permute-start(bf16[16,11264]{1,0:T(8,128)(2,1)S(1)} %collective-permute-done.12.refs_1_.refs_6_.refs_13_.refs_20_), channel_id=1, source_target_pairs={{2,3},{1,0},{6,7},{5,4},{10,11},{9,8},{14,15},{13,12},{18,19},{17,... | collective-permute-start | bytes 1081352 | tf_op jit(solution)/shard_map/ppermute | solution.py:467
  101.0 8.3 %collective-permute-start.14 = (bf16[192,512]{1,0:T(8,128)(2,1)S(1)}, bf16[192,512]{1,0:T(8,128)(2,1)S(1)}, u32[]{:S(2)}, u32[]{:S(2)}) collective-permute-start(bf16[192,512]{1,0:T(8,128)(2,1)S(1)} %get-tuple-element.54.refs_3_), channel_id=1, source_target_pairs={{0,1},{3,2},{4,5},{7,6},{8,9},{11,10},{12,13},{15,14},{16,17},{19,... | collective-permute-start | bytes 589832 | tf_op jit(solution)/shard_map/ppermute | solution.py:467
  106.2 6.7 %copy-start.3 = (bf16[192,1536]{1,0:T(8,128)(2,1)S(1)}, bf16[192,1536]{1,0:T(8,128)(2,1)}, u32[]{:S(2)}) copy-start(bf16[192,1536]{1,0:T(8,128)(2,1)} %copy-done.2) | copy-start | bytes 1769476
  106.2 6.7 %copy-start.6 = (bf16[192,1024]{1,0:T(8,128)(2,1)S(1)}, bf16[192,1024]{1,0:T(8,128)(2,1)}, u32[]{:S(2)}) copy-start(bf16[192,1024]{1,0:T(8,128)(2,1)} %copy-done.5) | copy-start | bytes 1179652
  106.2 6.7 %copy-start.11 = (bf16[128,2048]{1,0:T(8,128)(2,1)S(1)}, bf16[128,2048]{1,0:T(8,128)(2,1)}, u32[]{:S(2)}) copy-start(bf16[128,2048]{1,0:T(8,128)(2,1)} %copy-done.10) | copy-start | bytes 1572868
  106.3 9.7 %collective-permute-start.19 = (bf16[128,1024]{1,0:T(8,128)(2,1)S(1)}, bf16[128,1024]{1,0:T(8,128)(2,1)S(1)}, u32[]{:S(2)}, u32[]{:S(2)}) collective-permute-start(bf16[128,1024]{1,0:T(8,128)(2,1)S(1)} %shard_map.170.refs_2_), channel_id=1, source_target_pairs={{1,2},{2,1},{5,6},{6,5},{9,10},{10,9},{13,14},{14,13},{17,18},{18,... | collective-permute-start | bytes 786440 | tf_op jit(solution)/shard_map/ppermute | solution.py:467
  107.7 0.8 copy-start.8
  109.9 6.0 %collective-permute-start.20 = (bf16[128,512]{1,0:T(8,128)(2,1)S(1)}, bf16[128,512]{1,0:T(8,128)(2,1)S(1)}, u32[]{:S(2)}, u32[]{:S(2)}) collective-permute-start(bf16[128,512]{1,0:T(8,128)(2,1)S(1)} %shard_map.172.refs_3_), channel_id=1, source_target_pairs={{1,2},{2,1},{5,6},{6,5},{9,10},{10,9},{13,14},{14,13},{17,18},{18,... | collective-permute-start | bytes 393224 | tf_op jit(solution)/shard_map/ppermute | solution.py:467
  110.6 13.5 %collective-permute-start.23 = (bf16[64,2048]{1,0:T(8,128)(2,1)S(1)}, bf16[64,2048]{1,0:T(8,128)(2,1)S(1)}, u32[]{:S(2)}, u32[]{:S(2)}) collective-permute-start(bf16[64,2048]{1,0:T(8,128)(2,1)S(1)} %shard_map.171.refs_3_), channel_id=1, source_target_pairs={{2,3},{1,0},{6,7},{5,4},{10,11},{9,8},{14,15},{13,12},{18,19},{17,... | collective-permute-start | bytes 786440 | tf_op jit(solution)/shard_map/ppermute | solution.py:467
  114.5 9.6 %copy-start.9 = (bf16[128,2048]{1,0:T(8,128)(2,1)S(1)}, bf16[128,2048]{1,0:T(8,128)(2,1)}, u32[]{:S(2)}) copy-start(bf16[128,2048]{1,0:T(8,128)(2,1)} %copy-done.8) | copy-start | bytes 1572868
  114.5 15.2 %collective-permute-start.24 = (bf16[64,2048]{1,0:T(8,128)(2,1)S(1)}, bf16[64,2048]{1,0:T(8,128)(2,1)S(1)}, u32[]{:S(2)}, u32[]{:S(2)}) collective-permute-start(bf16[64,2048]{1,0:T(8,128)(2,1)S(1)} %shard_map.175.refs_4_), channel_id=1, source_target_pairs={{2,3},{1,0},{6,7},{5,4},{10,11},{9,8},{14,15},{13,12},{18,19},{17,... | collective-permute-start | bytes 786440 | tf_op jit(solution)/shard_map/ppermute | solution.py:467
  116.5 15.8 %collective-permute-start.22 = (bf16[64,1536]{1,0:T(8,128)(2,1)S(1)}, bf16[64,1536]{1,0:T(8,128)(2,1)S(1)}, u32[]{:S(2)}, u32[]{:S(2)}) collective-permute-start(bf16[64,1536]{1,0:T(8,128)(2,1)S(1)} %shard_map.176.refs_8_), channel_id=1, source_target_pairs={{2,3},{1,0},{6,7},{5,4},{10,11},{9,8},{14,15},{13,12},{18,19},{17,... | collective-permute-start | bytes 589832 | tf_op jit(solution)/shard_map/ppermute | solution.py:467
